TPU v7x, 32 devices: a whole 2x2x4 slice. The times are simulated.
32 devices in a mesh: sec: 4 (over x, core), dp: 4 (over z), tp: 2 (over y).
Axes of the slice: x: 2, y: 2, z: 4, core: 2. Of those that a mesh axis runs over, the one named last changes fastest.
Arguments:
- responses: bfloat16 [16, 128, 8192], P(('sec', 'dp'), 'tp'), may hold values from -6 to 6
- lengths: int32 [16], replicated, may hold values from 1 to 128, 1280 in all
- dest_dp: int32 [4, 16], replicated, may hold values from 0 to 3, as said below
- dest_slot: int32 [4, 16], replicated, may hold values from 0 to 5, as said below
- wq: bfloat16 [4, 8192, 4096], P('sec', None, 'tp'), may hold values from -0.0625 to 0.0625
- wkv: bfloat16 [4, 2, 8192, 1024], P('sec', None, None, 'tp'), may hold values from -0.0625 to 0.0625
- wo: bfloat16 [4, 4096, 8192], P('sec', 'tp'), may hold values from -0.09375 to 0.09375
- norm_gain: float32 [4, 8192], P('sec')
- head_vec: float32 [4, 8192], P('sec'), may hold values from -0.0625 to 0.0625
Outputs:
- layer_out: bfloat16 [4, 4, 128, 6, 8192], P('sec', 'dp', 'tp')
- sample_scores: float32 [4, 6, 4], P('dp')
Inputs may be any that keep to these rules, and one draw needn't show every extreme that they name: `dest_dp`: in each model's row, the responses go to the 4 groups; no group receives more than 6 responses and one group of every model receives exactly 6. `dest_slot`: within one model and one group, the responses take distinct rows; a group that receives c responses uses rows 0 to c - 1.
All inputs are finite; a program needn't handle non-finite values.
Results may differ from a plain program's by a relative error of at most 0.018.
The roundings to bfloat16 on the way count: a program that leaves them out, or rounds other values in their place, can miss the bound.
Values may be sent and summed in bfloat16 or wider, within the bound.
No kernel may reach another device: no remote copies, remote signals or barrier semaphores. Data moves between devices by JAX's collectives and lax.ppermute only.
A program may use at most 256 MiB of HBM per device.

v0:
```python
import math

import jax
import jax.numpy as jnp
from jax import lax
from jax.sharding import PartitionSpec as P

HD = 128


norm_eps = 1e-05
rope_theta = 500000.0


def rope_tables(positions, full_width):
    half_width = full_width // 2
    frequency = jnp.exp(
        jnp.arange(half_width, dtype=jnp.float32) * (-2.0 * math.log(rope_theta) / full_width)
    )
    angles = positions.astype(jnp.float32)[:, None] * frequency[None, :]
    return (jnp.cos(angles), jnp.sin(angles))


def rotate(values_in, cosine_table, sine_table):
    half_width = values_in.shape[-1] // 2
    first_half = values_in[..., :half_width]
    second_half = values_in[..., half_width:]
    return jnp.concatenate(
        [
            first_half * cosine_table - second_half * sine_table,
            second_half * cosine_table + first_half * sine_table,
        ],
        axis=-1,
    )


def spread_scores(selector, partial_value, n_sec, my_sec):
    contrib = jnp.sum(jnp.where(selector, partial_value[:, None], 0.0), axis=0)
    return jnp.where(jnp.arange(n_sec)[:, None] == my_sec, contrib[None, :], 0.0)


def on_device(responses, lengths, dest_dp, dest_slot, wq, wkv, wo, norm_gain, head_vec):
    n_sec = lax.axis_size("sec")
    n_dp = lax.axis_size("dp")
    n_groups = n_sec * n_dp
    samp_grp = responses.shape[0]
    local_len = responses.shape[1]
    width = responses.shape[2]
    samples = n_groups * samp_grp
    slot_count = 3 * samples // (2 * n_dp)
    my_sec = lax.axis_index("sec")
    my_dp = lax.axis_index("dp")
    my_group = my_sec * n_dp + my_dp
    own_dest = lax.dynamic_slice_in_dim(dest_dp, my_group * samp_grp, samp_grp, 1)
    group_ids = jnp.arange(n_groups)
    wanted = own_dest[group_ids // n_dp]
    matches = wanted == (group_ids % n_dp)[:, None]
    outgoing = jnp.where(matches[:, :, None, None], responses[None], jnp.zeros((), responses.dtype))
    arrived = lax.all_to_all(outgoing, ("sec", "dp"), split_axis=0, concat_axis=0, tiled=True)
    arrived = arrived.reshape(samples, local_len, width)
    row_dp = lax.dynamic_index_in_dim(dest_dp, my_sec, 0, keepdims=False)
    row_slot = lax.dynamic_index_in_dim(dest_slot, my_sec, 0, keepdims=False)
    selector = (row_dp == my_dp)[None, :] & (row_slot[None, :] == jnp.arange(slot_count)[:, None])
    slot_rows = jnp.einsum(
        "km,mpd->pkd", selector.astype(jnp.bfloat16), arrived, preferred_element_type=jnp.float32
    ).astype(jnp.bfloat16)
    slot_len = jnp.sum(jnp.where(selector, lengths[None, :], 0), axis=1)
    scale_vec = norm_gain[0]
    w_query = wq[0]
    w_key = wkv[0, 0]
    w_value = wkv[0, 1]
    block_rows = lax.all_gather(slot_rows, "tp", axis=0, tiled=True)
    row_count = block_rows.shape[0]
    as_float = block_rows.astype(jnp.float32)
    normed = (
        as_float
        * lax.rsqrt(jnp.mean(as_float * as_float, axis=-1, keepdims=True) + norm_eps)
        * scale_vec
    ).astype(jnp.bfloat16)
    cosine_table, sine_table = rope_tables(jnp.arange(row_count), HD)
    cosine_table = cosine_table[:, None, None, :]
    sine_table = sine_table[:, None, None, :]
    queries = jnp.einsum(
        "psd,dh->psh", normed, w_query, preferred_element_type=jnp.float32
    ).reshape(row_count, slot_count, -1, HD)
    queries = (
        rotate(queries, cosine_table, sine_table)
        .astype(jnp.bfloat16)
        .reshape(row_count, slot_count, -1)
    )
    keys_rot = jnp.einsum("psd,dh->psh", normed, w_key, preferred_element_type=jnp.float32).reshape(
        row_count, slot_count, -1, HD
    )
    keys_rot = (
        rotate(keys_rot, cosine_table, sine_table)
        .astype(jnp.bfloat16)
        .reshape(row_count, slot_count, -1)
    )
    values = jnp.einsum("psd,dh->psh", normed, w_value, preferred_element_type=jnp.float32).astype(
        jnp.bfloat16
    )
    projected = jnp.concatenate([queries, keys_rot, values], axis=-1)
    full_len = projected.shape[0]
    query_width = w_query.shape[1]
    kv_width = w_key.shape[1]
    heads_here = query_width // HD
    kv_here = kv_width // HD
    queries = projected[..., :query_width].reshape(
        full_len, slot_count, kv_here, heads_here // kv_here, HD
    )
    keys_rot = projected[..., query_width : query_width + kv_width].reshape(
        full_len, slot_count, kv_here, HD
    )
    values = projected[..., query_width + kv_width :].reshape(full_len, slot_count, kv_here, HD)
    scores = jnp.einsum(
        "iskgh,jskh->skgij", queries, keys_rot, preferred_element_type=jnp.float32
    ) / math.sqrt(HD)
    positions = jnp.arange(full_len)
    causal = positions[:, None] >= positions[None, :]
    scores = jnp.where(causal, scores, -1e30)
    peak = jnp.max(scores, axis=-1, keepdims=True)
    expo = jnp.exp(scores - peak)
    attention_weights = (expo / jnp.sum(expo, axis=-1, keepdims=True)).astype(jnp.bfloat16)
    context = jnp.einsum(
        "skgij,jskh->iskgh", attention_weights, values, preferred_element_type=jnp.float32
    )
    context = context.astype(jnp.bfloat16).reshape(full_len, slot_count, query_width)
    w_out = wo[0]
    attn_out = lax.psum_scatter(
        jnp.einsum("psf,fd->psd", context, w_out, preferred_element_type=jnp.float32).astype(
            jnp.bfloat16
        ),
        "tp",
        scatter_dimension=0,
        tiled=True,
    ).astype(jnp.float32)
    hidden = slot_rows.astype(jnp.float32) + attn_out
    my_positions = lax.axis_index("tp") * local_len + jnp.arange(local_len)
    is_valid = my_positions[:, None] < slot_len[None, :]
    layer_out = jnp.where(is_valid[:, :, None], hidden, 0.0).astype(jnp.bfloat16)
    layer_out = layer_out.reshape(1, 1, local_len, slot_count, width)
    token_scores = jnp.sum(
        hidden
        * lax.rsqrt(jnp.mean(hidden * hidden, axis=-1, keepdims=True) + norm_eps)
        * head_vec[0],
        axis=-1,
    )
    partial_value = jnp.sum(jnp.where(is_valid, token_scores, 0.0), axis=0)
    team_partial = lax.psum(partial_value, "tp")
    totals = lax.psum(spread_scores(selector, team_partial, n_sec, my_sec), ("sec", "dp"))
    averages = totals / lengths[None, :].astype(jnp.float32)
    owner_sel = (dest_dp[n_sec - 1] == my_dp)[None, :] & (
        dest_slot[n_sec - 1][None, :] == jnp.arange(slot_count)[:, None]
    )
    sample_scores = jnp.sum(jnp.where(owner_sel[:, None, :], averages[None, :, :], 0.0), axis=-1)
    return (layer_out, sample_scores.reshape(1, slot_count, n_sec))


def solution(mesh):
    placed = (
        P(("sec", "dp"), "tp", None),
        P(),
        P(),
        P(),
        P("sec", None, "tp"),
        P("sec", None, None, "tp"),
        P("sec", "tp", None),
        P("sec", None),
        P("sec", None),
    )
    return jax.shard_map(
        on_device,
        mesh=mesh,
        in_specs=placed,
        out_specs=(P("sec", "dp", "tp", None, None), P("dp", None, None)),
        check_vma=False,
    )
```

profile of v0, /device:TPU:8, one launch (start us, length us, event | category | flops | bytes accessed | tf_op | source)
XLA Modules:
  0.0 889.0 jit_solution(1844223595718103655)
XLA Ops:
  7.2 0.9 dynamic-slice_reduce_fusion
  8.1 0.7 gather_fusion
  8.7 6.9 broadcast_select_fusion
  15.6 6.4 all-to-all-start
  22.1 0.6 compare_bitcast_fusion
  22.7 0.5 slice_bitcast_fusion.1
  23.2 359.1 %all-to-all-done = bf16[16,1,64,8192]{3,2,1,0:T(8,128)(2,1)} async-done(((bf16[16,1,64,8192]{3,2,1,0:T(8,128)(2,1)}), bf16[16,1,64,8192]{3,2,1,0:T(8,128)(2,1)}, u32[]{:S(2)}, u32[]{:S(2)}) %all-to-all-start) | async-done | bytes 16777248 | tf_op jit(solution)/shard_map/all_to_all | solution.py:59
  382.3 18.7 %fusion.6 = bf16[64,8192,6]{1,2,0:T(8,128)(2,1)} fusion(bf16[16,1,64,8192]{3,2,1,0:T(8,128)(2,1)} %all-to-all-done, s32[16]{0:T(128)S(1)} %get-tuple-element.19, pred[16]{0:T(512)(128)(4,1)S(1)} %get-tuple-element.17), kind=kOutput, calls=%fused_computation.9 | convolution fusion | flops 100663488 | bytes 23068752 | tf_op jit(solution)/shard_map/km,mpd->pkd/dot_general | solution.py:64
  401.0 10.0 %copy.93 = bf16[64,8192,6]{1,0,2:T(8,128)(2,1)} copy(bf16[64,8192,6]{1,2,0:T(8,128)(2,1)} %fusion.6) | data formatting | bytes 12582912 | tf_op jit(solution)/shard_map/km,mpd->pkd/dot_general | solution.py:64
  411.0 41.7 %copy.81 = bf16[2048,8192]{1,0:T(8,128)(2,1)} copy(bf16[2048,8192]{0,1:T(8,128)(2,1)} %bitcast.95) | data formatting | bytes 67108864 | tf_op jit(solution)/shard_map/psd,dh->psh/dot_general | solution.py:83
  452.7 7.1 slice_bitcast_fusion
  459.8 11.8 %copy.64 = bf16[512,8192]{1,0:T(8,128)(2,1)} copy(bf16[512,8192]{0,1:T(8,128)(2,1)} %slice_bitcast_fusion) | data formatting | bytes 16777216 | tf_op jit(solution)/shard_map/psd,dh->psh/dot_general | solution.py:91
  471.9 93.9 %all-gather.2.cloned.1.call-done = bf16[128,6,8192]{2,0,1:T(8,128)(2,1)} async-done(((bf16[64,6,8192]{2,0,1:T(8,128)(2,1)}), bf16[128,6,8192]{2,0,1:T(8,128)(2,1)}) %all-gather.2.cloned.1.call-update) | async-done | bytes 12582928 | tf_op jit(solution)/shard_map/all_gather | solution.py:72
  565.8 7.1 fusion.3
  572.9 12.2 %fusion.34 = bf16[128,6,512]{2,0,1:T(8,128)(2,1)S(1)} fusion(bf16[1,2,8192,512]{3,2,1,0:T(8,128)(2,1)} %param.14, bf16[128,6,8192]{2,0,1:T(8,128)(2,1)} %all-gather.2.cloned.1.call-done, f32[8192]{0:T(1024)S(1)} %bitcast.105, f32[128,6]{0,1:T(8,128)S(1)} %add_rsqrt_fusion.1), kind=kOutput, calls=%fused_computation.44 | convolution fusion | flops 6468009984 | bytes 21793792 | tf_op jit(solution)/shard_map/psd,dh->psh/dot_general | solution.py:99
  585.1 1.2 copy.78
  586.3 33.3 %fusion.12 = f32[128,6,16,128]{0,3,2,1:T(8,128)S(1)} fusion(bf16[16,128,8192,1]{2,1,0,3:T(8,128)(2,1)} %bitcast.96, bf16[128,6,8192]{2,0,1:T(8,128)(2,1)} %all-gather.2.cloned.1.call-done, f32[8192]{0:T(1024)S(1)} %bitcast.106, f32[128,6]{0,1:T(8,128)S(1)} %add_rsqrt_fusion.1), kind=kOutput, calls=%fused_computation.14 | convolution fusion | flops 25794969600 | bytes 52464640 | tf_op jit(solution)/shard_map/psd,dh->psh/dot_general | solution.py:83
  619.5 2.6 subtract_convert_fusion
  622.1 3.1 copy.67
  625.2 4.1 copy.66
  629.3 11.2 %fusion.14 = f32[128,6,4,128]{0,3,2,1:T(8,128)S(1)} fusion(bf16[4,128,8192,1]{2,1,0,3:T(8,128)(2,1)} %bitcast.98, bf16[128,6,8192]{2,0,1:T(8,128)(2,1)} %all-gather.2.cloned.1.call-done, f32[8192]{0:T(1024)S(1)} %bitcast.107, f32[128,6]{0,1:T(8,128)S(1)} %add_rsqrt_fusion.1), kind=kOutput, calls=%fused_computation.16 | convolution fusion | flops 6467616768 | bytes 22580224 | tf_op jit(solution)/shard_map/psd,dh->psh/dot_general | solution.py:91
  640.7 2.6 fusion.25
  643.4 1.6 fusion.53
  645.0 1.0 fusion.33
  646.0 32.7 %fusion.9 = bf16[128,6,8192]{2,0,1:T(8,128)(2,1)} fusion(bf16[128,6,2048]{0,2,1:T(8,128)(2,1)S(1)} %bitcast.108, bf16[1,2048,8192]{2,1,0:T(8,128)(2,1)} %param.15), kind=kOutput, calls=%fused_computation.13 | convolution fusion | flops 25776095232 | bytes 49283072 | tf_op jit(solution)/shard_map/psf,fd->psd/dot_general | solution.py:130
  678.8 0.5 copy-done.5
  679.6 143.8 %reduce-scatter.2.cloned.1.call-done = bf16[64,6,8192]{2,0,1:T(8,128)(2,1)} async-done(((bf16[128,6,8192]{2,0,1:T(8,128)(2,1)}), bf16[64,6,8192]{2,0,1:T(8,128)(2,1)}) %reduce-scatter.2.cloned.1.call-update) | async-done | bytes 6291472 | tf_op jit(solution)/shard_map/reduce_scatter | solution.py:129
  823.4 12.3 %multiply_reduce_fusion.1 = f32[64,6]{0,1:T(8,128)S(1)} fusion(bf16[64,6,8192]{2,0,1:T(8,128)(2,1)} %reduce-scatter.2.cloned.1.call-done, bf16[64,8192,6]{1,2,0:T(8,128)(2,1)} %fusion.6), kind=kLoop, calls=%fused_computation.20 | loop fusion | flops 15728256 | bytes 12584448 | tf_op jit(solution)/shard_map/reduce_sum | solution.py:144
  835.7 9.5 %multiply_reduce_fusion = (f32[64,6]{0,1:T(8,128)S(1)}, bf16[1,1,64,6,8192]{4,2,3,1,0:T(8,128)(2,1)}) fusion(bf16[64,6,8192]{2,0,1:T(8,128)(2,1)S(1)} %copy-done, f32[8192]{0:T(1024)S(1)} %bitcast.103, f32[64,6]{0,1:T(8,128)S(1)} %add_rsqrt_fusion, pred[64,6]{0,1:T(8,128)(4,1)S(1)} %broadcast_compare_fusion, bf16[64,8192,6]{1,2,0:T(8,128)(2,1)} %fusion.6), kind=kLoop, calls=%fused_computation.19 | loop fusion | flops 25165440 | bytes 18910592 | tf_op jit(solution)/shard_map/reduce_sum | solution.py:142
  845.4 4.9 psum.14
  850.5 30.4 %psum.15 = f32[4,16]{1,0:T(4,128)S(1)} all-reduce(f32[4,16]{1,0:T(4,128)S(1)} %broadcast_select_fusion.1), channel_id=1, replica_groups=mesh['sec'=4,'dp'=4,'tp'=2] {'sec','dp'}, use_global_device_ids=true, to_apply=%region_10.11 | all-reduce | flops 64 | bytes 512 | tf_op jit(solution)/shard_map/psum | solution.py:150
  881.0 0.7 copy.72
  (52 shorter events, 1.4 us)
Async XLA Ops:
  15.6 6.4 copy-start.8
  15.6 7.0 copy-start.11
  15.6 366.6 %all-to-all-start = ((bf16[16,1,64,8192]{3,2,1,0:T(8,128)(2,1)}), bf16[16,1,64,8192]{3,2,1,0:T(8,128)(2,1)}, u32[]{:S(2)}, u32[]{:S(2)}) async-start(bf16[16,1,64,8192]{3,2,1,0:T(8,128)(2,1)} %broadcast_select_fusion), calls=%async_computation | async-start | bytes 33554432 | tf_op jit(solution)/shard_map/all_to_all | solution.py:59
  22.0 543.8 %all-gather.2.cloned.1.call-start = ((), (), s32[]{:S(2)}) async-start(), calls=%async_computation.2 | async-start | bytes 18874368 | tf_op jit(solution)/shard_map/all_gather | solution.py:72
  22.7 378.3 %copy-start.6 = (pred[16]{0:T(512)(128)(4,1)}, pred[16]{0:T(512)(128)(4,1)S(1)}, u32[]{:S(2)}) copy-start(pred[16]{0:T(512)(128)(4,1)S(1)} %get-tuple-element.17) | copy-start | bytes 52
  23.2 377.8 %copy-start.4 = (s32[16]{0:T(128)}, s32[16]{0:T(128)S(1)}, u32[]{:S(2)}) copy-start(s32[16]{0:T(128)S(1)} %get-tuple-element.19) | copy-start | bytes 196
  411.0 412.4 %reduce-scatter.2.cloned.1.call-start = ((), (), s32[]{:S(2)}) async-start(), calls=%async_computation.3 | async-start | bytes 18874368 | tf_op jit(solution)/shard_map/reduce_scatter | solution.py:129
  471.6 101.3 %copy-start.13 = (f32[1,8192]{1,0:T(1,128)S(1)}, f32[1,8192]{1,0:T(1,128)}, u32[]{:S(2)}) copy-start(f32[1,8192]{1,0:T(1,128)} %param.16) | copy-start | bytes 98308
  629.3 11.4 %copy-start.1 = (bf16[128,6,4,4,64]{4,0,3,2,1:T(8,128)(2,1)S(1)}, bf16[128,6,4,4,64]{4,0,3,2,1:T(8,128)(2,1)}, u32[]{:S(2)}) copy-start(bf16[128,6,4,4,64]{4,0,3,2,1:T(8,128)(2,1)} %copy.66) | copy-start | bytes 4718596
  643.3 1.7 copy-start.2
  678.7 0.6 copy-start.5
  678.7 0.6 copy-start.7
  678.7 0.7 copy-start.12
  678.7 0.8 copy-start.9
  678.8 0.8 copy-start.10
  678.8 156.9 %copy-start.3 = (f32[1,8192]{1,0:T(1,128)S(1)}, f32[1,8192]{1,0:T(1,128)}, u32[]{:S(2)}) copy-start(f32[1,8192]{1,0:T(1,128)} %param.17) | copy-start | bytes 98308
  823.4 12.3 %copy-start = (bf16[64,6,8192]{2,0,1:T(8,128)(2,1)S(1)}, bf16[64,6,8192]{2,0,1:T(8,128)(2,1)}, u32[]{:S(2)}) copy-start(bf16[64,6,8192]{2,0,1:T(8,128)(2,1)} %reduce-scatter.2.cloned.1.call-done) | copy-start | bytes 18874372
Sparse Core Ops, SparseCore 0:
  411.1 154.6 all-gather.1
  678.9 144.4 reduce-scatter.1
where the time goes:
time: 903 us; the launch traced here: 889 us
  waiting for transfers between devices  597 us (66%)
  matrix products  112 us (12%)
  local copies, waits for them, and re-layouts  82.3 us (9%)
  other arithmetic  41.7 us (5%)
  blocking collectives  35.3 us (4%)
  between operations  14.7 us (2%)
    all_to_all x1, waiting for transfers between devices, on_device(): lax.all_to_all(outgoing, ('sec', 'dp'), split_axis=0, concat_axis=0, tile...  359 us
    reduce_scatter x1, waiting for transfers between devices, on_device(): lax.psum_scatter(jnp.einsum('psf,fd->psd', context, w_out, preferred_elem...  144 us
    all_gather x1, waiting for transfers between devices, on_device(): block_rows = lax.all_gather(slot_rows, 'tp', axis=0, tiled=True)  93.9 us
    dot_general x1, local copies, waits for them, and re-layouts, on_device(): jnp.einsum('psd,dh->psh', normed, w_query, preferred_element_type=jnp.flo...  41.7 us
    dot_general x1, matrix products, on_device(): jnp.einsum('psd,dh->psh', normed, w_query, preferred_element_type=jnp.flo...  33.3 us
    dot_general x1, matrix products, on_device(): jnp.einsum('psf,fd->psd', context, w_out, preferred_element_type=jnp.floa...  32.7 us
    psum x1, blocking collectives, on_device(): lax.psum(spread_scores(selector, team_partial, n_sec, my_sec), ('sec', 'd...  30.4 us
    dot_general x2, local copies, waits for them, and re-layouts, on_device(): jnp.einsum('psd,dh->psh', normed, w_key, preferred_element_type=jnp.float32)  18.9 us
  transfers between devices with their start and end apart: 3, of which 3 were waited for; matrix products, arithmetic and copies ran while one was open for 7% of the time, Pallas kernels for 0%

commit v1 on v0

v1 whole, which is shorter than its diff:
```python
import functools
import math

import jax
import jax.numpy as jnp
from jax import lax
from jax.experimental import pallas as pl
from jax.experimental.pallas import tpu as pltpu
from jax.sharding import PartitionSpec as P

HD = 128
NORM_EPS = 1e-05
ROPE_THETA = 500000.0
VMEM_BYTES = 56 * 1024 * 1024
N_CHUNKS = 8


def params():
    return pltpu.CompilerParams(vmem_limit_bytes=VMEM_BYTES)


def swap(value, axis, size, step):
    return lax.ppermute(value, axis, [(j, j ^ step) for j in range(size)])


def shift(value, axis, size, step):
    return lax.ppermute(value, axis, [(j, (j + step) % size) for j in range(size)])


def attention_kernel(n_dp, n_tp, x_ref, gain_ref, cos_ref, sin_ref, mask_ref, wq_ref, wkv_ref, out_ref, normed, acc_q, acc_k, acc_v):
    group, step = pl.program_id(0), pl.program_id(1)
    steps, rows, depth = normed.shape
    seq = mask_ref.shape[0]
    width = steps * depth

    @pl.when((group == 0) & (step == 0))
    def _():
        def norm_rows(i, carry):
            at = pl.ds(pl.multiple_of(i * 16, 16), 16)
            x = x_ref[at, :].astype(jnp.float32)
            inv = lax.rsqrt(jnp.sum(x * x, axis=-1, keepdims=True) * (1.0 / width) + NORM_EPS)
            y = (x * inv * gain_ref[...]).astype(jnp.bfloat16)
            for j in range(steps):
                normed[j, at, :] = y[:, j * depth : (j + 1) * depth]
            return carry

        lax.fori_loop(0, rows // 16, norm_rows, 0)

    lhs = normed[step]
    part_q = jnp.dot(lhs, wq_ref[...], preferred_element_type=jnp.float32)
    part_k = jnp.dot(lhs, wkv_ref[0], preferred_element_type=jnp.float32)
    part_v = jnp.dot(lhs, wkv_ref[1], preferred_element_type=jnp.float32)

    @pl.when(step == 0)
    def _():
        acc_q[...] = part_q
        acc_k[...] = part_k
        acc_v[...] = part_v

    @pl.when(step > 0)
    def _():
        acc_q[...] += part_q
        acc_k[...] += part_k
        acc_v[...] += part_v

    @pl.when(step == steps - 1)
    def _():
        cos, sin = cos_ref[...], sin_ref[...]
        causal = mask_ref[...] > 0.0
        block = seq // (n_dp * n_tp)
        kv_here = acc_k.shape[1] // HD
        per_kv = acc_q.shape[1] // acc_k.shape[1]

        def rope(v):
            return (v * cos + pltpu.roll(v, HD // 2, 1) * sin).astype(jnp.bfloat16)

        for s in range(rows // seq):
            at = slice(s * seq, (s + 1) * seq)
            for j in range(kv_here):
                cols = slice(j * HD, (j + 1) * HD)
                keys = rope(acc_k[at, cols])
                values = acc_v[at, cols].astype(jnp.bfloat16)
                for h in range(per_kv):
                    head = j * per_kv + h
                    hcols = slice(head * HD, (head + 1) * HD)
                    queries = rope(acc_q[at, hcols])
                    scores = lax.dot_general(
                        queries, keys, (((1,), (1,)), ((), ())), preferred_element_type=jnp.float32
                    ) * (1.0 / math.sqrt(HD))
                    scores = jnp.where(causal, scores, -1e30)
                    expo = jnp.exp(scores - jnp.max(scores, axis=-1, keepdims=True))
                    weights = (expo / jnp.sum(expo, axis=-1, keepdims=True)).astype(jnp.bfloat16)
                    context = jnp.dot(weights, values, preferred_element_type=jnp.float32).astype(jnp.bfloat16)
                    for t in range(n_tp):
                        for z in range(n_dp):
                            start = (t * n_dp + z) * block
                            out_ref[z, t, s, :, hcols] = context[start : start + block]


def attention(rows_in, gain, cos, sin, mask, wq, wkv, n_dp, n_tp):
    rows, width = rows_in.shape
    seq = mask.shape[0]
    q_width, kv_width = wq.shape[2], wkv.shape[3]
    kv_block = min(2 * HD, kv_width)
    groups = kv_width // kv_block
    q_block = q_width // groups
    steps = 4
    depth = width // steps
    samples = rows // seq
    block = seq // (n_dp * n_tp)
    fixed = lambda g, k: (0, 0)
    return pl.pallas_call(
        functools.partial(attention_kernel, n_dp, n_tp),
        out_shape=jax.ShapeDtypeStruct((n_dp, n_tp, samples, block, q_width), jnp.bfloat16),
        grid=(groups, steps),
        in_specs=[
            pl.BlockSpec((rows, width), fixed),
            pl.BlockSpec((1, width), fixed),
            pl.BlockSpec((seq, HD), fixed),
            pl.BlockSpec((seq, HD), fixed),
            pl.BlockSpec((seq, seq), fixed),
            pl.BlockSpec((None, depth, q_block), lambda g, k: (0, k, g)),
            pl.BlockSpec((None, 2, depth, kv_block), lambda g, k: (0, 0, k, g)),
        ],
        out_specs=pl.BlockSpec((n_dp, n_tp, samples, block, q_block), lambda g, k: (0, 0, 0, 0, g)),
        scratch_shapes=[
            pltpu.VMEM((steps, rows, depth), jnp.bfloat16),
            pltpu.VMEM((rows, q_block), jnp.float32),
            pltpu.VMEM((rows, kv_block), jnp.float32),
            pltpu.VMEM((rows, kv_block), jnp.float32),
        ],
        compiler_params=params(),
        cost_estimate=pl.CostEstimate(
            flops=2 * rows * width * (q_width + 2 * kv_width),
            bytes_accessed=2 * width * (q_width + 2 * kv_width) + 4 * rows * width,
            transcendentals=0,
        ),
        name="project_and_attend",
    )(rows_in, gain, cos, sin, mask, wq, wkv)


def out_kernel(ctx_ref, wo_ref, own_ref, send_ref):
    full = jnp.dot(ctx_ref[...], wo_ref[...], preferred_element_type=jnp.float32).astype(jnp.bfloat16)
    mine = own_ref.shape[0]
    own_ref[...] = full[:mine]
    send_ref[...] = full[mine:]


def out_projection(ctx, wo, mine, chunk, cols):
    rows, depth = ctx.shape
    col_block = min(512, cols)
    inner = cols // col_block
    return pl.pallas_call(
        out_kernel,
        out_shape=[
            jax.ShapeDtypeStruct((mine, cols), jnp.bfloat16),
            jax.ShapeDtypeStruct((rows - mine, cols), jnp.bfloat16),
        ],
        grid=(inner,),
        in_specs=[
            pl.BlockSpec((rows, depth), lambda n: (0, 0)),
            pl.BlockSpec((None, depth, col_block), lambda n: (0, 0, chunk * inner + n)),
        ],
        out_specs=[
            pl.BlockSpec((mine, col_block), lambda n: (0, n)),
            pl.BlockSpec((rows - mine, col_block), lambda n: (0, n)),
        ],
        compiler_params=params(),
        cost_estimate=pl.CostEstimate(
            flops=2 * rows * depth * cols,
            bytes_accessed=2 * depth * cols + 2 * rows * (depth + cols),
            transcendentals=0,
        ),
        name="out_projection",
    )(ctx, wo)


def join_kernel(n_slots, block, table_ref, own_ref, other_ref, resid_ref, head_ref, packed_ref, stats_ref):
    dest = pl.program_id(0)
    head = head_ref[...]
    lane = lax.broadcasted_iota(jnp.int32, (block, HD), 1)
    row = lax.broadcasted_iota(jnp.int32, (block, 1), 0)

    def one_slot(slot, carry):
        entry = dest * n_slots + slot
        part, resid, live = table_ref[0, entry], table_ref[1, entry], table_ref[2, entry]
        added = own_ref[part].astype(jnp.float32)
        for k in range(other_ref.shape[0]):
            added = added + other_ref[k, part].astype(jnp.float32)
        hidden = resid_ref[resid].astype(jnp.float32) + added
        packed_ref[slot] = jnp.where(row < live, hidden, 0.0).astype(jnp.bfloat16)
        squares = jnp.sum(hidden * hidden, axis=-1, keepdims=True)
        scored = jnp.sum(hidden * head, axis=-1, keepdims=True)
        stats_ref[slot] = jnp.where(lane == 0, squares, jnp.where(lane == 1, scored, 0.0))
        return carry

    lax.fori_loop(0, n_slots, one_slot, 0)


def join(table, own, other, resid, head, chunk, n_dp, n_slots, block):
    blocks, _, cols = own.shape
    return pl.pallas_call(
        functools.partial(join_kernel, n_slots, block),
        out_shape=[
            jax.ShapeDtypeStruct((n_dp, n_slots, block, cols), jnp.bfloat16),
            jax.ShapeDtypeStruct((n_dp, n_slots, block, HD), jnp.float32),
        ],
        grid_spec=pltpu.PrefetchScalarGridSpec(
            num_scalar_prefetch=1,
            grid=(n_dp,),
            in_specs=[
                pl.BlockSpec(own.shape, lambda d, t: (0, 0, 0)),
                pl.BlockSpec(other.shape, lambda d, t: (0, 0, 0, 0)),
                pl.BlockSpec((blocks, block, cols), lambda d, t: (0, 0, chunk)),
                pl.BlockSpec((1, cols), lambda d, t: (0, chunk)),
            ],
            out_specs=[
                pl.BlockSpec((None, n_slots, block, cols), lambda d, t: (d, 0, 0, 0)),
                pl.BlockSpec((None, n_slots, block, HD), lambda d, t: (d, 0, 0, 0)),
            ],
        ),
        compiler_params=params(),
        cost_estimate=pl.CostEstimate(
            flops=12 * n_dp * n_slots * block * cols,
            bytes_accessed=2 * cols * block * (3 * blocks + n_dp * n_slots),
            transcendentals=0,
        ),
        name="join_partials",
    )(table, own, other, resid, head)


def place_kernel(count, order_ref, *refs):
    out_ref = refs[-1]
    for k in range(count):
        out_ref[:, order_ref[k]] = refs[k][...]


def place(order, pieces, whole, chunk, width):
    n_slots, block, cols = pieces[0].shape
    count = len(pieces)
    specs = [pl.BlockSpec((n_slots, block, cols), lambda i, o: (0, 0, 0)) for _ in pieces]
    operands = list(pieces)
    aliases = {}
    if whole is not None:
        specs.append(pl.BlockSpec(memory_space=pl.ANY))
        operands.append(whole)
        aliases = {1 + len(pieces): 0}
    return pl.pallas_call(
        functools.partial(place_kernel, count),
        out_shape=jax.ShapeDtypeStruct((n_slots, count, block, width), jnp.bfloat16),
        grid_spec=pltpu.PrefetchScalarGridSpec(
            num_scalar_prefetch=1,
            grid=(1,),
            in_specs=specs,
            out_specs=pl.BlockSpec((n_slots, count, block, cols), lambda i, o: (0, 0, 0, chunk)),
        ),
        input_output_aliases=aliases,
        compiler_params=params(),
        cost_estimate=pl.CostEstimate(
            flops=0, bytes_accessed=4 * n_slots * count * block * cols, transcendentals=0
        ),
        name="place_rows",
    )(order, *operands)


def on_device(responses, lengths, dest_dp, dest_slot, wq, wkv, wo, norm_gain, head_vec):
    n_sec = lax.axis_size("sec")
    n_dp = lax.axis_size("dp")
    n_tp = lax.axis_size("tp")
    _, local_len, width = responses.shape
    samples = lengths.shape[0]
    n_slots = 3 * samples // (2 * n_dp)
    seq = local_len * n_tp
    block = local_len // n_dp
    my_sec, my_dp, my_tp = lax.axis_index("sec"), lax.axis_index("dp"), lax.axis_index("tp")

    mine = responses[0]
    near = [mine] + [shift(mine, "tp", n_tp, k) for k in range(1, n_tp)]
    far_mine = swap(mine, "sec", n_sec, 2)
    half = local_len // 2
    far = [far_mine]
    for k in range(1, n_tp):
        upper = shift(far_mine[:half], "tp", n_tp, k)
        lower = swap(near[k][half:], "sec", n_sec, 2)
        far.append(jnp.concatenate([upper, lower], axis=0))
    near_pair = [swap(v, "sec", n_sec, 1) for v in near]
    far_pair = [swap(v, "sec", n_sec, 1) for v in far]
    batches = [near + near_pair, far + far_pair]

    quarter = lambda v, k: lax.dynamic_slice_in_dim(v, lax.rem(my_dp + k, n_dp) * block, block, 0)
    resid_0 = jnp.concatenate(
        [quarter(mine, 0)] + [shift(quarter(mine, k), "dp", n_dp, k) for k in range(1, n_dp)], axis=0
    )
    resid_0 = resid_0.reshape(n_dp, block, width)
    resid_2 = swap(resid_0, "sec", n_sec, 2)
    resid = jnp.concatenate(
        [resid_0, swap(resid_0, "sec", n_sec, 1), resid_2, swap(resid_2, "sec", n_sec, 1)], axis=0
    )

    owners = lax.rem(my_tp - jnp.arange(n_tp) + n_tp, n_tp)
    positions = (owners[:, None] * local_len + jnp.arange(local_len)[None, :]).reshape(seq)
    frequency = jnp.exp(jnp.arange(HD // 2, dtype=jnp.float32) * (-2.0 * math.log(ROPE_THETA) / HD))
    angles = positions.astype(jnp.float32)[:, None] * frequency[None, :]
    cos = jnp.tile(jnp.cos(angles), (1, 2))
    sin = jnp.concatenate([-jnp.sin(angles), jnp.sin(angles)], axis=1)
    mask = (positions[:, None] >= positions[None, :]).astype(jnp.float32)

    spread = []
    for rows in batches:
        ctx = attention(jnp.concatenate(rows, axis=0), norm_gain, cos, sin, mask, wq, wkv, n_dp, n_tp)
        for k in range(n_dp):
            piece = lax.dynamic_index_in_dim(ctx, lax.rem(my_dp + k, n_dp), 0, keepdims=False)
            spread.append(shift(piece, "dp", n_dp, k) if k else piece)
    q_width = wq.shape[2]
    ctx_rows = jnp.stack(spread, axis=1).reshape(-1, q_width)
    owned = ctx_rows.shape[0] // n_tp

    row_dp = lax.dynamic_index_in_dim(dest_dp, my_sec, 0, keepdims=False)
    row_slot = lax.dynamic_index_in_dim(dest_slot, my_sec, 0, keepdims=False)
    sample = jnp.arange(samples)
    i_rel = my_sec ^ (sample // n_dp)
    k_rel = lax.rem(my_dp - sample % n_dp + n_dp, n_dp)
    part_at = ((i_rel // 2) * n_dp + k_rel) * 2 + i_rel % 2
    resid_at = i_rel * n_dp + k_rel
    dests = lax.rem(my_dp + jnp.arange(n_dp), n_dp)
    chosen = (row_dp[None, None, :] == dests[:, None, None]) & (
        row_slot[None, None, :] == jnp.arange(n_slots)[None, :, None]
    )
    first_pos = my_tp * local_len + my_dp * block
    live = jnp.clip(lengths - first_pos, 0, block)
    pick = lambda v: jnp.sum(jnp.where(chosen, v[None, None, :], 0), axis=-1).reshape(-1)
    table = jnp.stack([pick(part_at), pick(resid_at), pick(live)]).astype(jnp.int32)
    order = lax.rem(my_dp - jnp.arange(n_dp) + n_dp, n_dp).astype(jnp.int32)

    cols = width // N_CHUNKS
    whole, stats = None, 0.0
    for chunk in range(N_CHUNKS):
        own, send = out_projection(ctx_rows, wo, owned, chunk, cols)
        own = own.reshape(-1, block, cols)
        send = send.reshape(n_tp - 1, -1, block, cols)
        other = jnp.stack([shift(send[k - 1], "tp", n_tp, n_tp - k) for k in range(1, n_tp)])
        packed, part_stats = join(table, own, other, resid, head_vec, chunk, n_dp, n_slots, block)
        stats = stats + part_stats[..., :2]
        pieces = [packed[0]] + [shift(packed[k], "dp", n_dp, k) for k in range(1, n_dp)]
        whole = place(order, pieces, whole, chunk, width)
    layer_out = jnp.transpose(whole.reshape(n_slots, local_len, width), (1, 0, 2))[None, None]

    token_scores = stats[..., 1] * lax.rsqrt(stats[..., 0] * (1.0 / width) + NORM_EPS)
    is_live = jnp.arange(block)[None, None, :] < table[2].reshape(n_dp, n_slots, 1)
    slot_sums = jnp.sum(jnp.where(is_live, token_scores, 0.0), axis=-1)
    by_sample = jnp.sum(jnp.where(chosen, slot_sums[:, :, None], 0.0), axis=(0, 1))
    by_model = jnp.where(jnp.arange(n_sec)[:, None] == my_sec, by_sample[None, :], 0.0)
    totals = lax.psum(by_model, ("sec", "dp", "tp"))
    averages = totals / lengths[None, :].astype(jnp.float32)
    owner = (dest_dp[n_sec - 1] == my_dp)[None, :] & (
        dest_slot[n_sec - 1][None, :] == jnp.arange(n_slots)[:, None]
    )
    sample_scores = jnp.sum(jnp.where(owner[:, None, :], averages[None, :, :], 0.0), axis=-1)
    return layer_out, sample_scores[None]


def solution(mesh):
    placed = (
        P(("sec", "dp"), "tp", None),
        P(),
        P(),
        P(),
        P("sec", None, "tp"),
        P("sec", None, None, "tp"),
        P("sec", "tp", None),
        P("sec", None),
        P("sec", None),
    )
    return jax.shard_map(
        on_device,
        mesh=mesh,
        in_specs=placed,
        out_specs=(P("sec", "dp", "tp", None, None), P("dp", None, None)),
        check_vma=False,
    )
```

time: 903 us -> 495 us (0.55)
  waiting for transfers between devices: 597 us -> 138 us
  Pallas kernels: 0 us -> 187 us
  matrix products: 112 us -> 0 us
  starting transfers between devices: 6.48 us -> 77.7 us
  local copies, waits for them, and re-layouts: 82.3 us -> 25.5 us
  other arithmetic: 41.7 us -> 17.4 us
  between operations: 14.7 us -> 1.21 us
    all_to_all x1 -> x0, waiting for transfers between devices: 359 us -> none  [on_device(): lax.all_to_all(outgoing, ('sec', 'dp'), split_axis=0, concat_axis=0, tile...]
    pallas_call x0 -> x26, Pallas kernels: none -> 187 us  [the longest x2 76.9 us: attention(): pl.pallas_call(functools.partial(attention_kernel, n_dp, n_tp), out_shape...]
    reduce_scatter x1 -> x0, waiting for transfers between devices: 144 us -> none  [on_device(): lax.psum_scatter(jnp.einsum('psf,fd->psd', context, w_out, preferred_elem...]
    ppermute x0 -> x52, waiting for transfers between devices: none -> 138 us  [the longest x43 118 us: shift(): lax.ppermute(value, axis, [(j, (j + step) % size) for j in range(size)])]
    dot_general x7 -> x0, matrix products: 112 us -> none  [the longest x1 33.3 us: on_device(): jnp.einsum('psd,dh->psh', normed, w_query, preferred_element_type=jnp.flo...]
    all_gather x1 -> x0, waiting for transfers between devices: 93.9 us -> none  [on_device(): block_rows = lax.all_gather(slot_rows, 'tp', axis=0, tiled=True)]
    ppermute x0 -> x52, starting transfers between devices: none -> 77.7 us  [the longest x43 73.5 us: shift(): lax.ppermute(value, axis, [(j, (j + step) % size) for j in range(size)])]
    dot_general x4 -> x0, local copies, waits for them, and re-layouts: 70.6 us -> none  [the longest x1 41.7 us: on_device(): jnp.einsum('psd,dh->psh', normed, w_query, preferred_element_type=jnp.flo...]
  transfers between devices with their start and end apart: 3 -> 52, of which waited for: 3 -> 24; matrix products, arithmetic and copies ran while one was open for 7% -> 8% of each run, Pallas kernels for 0% -> 33%
where the time goes in v1:
time: 495 us; the launch traced here: 486 us
  Pallas kernels  187 us (38%)
  waiting for transfers between devices  138 us (28%)
  starting transfers between devices  77.7 us (16%)
  blocking collectives  38.6 us (8%)
  local copies, waits for them, and re-layouts  25.5 us (5%)
  other arithmetic  17.4 us (4%)
    ppermute x43, waiting for transfers between devices, shift(): lax.ppermute(value, axis, [(j, (j + step) % size) for j in range(size)])  118 us
    pallas_call x2, Pallas kernels, attention(): pl.pallas_call(functools.partial(attention_kernel, n_dp, n_tp), out_shape...  76.9 us
    ppermute x43, starting transfers between devices, shift(): lax.ppermute(value, axis, [(j, (j + step) % size) for j in range(size)])  73.5 us
    pallas_call x8, Pallas kernels, out_projection(): pl.pallas_call(out_kernel, out_shape=[jax.ShapeDtypeStruct((mine, cols),...  44.5 us
    pallas_call x8, Pallas kernels, join(): pl.pallas_call(functools.partial(join_kernel, n_slots, block), out_shape=...  43.4 us
    psum x1, blocking collectives, on_device(): totals = lax.psum(by_model, ('sec', 'dp', 'tp'))  38.6 us
    pallas_call x8, Pallas kernels, place(): pl.pallas_call(functools.partial(place_kernel, count), out_shape=jax.Shap...  22.5 us
    ppermute x9, waiting for transfers between devices, swap(): return lax.ppermute(value, axis, [(j, j ^ step) for j in range(size)])  19.6 us
  transfers between devices with their start and end apart: 52, of which 24 were waited for; matrix products, arithmetic and copies ran while one was open for 8% of the time, Pallas kernels for 33%

profile of v1, /device:TPU:8, one launch (start us, length us, event | category | flops | bytes accessed | tf_op | source)
XLA Modules:
  0.0 485.8 jit_solution(1790434781374638152)
XLA Ops:
  18.3 6.3 %collective-permute-done.15 = bf16[16,8192]{1,0:T(8,128)(2,1)S(1)} collective-permute-done((bf16[16,8192]{1,0:T(8,128)(2,1)S(1)}, bf16[16,8192]{1,0:T(8,128)(2,1)S(1)}, u32[]{:S(2)}, u32[]{:S(2)}) %collective-permute-start.15) | collective-permute-done | bytes 262176 | tf_op jit(solution)/shard_map/ppermute | solution.py:27
  32.5 11.1 %collective-permute-done.7 = bf16[32,8192]{1,0:T(8,128)(2,1)S(1)} collective-permute-done((bf16[32,8192]{1,0:T(8,128)(2,1)S(1)}, bf16[32,8192]{1,0:T(8,128)(2,1)S(1)}, u32[]{:S(2)}, u32[]{:S(2)}) %collective-permute-start.7) | collective-permute-done | bytes 524320 | tf_op jit(solution)/shard_map/ppermute | solution.py:27
  43.6 11.2 %collective-permute-done.19 = bf16[4,16,8192]{2,1,0:T(8,128)(2,1)} collective-permute-done((bf16[4,16,8192]{2,1,0:T(8,128)(2,1)S(1)}, bf16[4,16,8192]{2,1,0:T(8,128)(2,1)}, u32[]{:S(2)}, u32[]{:S(2)}) %collective-permute-start.19) | collective-permute-done | bytes 1048608 | tf_op jit(solution)/shard_map/ppermute | solution.py:23
  54.8 8.4 %collective-permute-done.8 = bf16[32,8192]{1,0:T(8,128)(2,1)S(1)} collective-permute-done((bf16[32,8192]{1,0:T(8,128)(2,1)S(1)}, bf16[32,8192]{1,0:T(8,128)(2,1)S(1)}, u32[]{:S(2)}, u32[]{:S(2)}) %collective-permute-start.8) | collective-permute-done | bytes 524320 | tf_op jit(solution)/shard_map/ppermute | solution.py:23
  68.2 38.5 %project_and_attend.2 = bf16[4,2,2,16,2048]{4,3,2,1,0:T(8,128)(2,1)} custom-call(bf16[256,8192]{1,0:T(8,128)(2,1)} %pad_maximum_fusion.x_ref, f32[1,8192]{1,0:T(1,128)} %gain_ref.3, f32[128,128]{1,0:T(8,128)} %copy.43.cos_ref, f32[128,128]{1,0:T(8,128)} %pad_maximum_fusion.4.sin_ref, f32[128,128]{1,0:T(8,128)} %compare_convert_fusion.mask_ref, ...), custom_call_target="tpu_custom_call" | custom-call | flops 12884901888 | bytes 58720256 | tf_op jit(solution)/shard_map/project_and_attend/pallas_call | solution.py:112
  115.1 9.9 %collective-permute-done.3 = bf16[2,2,16,2048]{3,2,1,0:T(8,128)(2,1)S(1)} collective-permute-done((bf16[2,2,16,2048]{3,2,1,0:T(8,128)(2,1)S(1)}, bf16[2,2,16,2048]{3,2,1,0:T(8,128)(2,1)S(1)}, u32[]{:S(2)}, u32[]{:S(2)}) %collective-permute-start.3) | collective-permute-done | bytes 262176 | tf_op jit(solution)/shard_map/ppermute | solution.py:27
  125.9 10.2 %collective-permute-done.4 = bf16[2,2,16,2048]{3,2,1,0:T(8,128)(2,1)S(1)} collective-permute-done((bf16[2,2,16,2048]{3,2,1,0:T(8,128)(2,1)S(1)}, bf16[2,2,16,2048]{3,2,1,0:T(8,128)(2,1)S(1)}, u32[]{:S(2)}, u32[]{:S(2)}) %collective-permute-start.4) | collective-permute-done | bytes 262176 | tf_op jit(solution)/shard_map/ppermute | solution.py:27
  143.1 38.4 %project_and_attend.3 = bf16[4,2,2,16,2048]{4,3,2,1,0:T(8,128)(2,1)} custom-call(bf16[256,8192]{1,0:T(8,128)(2,1)} %copy-done.1, f32[1,8192]{1,0:T(1,128)} %gain_ref.3, f32[128,128]{1,0:T(8,128)} %copy.43.cos_ref, f32[128,128]{1,0:T(8,128)} %pad_maximum_fusion.4.sin_ref, f32[128,128]{1,0:T(8,128)} %compare_convert_fusion.mask_ref, ...), custom_call_target="tpu_custom_call" | custom-call | flops 12884901888 | bytes 58720256 | tf_op jit(solution)/shard_map/project_and_attend/pallas_call | solution.py:112
  193.8 12.7 %collective-permute-done.12 = bf16[2,2,16,2048]{3,2,1,0:T(8,128)(2,1)S(1)} collective-permute-done((bf16[2,2,16,2048]{3,2,1,0:T(8,128)(2,1)S(1)}, bf16[2,2,16,2048]{3,2,1,0:T(8,128)(2,1)S(1)}, u32[]{:S(2)}, u32[]{:S(2)}) %collective-permute-start.12) | collective-permute-done | bytes 262176 | tf_op jit(solution)/shard_map/ppermute | solution.py:27
  207.9 5.5 %out_projection.15 = (bf16[256,1024]{1,0:T(8,128)(2,1)}, bf16[256,1024]{1,0:T(8,128)(2,1)}) custom-call(bf16[512,2048]{1,0:T(8,128)(2,1)} %bitcast.150, bf16[1,2048,8192]{2,1,0:T(8,128)(2,1)} %wo_ref.15), custom_call_target="tpu_custom_call" | custom-call | flops 2147483648 | bytes 7340032 | tf_op jit(solution)/shard_map/out_projection/pallas_call | solution.py:153
  213.4 5.6 %out_projection.14 = (bf16[256,1024]{1,0:T(8,128)(2,1)}, bf16[256,1024]{1,0:T(8,128)(2,1)}) custom-call(bf16[512,2048]{1,0:T(8,128)(2,1)} %bitcast.151, bf16[1,2048,8192]{2,1,0:T(8,128)(2,1)} %wo_ref.15), custom_call_target="tpu_custom_call" | custom-call | flops 2147483648 | bytes 7340032 | tf_op jit(solution)/shard_map/out_projection/pallas_call | solution.py:153
  219.0 5.5 %out_projection.13 = (bf16[256,1024]{1,0:T(8,128)(2,1)}, bf16[256,1024]{1,0:T(8,128)(2,1)}) custom-call(bf16[512,2048]{1,0:T(8,128)(2,1)} %bitcast.152, bf16[1,2048,8192]{2,1,0:T(8,128)(2,1)} %wo_ref.15), custom_call_target="tpu_custom_call" | custom-call | flops 2147483648 | bytes 7340032 | tf_op jit(solution)/shard_map/out_projection/pallas_call | solution.py:153
  224.5 5.7 %out_projection.12 = (bf16[256,1024]{1,0:T(8,128)(2,1)}, bf16[256,1024]{1,0:T(8,128)(2,1)}) custom-call(bf16[512,2048]{1,0:T(8,128)(2,1)} %bitcast.153, bf16[1,2048,8192]{2,1,0:T(8,128)(2,1)} %wo_ref.15), custom_call_target="tpu_custom_call" | custom-call | flops 2147483648 | bytes 7340032 | tf_op jit(solution)/shard_map/out_projection/pallas_call | solution.py:153
  232.8 5.6 %out_projection.11 = (bf16[256,1024]{1,0:T(8,128)(2,1)}, bf16[256,1024]{1,0:T(8,128)(2,1)}) custom-call(bf16[512,2048]{1,0:T(8,128)(2,1)} %bitcast.154, bf16[1,2048,8192]{2,1,0:T(8,128)(2,1)} %wo_ref.15), custom_call_target="tpu_custom_call" | custom-call | flops 2147483648 | bytes 7340032 | tf_op jit(solution)/shard_map/out_projection/pallas_call | solution.py:153
  238.3 5.5 %out_projection.10 = (bf16[256,1024]{1,0:T(8,128)(2,1)}, bf16[256,1024]{1,0:T(8,128)(2,1)}) custom-call(bf16[512,2048]{1,0:T(8,128)(2,1)} %bitcast.155, bf16[1,2048,8192]{2,1,0:T(8,128)(2,1)} %wo_ref.15), custom_call_target="tpu_custom_call" | custom-call | flops 2147483648 | bytes 7340032 | tf_op jit(solution)/shard_map/out_projection/pallas_call | solution.py:153
  243.9 5.6 %out_projection.9 = (bf16[256,1024]{1,0:T(8,128)(2,1)}, bf16[256,1024]{1,0:T(8,128)(2,1)}) custom-call(bf16[512,2048]{1,0:T(8,128)(2,1)} %bitcast.156, bf16[1,2048,8192]{2,1,0:T(8,128)(2,1)} %wo_ref.15), custom_call_target="tpu_custom_call" | custom-call | flops 2147483648 | bytes 7340032 | tf_op jit(solution)/shard_map/out_projection/pallas_call | solution.py:153
  256.8 5.5 %out_projection.8 = (bf16[256,1024]{1,0:T(8,128)(2,1)}, bf16[256,1024]{1,0:T(8,128)(2,1)}) custom-call(bf16[512,2048]{1,0:T(8,128)(2,1)} %bitcast.157, bf16[1,2048,8192]{2,1,0:T(8,128)(2,1)} %wo_ref.15), custom_call_target="tpu_custom_call" | custom-call | flops 2147483648 | bytes 7340032 | tf_op jit(solution)/shard_map/out_projection/pallas_call | solution.py:153
  262.4 5.4 %join_partials.15 = (bf16[4,6,16,1024]{3,2,1,0:T(8,128)(2,1)}, f32[4,6,16,128]{3,2,1,0:T(8,128)}) custom-call(s32[3,24]{1,0:T(4,128)} %pad_add_fusion.table_ref, bf16[16,16,1024]{2,1,0:T(8,128)(2,1)} %bitcast.178, bf16[1,16,16,1024]{3,2,1,0:T(8,128)(2,1)} %bitcast.180, bf16[16,16,8192]{2,1,0:T(8,128)(2,1)} %pad_maximum_fusion.1.resid_ref, f32[1,8192]{1,0:T(1,128)} %head_ref.15), custom_call_target="tpu_custom_call" | custom-call | flops 4718592 | bytes 2359296 | tf_op jit(solution)/shard_map/join_partials/pallas_call | solution.py:202
  267.8 5.5 %join_partials.14 = (bf16[4,6,16,1024]{3,2,1,0:T(8,128)(2,1)}, f32[4,6,16,128]{3,2,1,0:T(8,128)}) custom-call(s32[3,24]{1,0:T(4,128)} %pad_add_fusion.table_ref, bf16[16,16,1024]{2,1,0:T(8,128)(2,1)} %bitcast.177, bf16[1,16,16,1024]{3,2,1,0:T(8,128)(2,1)} %bitcast.179, bf16[16,16,8192]{2,1,0:T(8,128)(2,1)} %pad_maximum_fusion.1.resid_ref, f32[1,8192]{1,0:T(1,128)} %head_ref.15), custom_call_target="tpu_custom_call" | custom-call | flops 4718592 | bytes 2359296 | tf_op jit(solution)/shard_map/join_partials/pallas_call | solution.py:202
  277.9 5.4 %join_partials.13 = (bf16[4,6,16,1024]{3,2,1,0:T(8,128)(2,1)}, f32[4,6,16,128]{3,2,1,0:T(8,128)}) custom-call(s32[3,24]{1,0:T(4,128)} %pad_add_fusion.table_ref, bf16[16,16,1024]{2,1,0:T(8,128)(2,1)} %bitcast.173, bf16[1,16,16,1024]{3,2,1,0:T(8,128)(2,1)} %bitcast.176, bf16[16,16,8192]{2,1,0:T(8,128)(2,1)} %pad_maximum_fusion.1.resid_ref, f32[1,8192]{1,0:T(1,128)} %head_ref.15), custom_call_target="tpu_custom_call" | custom-call | flops 4718592 | bytes 2359296 | tf_op jit(solution)/shard_map/join_partials/pallas_call | solution.py:202
  293.4 5.4 %join_partials.11 = (bf16[4,6,16,1024]{3,2,1,0:T(8,128)(2,1)}, f32[4,6,16,128]{3,2,1,0:T(8,128)}) custom-call(s32[3,24]{1,0:T(4,128)} %pad_add_fusion.table_ref, bf16[16,16,1024]{2,1,0:T(8,128)(2,1)} %bitcast.169, bf16[1,16,16,1024]{3,2,1,0:T(8,128)(2,1)} %bitcast.174, bf16[16,16,8192]{2,1,0:T(8,128)(2,1)} %pad_maximum_fusion.1.resid_ref, f32[1,8192]{1,0:T(1,128)} %head_ref.15), custom_call_target="tpu_custom_call" | custom-call | flops 4718592 | bytes 2359296 | tf_op jit(solution)/shard_map/join_partials/pallas_call | solution.py:202
  303.3 5.5 %join_partials.10 = (bf16[4,6,16,1024]{3,2,1,0:T(8,128)(2,1)}, f32[4,6,16,128]{3,2,1,0:T(8,128)}) custom-call(s32[3,24]{1,0:T(4,128)} %pad_add_fusion.table_ref, bf16[16,16,1024]{2,1,0:T(8,128)(2,1)} %bitcast.167, bf16[1,16,16,1024]{3,2,1,0:T(8,128)(2,1)} %bitcast.172, bf16[16,16,8192]{2,1,0:T(8,128)(2,1)} %pad_maximum_fusion.1.resid_ref, f32[1,8192]{1,0:T(1,128)} %head_ref.15), custom_call_target="tpu_custom_call" | custom-call | flops 4718592 | bytes 2359296 | tf_op jit(solution)/shard_map/join_partials/pallas_call | solution.py:202
  316.4 5.4 %join_partials.9 = (bf16[4,6,16,1024]{3,2,1,0:T(8,128)(2,1)}, f32[4,6,16,128]{3,2,1,0:T(8,128)}) custom-call(s32[3,24]{1,0:T(4,128)} %pad_add_fusion.table_ref, bf16[16,16,1024]{2,1,0:T(8,128)(2,1)} %bitcast.166, bf16[1,16,16,1024]{3,2,1,0:T(8,128)(2,1)} %bitcast.170, bf16[16,16,8192]{2,1,0:T(8,128)(2,1)} %pad_maximum_fusion.1.resid_ref, f32[1,8192]{1,0:T(1,128)} %head_ref.15), custom_call_target="tpu_custom_call" | custom-call | flops 4718592 | bytes 2359296 | tf_op jit(solution)/shard_map/join_partials/pallas_call | solution.py:202
  325.0 5.5 %join_partials.8 = (bf16[4,6,16,1024]{3,2,1,0:T(8,128)(2,1)}, f32[4,6,16,128]{3,2,1,0:T(8,128)}) custom-call(s32[3,24]{1,0:T(4,128)} %pad_add_fusion.table_ref, bf16[16,16,1024]{2,1,0:T(8,128)(2,1)} %bitcast.165, bf16[1,16,16,1024]{3,2,1,0:T(8,128)(2,1)} %bitcast.171, bf16[16,16,8192]{2,1,0:T(8,128)(2,1)} %pad_maximum_fusion.1.resid_ref, f32[1,8192]{1,0:T(1,128)} %head_ref.15), custom_call_target="tpu_custom_call" | custom-call | flops 4718592 | bytes 2359296 | tf_op jit(solution)/shard_map/join_partials/pallas_call | solution.py:202
  333.5 38.6 %psum.7 = f32[4,16]{1,0:T(4,128)S(1)} all-reduce(f32[4,16]{1,0:T(4,128)S(1)} %broadcast_select_fusion), channel_id=1, replica_groups=mesh['sec'=4,'dp'=4,'tp'=2] {'sec','dp','tp'}, use_global_device_ids=true, to_apply=%region_5.6 | all-reduce | flops 64 | bytes 512 | tf_op jit(solution)/shard_map/psum | solution.py:353
  380.0 8.1 %collective-permute-done.45.refs_1_ = bf16[6,16,1024]{2,1,0:T(8,128)(2,1)S(1)} collective-permute-done((bf16[6,16,1024]{2,1,0:T(8,128)(2,1)}, bf16[6,16,1024]{2,1,0:T(8,128)(2,1)S(1)}, u32[]{:S(2)}, u32[]{:S(2)}) %collective-permute-start.45) | collective-permute-done | bytes 196640 | tf_op jit(solution)/shard_map/ppermute | solution.py:27
  391.3 9.4 %collective-permute-done.42.refs_2_ = bf16[6,16,1024]{2,1,0:T(8,128)(2,1)S(1)} collective-permute-done((bf16[6,16,1024]{2,1,0:T(8,128)(2,1)}, bf16[6,16,1024]{2,1,0:T(8,128)(2,1)S(1)}, u32[]{:S(2)}, u32[]{:S(2)}) %collective-permute-start.42) | collective-permute-done | bytes 196640 | tf_op jit(solution)/shard_map/ppermute | solution.py:27
  405.5 6.1 %collective-permute-done.41.refs_1_ = bf16[6,16,1024]{2,1,0:T(8,128)(2,1)S(1)} collective-permute-done((bf16[6,16,1024]{2,1,0:T(8,128)(2,1)}, bf16[6,16,1024]{2,1,0:T(8,128)(2,1)S(1)}, u32[]{:S(2)}, u32[]{:S(2)}) %collective-permute-start.41) | collective-permute-done | bytes 196640 | tf_op jit(solution)/shard_map/ppermute | solution.py:27
  415.8 7.9 %collective-permute-start.31 = (bf16[6,16,1024]{2,1,0:T(8,128)(2,1)S(1)}, bf16[6,16,1024]{2,1,0:T(8,128)(2,1)S(1)}, u32[]{:S(2)}, u32[]{:S(2)}) collective-permute-start(bf16[6,16,1024]{2,1,0:T(8,128)(2,1)S(1)} %get-tuple-element.99), channel_id=1, source_target_pairs={{0,6},{2,0},{4,2},{6,4},{1,7},{3,1},{5,3},{7,5},{8,14},{10,8},{12,... | collective-permute-start | bytes 589832 | tf_op jit(solution)/shard_map/ppermute | solution.py:27
  432.6 8.4 %collective-permute-start.27 = (bf16[6,16,1024]{2,1,0:T(8,128)(2,1)S(1)}, bf16[6,16,1024]{2,1,0:T(8,128)(2,1)S(1)}, u32[]{:S(2)}, u32[]{:S(2)}) collective-permute-start(bf16[6,16,1024]{2,1,0:T(8,128)(2,1)S(1)} %get-tuple-element.103), channel_id=1, source_target_pairs={{0,6},{2,0},{4,2},{6,4},{1,7},{3,1},{5,3},{7,5},{8,14},{10,8},{12,... | collective-permute-start | bytes 589832 | tf_op jit(solution)/shard_map/ppermute | solution.py:27
  443.7 7.8 %collective-permute-done.30.refs_2_ = bf16[6,16,1024]{2,1,0:T(8,128)(2,1)S(1)} collective-permute-done((bf16[6,16,1024]{2,1,0:T(8,128)(2,1)S(1)}, bf16[6,16,1024]{2,1,0:T(8,128)(2,1)S(1)}, u32[]{:S(2)}, u32[]{:S(2)}) %collective-permute-start.30) | collective-permute-done | bytes 196640 | tf_op jit(solution)/shard_map/ppermute | solution.py:27
  451.5 6.3 %collective-permute-start.23 = (bf16[6,16,1024]{2,1,0:T(8,128)(2,1)S(1)}, bf16[6,16,1024]{2,1,0:T(8,128)(2,1)S(1)}, u32[]{:S(2)}, u32[]{:S(2)}) collective-permute-start(bf16[6,16,1024]{2,1,0:T(8,128)(2,1)S(1)} %get-tuple-element.107), channel_id=1, source_target_pairs={{0,6},{2,0},{4,2},{6,4},{1,7},{3,1},{5,3},{7,5},{8,14},{10,8},{12,... | collective-permute-start | bytes 589832 | tf_op jit(solution)/shard_map/ppermute | solution.py:27
  (278 shorter events, 162.8 us)
Async XLA Ops:
  0.6 28.5 %collective-permute-start.6 = (bf16[64,8192]{1,0:T(8,128)(2,1)}, bf16[64,8192]{1,0:T(8,128)(2,1)S(1)}, u32[]{:S(2)}, u32[]{:S(2)}) collective-permute-start(bf16[64,8192]{1,0:T(8,128)(2,1)} %bitcast.158), channel_id=1, source_target_pairs={{0,16},{8,24},{16,0},{24,8},{1,17},{9,25},{17,1},{25,9},{2,18},{10... | collective-permute-start | bytes 3145736 | tf_op jit(solution)/shard_map/ppermute | solution.py:23
  2.2 27.6 %collective-permute-start = (bf16[64,8192]{1,0:T(8,128)(2,1)}, bf16[64,8192]{1,0:T(8,128)(2,1)}, u32[]{:S(2)}, u32[]{:S(2)}) collective-permute-start(bf16[64,8192]{1,0:T(8,128)(2,1)} %bitcast.159), channel_id=1, source_target_pairs={{0,1},{1,0},{2,3},{3,2},{4,5},{5,4},{6,7},{7,6},{8,9},{9,8},{10,11... | collective-permute-start | bytes 3145736 | tf_op jit(solution)/shard_map/ppermute | solution.py:27
  24.6 39.9 %collective-permute-start.1 = (bf16[64,8192]{1,0:T(8,128)(2,1)}, bf16[64,8192]{1,0:T(8,128)(2,1)S(1)}, u32[]{:S(2)}, u32[]{:S(2)}) collective-permute-start(bf16[64,8192]{1,0:T(8,128)(2,1)} %bitcast.160), channel_id=1, source_target_pairs={{0,8},{8,0},{16,24},{24,16},{1,9},{9,1},{17,25},{25,17},{2,10},{10... | collective-permute-start | bytes 3145736 | tf_op jit(solution)/shard_map/ppermute | solution.py:23
  29.1 107.0 %collective-permute-start.18 = (bf16[4,16,8192]{2,1,0:T(8,128)(2,1)S(1)}, bf16[4,16,8192]{2,1,0:T(8,128)(2,1)}, u32[]{:S(2)}, u32[]{:S(2)}) collective-permute-start(bf16[4,16,8192]{2,1,0:T(8,128)(2,1)S(1)} %bitcast.163), channel_id=1, source_target_pairs={{0,8},{8,0},{16,24},{24,16},{1,9},{9,1},{17,25},{25,17},{2,10},{10... | collective-permute-start | bytes 3145736 | tf_op jit(solution)/shard_map/ppermute | solution.py:23
  30.8 32.4 %collective-permute-start.8 = (bf16[32,8192]{1,0:T(8,128)(2,1)S(1)}, bf16[32,8192]{1,0:T(8,128)(2,1)S(1)}, u32[]{:S(2)}, u32[]{:S(2)}) collective-permute-start(bf16[32,8192]{1,0:T(8,128)(2,1)S(1)} %slice.185), channel_id=1, source_target_pairs={{0,16},{8,24},{16,0},{24,8},{1,17},{9,25},{17,1},{25,9},{2,18},{10... | collective-permute-start | bytes 1572872 | tf_op jit(solution)/shard_map/ppermute | solution.py:23
  43.6 69.2 %collective-permute-start.9 = (bf16[64,8192]{1,0:T(8,128)(2,1)S(1)}, bf16[64,8192]{1,0:T(8,128)(2,1)}, u32[]{:S(2)}, u32[]{:S(2)}) collective-permute-start(bf16[64,8192]{1,0:T(8,128)(2,1)S(1)} %collective-permute-done.6), channel_id=1, source_target_pairs={{0,8},{8,0},{16,24},{24,16},{1,9},{9,1},{17,25},{25,17},{2,10},{10... | collective-permute-start | bytes 3145736 | tf_op jit(solution)/shard_map/ppermute | solution.py:23
  63.2 72.9 %collective-permute-start.20 = (bf16[4,16,8192]{2,1,0:T(8,128)(2,1)}, bf16[4,16,8192]{2,1,0:T(8,128)(2,1)}, u32[]{:S(2)}, u32[]{:S(2)}) collective-permute-start(bf16[4,16,8192]{2,1,0:T(8,128)(2,1)} %collective-permute-done.19), channel_id=1, source_target_pairs={{0,8},{8,0},{16,24},{24,16},{1,9},{9,1},{17,25},{25,17},{2,10},{10... | collective-permute-start | bytes 3145736 | tf_op jit(solution)/shard_map/ppermute | solution.py:23
  64.5 75.4 %collective-permute-start.10 = (bf16[64,8192]{1,0:T(8,128)(2,1)}, bf16[64,8192]{1,0:T(8,128)(2,1)}, u32[]{:S(2)}, u32[]{:S(2)}) collective-permute-start(bf16[64,8192]{1,0:T(8,128)(2,1)} %pad_maximum_fusion.2), channel_id=1, source_target_pairs={{0,8},{8,0},{16,24},{24,16},{1,9},{9,1},{17,25},{25,17},{2,10},{10... | collective-permute-start | bytes 3145736 | tf_op jit(solution)/shard_map/ppermute | solution.py:23
  107.9 76.8 %collective-permute-start.5 = (bf16[2,2,16,2048]{3,2,1,0:T(8,128)(2,1)S(1)}, bf16[2,2,16,2048]{3,2,1,0:T(8,128)(2,1)S(1)}, u32[]{:S(2)}, u32[]{:S(2)}) collective-permute-start(bf16[2,2,16,2048]{3,2,1,0:T(8,128)(2,1)S(1)} %get-tuple-element.76), channel_id=1, source_target_pairs={{0,6},{2,0},{4,2},{6,4},{1,7},{3,1},{5,3},{7,5},{8,14},{10,8},{12,... | collective-permute-start | bytes 786440 | tf_op jit(solution)/shard_map/ppermute | solution.py:27
  232.3 41.9 %collective-permute-start.40 = (bf16[16,16,1024]{2,1,0:T(8,128)(2,1)S(1)}, bf16[16,16,1024]{2,1,0:T(8,128)(2,1)S(1)}, u32[]{:S(2)}, u32[]{:S(2)}) collective-permute-start(bf16[16,16,1024]{2,1,0:T(8,128)(2,1)S(1)} %bitcast.188), channel_id=1, source_target_pairs={{0,1},{1,0},{2,3},{3,2},{4,5},{5,4},{6,7},{7,6},{8,9},{9,8},{10,11... | collective-permute-start | bytes 1572872 | tf_op jit(solution)/shard_map/ppermute | solution.py:27
  249.5 33.8 %collective-permute-start.36 = (bf16[16,16,1024]{2,1,0:T(8,128)(2,1)S(1)}, bf16[16,16,1024]{2,1,0:T(8,128)(2,1)S(1)}, u32[]{:S(2)}, u32[]{:S(2)}) collective-permute-start(bf16[16,16,1024]{2,1,0:T(8,128)(2,1)S(1)} %bitcast.186), channel_id=1, source_target_pairs={{0,1},{1,0},{2,3},{3,2},{4,5},{5,4},{6,7},{7,6},{8,9},{9,8},{10,11... | collective-permute-start | bytes 1572872 | tf_op jit(solution)/shard_map/ppermute | solution.py:27
  251.0 41.6 %collective-permute-start.32 = (bf16[16,16,1024]{2,1,0:T(8,128)(2,1)S(1)}, bf16[16,16,1024]{2,1,0:T(8,128)(2,1)S(1)}, u32[]{:S(2)}, u32[]{:S(2)}) collective-permute-start(bf16[16,16,1024]{2,1,0:T(8,128)(2,1)S(1)} %bitcast.187), channel_id=1, source_target_pairs={{0,1},{1,0},{2,3},{3,2},{4,5},{5,4},{6,7},{7,6},{8,9},{9,8},{10,11... | collective-permute-start | bytes 1572872 | tf_op jit(solution)/shard_map/ppermute | solution.py:27
  251.5 49.7 %collective-permute-start.28 = (bf16[16,16,1024]{2,1,0:T(8,128)(2,1)S(1)}, bf16[16,16,1024]{2,1,0:T(8,128)(2,1)S(1)}, u32[]{:S(2)}, u32[]{:S(2)}) collective-permute-start(bf16[16,16,1024]{2,1,0:T(8,128)(2,1)S(1)} %bitcast.185), channel_id=1, source_target_pairs={{0,1},{1,0},{2,3},{3,2},{4,5},{5,4},{6,7},{7,6},{8,9},{9,8},{10,11... | collective-permute-start | bytes 1572872 | tf_op jit(solution)/shard_map/ppermute | solution.py:27
  256.3 56.2 %collective-permute-start.24 = (bf16[16,16,1024]{2,1,0:T(8,128)(2,1)}, bf16[16,16,1024]{2,1,0:T(8,128)(2,1)S(1)}, u32[]{:S(2)}, u32[]{:S(2)}) collective-permute-start(bf16[16,16,1024]{2,1,0:T(8,128)(2,1)} %bitcast.183), channel_id=1, source_target_pairs={{0,1},{1,0},{2,3},{3,2},{4,5},{5,4},{6,7},{7,6},{8,9},{9,8},{10,11... | collective-permute-start | bytes 1572872 | tf_op jit(solution)/shard_map/ppermute | solution.py:27
  274.2 49.6 %collective-permute-start.14 = (bf16[16,16,1024]{2,1,0:T(8,128)(2,1)S(1)}, bf16[16,16,1024]{2,1,0:T(8,128)(2,1)S(1)}, u32[]{:S(2)}, u32[]{:S(2)}) collective-permute-start(bf16[16,16,1024]{2,1,0:T(8,128)(2,1)S(1)} %bitcast.184), channel_id=1, source_target_pairs={{0,1},{1,0},{2,3},{3,2},{4,5},{5,4},{6,7},{7,6},{8,9},{9,8},{10,11... | collective-permute-start | bytes 1572872 | tf_op jit(solution)/shard_map/ppermute | solution.py:27
  283.3 89.6 %collective-permute-start.51 = (bf16[6,16,1024]{2,1,0:T(8,128)(2,1)}, bf16[6,16,1024]{2,1,0:T(8,128)(2,1)S(1)}, u32[]{:S(2)}, u32[]{:S(2)}) collective-permute-start(bf16[6,16,1024]{2,1,0:T(8,128)(2,1)} %get-tuple-element.79), channel_id=1, source_target_pairs={{0,6},{2,0},{4,2},{6,4},{1,7},{3,1},{5,3},{7,5},{8,14},{10,8},{12,... | collective-permute-start | bytes 589832 | tf_op jit(solution)/shard_map/ppermute | solution.py:27
  292.6 81.7 %collective-permute-start.50 = (bf16[6,16,1024]{2,1,0:T(8,128)(2,1)}, bf16[6,16,1024]{2,1,0:T(8,128)(2,1)}, u32[]{:S(2)}, u32[]{:S(2)}) collective-permute-start(bf16[6,16,1024]{2,1,0:T(8,128)(2,1)} %get-tuple-element.80), channel_id=1, source_target_pairs={{0,4},{2,6},{4,0},{6,2},{1,5},{3,7},{5,1},{7,3},{8,12},{10,14},{12... | collective-permute-start | bytes 589832 | tf_op jit(solution)/shard_map/ppermute | solution.py:27
  301.3 73.7 %collective-permute-start.49 = (bf16[6,16,1024]{2,1,0:T(8,128)(2,1)}, bf16[6,16,1024]{2,1,0:T(8,128)(2,1)}, u32[]{:S(2)}, u32[]{:S(2)}) collective-permute-start(bf16[6,16,1024]{2,1,0:T(8,128)(2,1)} %get-tuple-element.81), channel_id=1, source_target_pairs={{0,2},{2,4},{4,6},{6,0},{1,3},{3,5},{5,7},{7,1},{8,10},{10,12},{12... | collective-permute-start | bytes 589832 | tf_op jit(solution)/shard_map/ppermute | solution.py:27
  312.5 64.2 %collective-permute-start.47 = (bf16[6,16,1024]{2,1,0:T(8,128)(2,1)}, bf16[6,16,1024]{2,1,0:T(8,128)(2,1)}, u32[]{:S(2)}, u32[]{:S(2)}) collective-permute-start(bf16[6,16,1024]{2,1,0:T(8,128)(2,1)} %get-tuple-element.83), channel_id=1, source_target_pairs={{0,6},{2,0},{4,2},{6,4},{1,7},{3,1},{5,3},{7,5},{8,14},{10,8},{12,... | collective-permute-start | bytes 589832 | tf_op jit(solution)/shard_map/ppermute | solution.py:27
  323.8 56.2 %collective-permute-start.46 = (bf16[6,16,1024]{2,1,0:T(8,128)(2,1)}, bf16[6,16,1024]{2,1,0:T(8,128)(2,1)}, u32[]{:S(2)}, u32[]{:S(2)}) collective-permute-start(bf16[6,16,1024]{2,1,0:T(8,128)(2,1)} %get-tuple-element.84), channel_id=1, source_target_pairs={{0,4},{2,6},{4,0},{6,2},{1,5},{3,7},{5,1},{7,3},{8,12},{10,14},{12... | collective-permute-start | bytes 589832 | tf_op jit(solution)/shard_map/ppermute | solution.py:27
  376.7 34.9 %collective-permute-start.41 = (bf16[6,16,1024]{2,1,0:T(8,128)(2,1)}, bf16[6,16,1024]{2,1,0:T(8,128)(2,1)S(1)}, u32[]{:S(2)}, u32[]{:S(2)}) collective-permute-start(bf16[6,16,1024]{2,1,0:T(8,128)(2,1)} %get-tuple-element.89), channel_id=1, source_target_pairs={{0,2},{2,4},{4,6},{6,0},{1,3},{3,5},{5,7},{7,1},{8,10},{10,12},{12... | collective-permute-start | bytes 589832 | tf_op jit(solution)/shard_map/ppermute | solution.py:27
  380.0 34.2 %collective-permute-start.39 = (bf16[6,16,1024]{2,1,0:T(8,128)(2,1)}, bf16[6,16,1024]{2,1,0:T(8,128)(2,1)S(1)}, u32[]{:S(2)}, u32[]{:S(2)}) collective-permute-start(bf16[6,16,1024]{2,1,0:T(8,128)(2,1)} %get-tuple-element.91), channel_id=1, source_target_pairs={{0,6},{2,0},{4,2},{6,4},{1,7},{3,1},{5,3},{7,5},{8,14},{10,8},{12,... | collective-permute-start | bytes 589832 | tf_op jit(solution)/shard_map/ppermute | solution.py:27
  388.1 27.7 %collective-permute-start.38 = (bf16[6,16,1024]{2,1,0:T(8,128)(2,1)}, bf16[6,16,1024]{2,1,0:T(8,128)(2,1)S(1)}, u32[]{:S(2)}, u32[]{:S(2)}) collective-permute-start(bf16[6,16,1024]{2,1,0:T(8,128)(2,1)} %get-tuple-element.92), channel_id=1, source_target_pairs={{0,4},{2,6},{4,0},{6,2},{1,5},{3,7},{5,1},{7,3},{8,12},{10,14},{12... | collective-permute-start | bytes 589832 | tf_op jit(solution)/shard_map/ppermute | solution.py:27
  391.3 37.2 %collective-permute-start.37 = (bf16[6,16,1024]{2,1,0:T(8,128)(2,1)}, bf16[6,16,1024]{2,1,0:T(8,128)(2,1)S(1)}, u32[]{:S(2)}, u32[]{:S(2)}) collective-permute-start(bf16[6,16,1024]{2,1,0:T(8,128)(2,1)} %get-tuple-element.93), channel_id=1, source_target_pairs={{0,2},{2,4},{4,6},{6,0},{1,3},{3,5},{5,7},{7,1},{8,10},{10,12},{12... | collective-permute-start | bytes 589832 | tf_op jit(solution)/shard_map/ppermute | solution.py:27
  400.7 30.4 %collective-permute-start.35 = (bf16[6,16,1024]{2,1,0:T(8,128)(2,1)S(1)}, bf16[6,16,1024]{2,1,0:T(8,128)(2,1)S(1)}, u32[]{:S(2)}, u32[]{:S(2)}) collective-permute-start(bf16[6,16,1024]{2,1,0:T(8,128)(2,1)S(1)} %get-tuple-element.95), channel_id=1, source_target_pairs={{0,6},{2,0},{4,2},{6,4},{1,7},{3,1},{5,3},{7,5},{8,14},{10,8},{12,... | collective-permute-start | bytes 589832 | tf_op jit(solution)/shard_map/ppermute | solution.py:27
  414.2 27.5 %collective-permute-start.33 = (bf16[6,16,1024]{2,1,0:T(8,128)(2,1)S(1)}, bf16[6,16,1024]{2,1,0:T(8,128)(2,1)S(1)}, u32[]{:S(2)}, u32[]{:S(2)}) collective-permute-start(bf16[6,16,1024]{2,1,0:T(8,128)(2,1)S(1)} %get-tuple-element.97), channel_id=1, source_target_pairs={{0,2},{2,4},{4,6},{6,0},{1,3},{3,5},{5,7},{7,1},{8,10},{10,12},{12... | collective-permute-start | bytes 589832 | tf_op jit(solution)/shard_map/ppermute | solution.py:27
  415.8 27.9 %collective-permute-start.31 = (bf16[6,16,1024]{2,1,0:T(8,128)(2,1)S(1)}, bf16[6,16,1024]{2,1,0:T(8,128)(2,1)S(1)}, u32[]{:S(2)}, u32[]{:S(2)}) collective-permute-start(bf16[6,16,1024]{2,1,0:T(8,128)(2,1)S(1)} %get-tuple-element.99), channel_id=1, source_target_pairs={{0,6},{2,0},{4,2},{6,4},{1,7},{3,1},{5,3},{7,5},{8,14},{10,8},{12,... | collective-permute-start | bytes 589832 | tf_op jit(solution)/shard_map/ppermute | solution.py:27
  431.1 26.7 %collective-permute-start.29 = (bf16[6,16,1024]{2,1,0:T(8,128)(2,1)S(1)}, bf16[6,16,1024]{2,1,0:T(8,128)(2,1)S(1)}, u32[]{:S(2)}, u32[]{:S(2)}) collective-permute-start(bf16[6,16,1024]{2,1,0:T(8,128)(2,1)S(1)} %get-tuple-element.101), channel_id=1, source_target_pairs={{0,2},{2,4},{4,6},{6,0},{1,3},{3,5},{5,7},{7,1},{8,10},{10,12},{12... | collective-permute-start | bytes 589832 | tf_op jit(solution)/shard_map/ppermute | solution.py:27
  432.6 28.3 %collective-permute-start.27 = (bf16[6,16,1024]{2,1,0:T(8,128)(2,1)S(1)}, bf16[6,16,1024]{2,1,0:T(8,128)(2,1)S(1)}, u32[]{:S(2)}, u32[]{:S(2)}) collective-permute-start(bf16[6,16,1024]{2,1,0:T(8,128)(2,1)S(1)} %get-tuple-element.103), channel_id=1, source_target_pairs={{0,6},{2,0},{4,2},{6,4},{1,7},{3,1},{5,3},{7,5},{8,14},{10,8},{12,... | collective-permute-start | bytes 589832 | tf_op jit(solution)/shard_map/ppermute | solution.py:27
  441.7 36.9 %collective-permute-start.26 = (bf16[6,16,1024]{2,1,0:T(8,128)(2,1)S(1)}, bf16[6,16,1024]{2,1,0:T(8,128)(2,1)S(1)}, u32[]{:S(2)}, u32[]{:S(2)}) collective-permute-start(bf16[6,16,1024]{2,1,0:T(8,128)(2,1)S(1)} %get-tuple-element.104), channel_id=1, source_target_pairs={{0,4},{2,6},{4,0},{6,2},{1,5},{3,7},{5,1},{7,3},{8,12},{10,14},{12... | collective-permute-start | bytes 589832 | tf_op jit(solution)/shard_map/ppermute | solution.py:27
  443.7 34.9 %collective-permute-start.25 = (bf16[6,16,1024]{2,1,0:T(8,128)(2,1)S(1)}, bf16[6,16,1024]{2,1,0:T(8,128)(2,1)S(1)}, u32[]{:S(2)}, u32[]{:S(2)}) collective-permute-start(bf16[6,16,1024]{2,1,0:T(8,128)(2,1)S(1)} %get-tuple-element.105), channel_id=1, source_target_pairs={{0,2},{2,4},{4,6},{6,0},{1,3},{3,5},{5,7},{7,1},{8,10},{10,12},{12... | collective-permute-start | bytes 589832 | tf_op jit(solution)/shard_map/ppermute | solution.py:27
  451.5 30.6 %collective-permute-start.23 = (bf16[6,16,1024]{2,1,0:T(8,128)(2,1)S(1)}, bf16[6,16,1024]{2,1,0:T(8,128)(2,1)S(1)}, u32[]{:S(2)}, u32[]{:S(2)}) collective-permute-start(bf16[6,16,1024]{2,1,0:T(8,128)(2,1)S(1)} %get-tuple-element.107), channel_id=1, source_target_pairs={{0,6},{2,0},{4,2},{6,4},{1,7},{3,1},{5,3},{7,5},{8,14},{10,8},{12,... | collective-permute-start | bytes 589832 | tf_op jit(solution)/shard_map/ppermute | solution.py:27
  (76 other events, 1741.7 us)

commit v2 on v1

v2 whole, which is shorter than its diff:
```python
import functools
import math

import jax
import jax.numpy as jnp
from jax import lax
from jax.experimental import pallas as pl
from jax.experimental.pallas import tpu as pltpu
from jax.sharding import PartitionSpec as P

HD = 128
NORM_EPS = 1e-05
ROPE_THETA = 500000.0
VMEM_BYTES = 56 * 1024 * 1024
CHUNKS = (1, 1, 2, 2, 2)
AHEAD = 2


def params():
    return pltpu.CompilerParams(vmem_limit_bytes=VMEM_BYTES)


def swap(value, axis, size, step):
    return lax.ppermute(value, axis, [(j, j ^ step) for j in range(size)])


def shift(value, axis, size, step):
    return lax.ppermute(value, axis, [(j, (j + step) % size) for j in range(size)])


def attention_kernel(n_dp, n_tp, n_pieces, *refs):
    x_refs, refs = refs[:n_pieces], refs[n_pieces:]
    (gain_ref, cos_ref, sin_ref, mask_ref, wq_ref, wkv_ref, out_ref, normed, acc_q, acc_k, acc_v) = refs
    group, step = pl.program_id(0), pl.program_id(1)
    steps, rows, depth = normed.shape
    seq = mask_ref.shape[0]
    width = steps * depth

    @pl.when((group == 0) & (step == 0))
    def _():
        start = 0
        for x_ref in x_refs:
            size = min(16, x_ref.shape[0])

            def norm_rows(i, carry, x_ref=x_ref, start=start, size=size):
                x = x_ref[pl.ds(pl.multiple_of(i * size, size), size), :].astype(jnp.float32)
                inv = lax.rsqrt(jnp.sum(x * x, axis=-1, keepdims=True) * (1.0 / width) + NORM_EPS)
                y = (x * inv * gain_ref[...]).astype(jnp.bfloat16)
                to = pl.ds(pl.multiple_of(start + i * size, size), size)
                for j in range(steps):
                    normed[j, to, :] = y[:, j * depth : (j + 1) * depth]
                return carry

            lax.fori_loop(0, x_ref.shape[0] // size, norm_rows, 0)
            start += x_ref.shape[0]

    lhs = normed[step]
    part_q = jnp.dot(lhs, wq_ref[...], preferred_element_type=jnp.float32)
    part_k = jnp.dot(lhs, wkv_ref[0], preferred_element_type=jnp.float32)
    part_v = jnp.dot(lhs, wkv_ref[1], preferred_element_type=jnp.float32)

    @pl.when(step == 0)
    def _():
        acc_q[...] = part_q
        acc_k[...] = part_k
        acc_v[...] = part_v

    @pl.when(step > 0)
    def _():
        acc_q[...] += part_q
        acc_k[...] += part_k
        acc_v[...] += part_v

    @pl.when(step == steps - 1)
    def _():
        cos, sin = cos_ref[...], sin_ref[...]
        causal = jnp.concatenate([mask_ref[...]] * (acc_q.shape[1] // acc_k.shape[1]), axis=0) > 0.0
        block = seq // (n_dp * n_tp)
        kv_here = acc_k.shape[1] // HD
        per_kv = acc_q.shape[1] // acc_k.shape[1]

        def rope(v):
            return (v * cos + pltpu.roll(v, HD // 2, 1) * sin).astype(jnp.bfloat16)

        for s in range(rows // seq):
            at = slice(s * seq, (s + 1) * seq)
            for j in range(kv_here):
                cols = slice(j * HD, (j + 1) * HD)
                keys = rope(acc_k[at, cols])
                values = acc_v[at, cols].astype(jnp.bfloat16)
                heads = range(j * per_kv, (j + 1) * per_kv)
                queries = jnp.concatenate([rope(acc_q[at, h * HD : (h + 1) * HD]) for h in heads], axis=0)
                scores = lax.dot_general(
                    queries, keys, (((1,), (1,)), ((), ())), preferred_element_type=jnp.float32
                ) * (1.0 / math.sqrt(HD))
                scores = jnp.where(causal, scores, -1e30)
                expo = jnp.exp(scores - jnp.max(scores, axis=-1, keepdims=True))
                weights = (expo / jnp.sum(expo, axis=-1, keepdims=True)).astype(jnp.bfloat16)
                context = jnp.dot(weights, values, preferred_element_type=jnp.float32).astype(jnp.bfloat16)
                for n, h in enumerate(heads):
                    for t in range(n_tp):
                        for z in range(n_dp):
                            start = n * seq + (t * n_dp + z) * block
                            out_ref[z, t, s, :, h * HD : (h + 1) * HD] = context[start : start + block]


def attention(pieces, gain, cos, sin, mask, wq, wkv, n_dp, n_tp):
    rows, width = sum(p.shape[0] for p in pieces), pieces[0].shape[1]
    seq = mask.shape[0]
    q_width, kv_width = wq.shape[2], wkv.shape[3]
    kv_block = min(2 * HD, kv_width)
    groups = kv_width // kv_block
    q_block = q_width // groups
    steps = 2
    depth = width // steps
    samples = rows // seq
    block = seq // (n_dp * n_tp)
    fixed = lambda g, k: (0, 0)
    return pl.pallas_call(
        functools.partial(attention_kernel, n_dp, n_tp, len(pieces)),
        out_shape=jax.ShapeDtypeStruct((n_dp, n_tp, samples, block, q_width), jnp.bfloat16),
        grid=(groups, steps),
        in_specs=[pl.BlockSpec(p.shape, fixed) for p in pieces]
        + [
            pl.BlockSpec((1, width), fixed),
            pl.BlockSpec((seq, HD), fixed),
            pl.BlockSpec((seq, HD), fixed),
            pl.BlockSpec((seq, seq), fixed),
            pl.BlockSpec((None, depth, q_block), lambda g, k: (0, k, g)),
            pl.BlockSpec((None, 2, depth, kv_block), lambda g, k: (0, 0, k, g)),
        ],
        out_specs=pl.BlockSpec((n_dp, n_tp, samples, block, q_block), lambda g, k: (0, 0, 0, 0, g)),
        scratch_shapes=[
            pltpu.VMEM((steps, rows, depth), jnp.bfloat16),
            pltpu.VMEM((rows, q_block), jnp.float32),
            pltpu.VMEM((rows, kv_block), jnp.float32),
            pltpu.VMEM((rows, kv_block), jnp.float32),
        ],
        compiler_params=params(),
        cost_estimate=pl.CostEstimate(flops=1, bytes_accessed=1, transcendentals=0),
        name="project_and_attend",
    )(*pieces, gain, cos, sin, mask, wq, wkv)


def out_kernel(ctx_ref, wo_ref, own_ref, send_ref):
    full = jnp.dot(ctx_ref[...], wo_ref[...], preferred_element_type=jnp.float32).astype(jnp.bfloat16)
    mine = own_ref.shape[0]
    own_ref[...] = full[:mine]
    send_ref[...] = full[mine:]


def out_projection(ctx, wo, mine, first, cols):
    rows, depth = ctx.shape
    col_block = min(512, cols)
    inner = cols // col_block
    base = first // col_block
    return pl.pallas_call(
        out_kernel,
        out_shape=[
            jax.ShapeDtypeStruct((mine, cols), jnp.bfloat16),
            jax.ShapeDtypeStruct((rows - mine, cols), jnp.bfloat16),
        ],
        grid=(inner,),
        in_specs=[
            pl.BlockSpec((rows, depth), lambda n: (0, 0)),
            pl.BlockSpec((None, depth, col_block), lambda n: (0, 0, base + n)),
        ],
        out_specs=[
            pl.BlockSpec((mine, col_block), lambda n: (0, n)),
            pl.BlockSpec((rows - mine, col_block), lambda n: (0, n)),
        ],
        compiler_params=params(),
        cost_estimate=pl.CostEstimate(flops=1, bytes_accessed=1, transcendentals=0),
        name="out_projection",
    )(ctx, wo)


def join_kernel(n_slots, block, table_ref, own_ref, other_ref, resid_ref, head_ref, packed_ref, stats_ref):
    dest = pl.program_id(0)
    head = head_ref[...]
    lane = lax.broadcasted_iota(jnp.int32, (block, HD), 1)
    row = lax.broadcasted_iota(jnp.int32, (block, 1), 0)

    for slot in range(n_slots):
        entry = dest * n_slots + slot
        part, resid, live = table_ref[0, entry], table_ref[1, entry], table_ref[2, entry]
        added = own_ref[part].astype(jnp.float32)
        for k in range(other_ref.shape[0]):
            added = added + other_ref[k, part].astype(jnp.float32)
        hidden = resid_ref[resid].astype(jnp.float32) + added
        packed_ref[slot] = jnp.where(row < live, hidden, 0.0).astype(jnp.bfloat16)
        squares = jnp.sum(hidden * hidden, axis=-1, keepdims=True)
        scored = jnp.sum(hidden * head, axis=-1, keepdims=True)
        stats_ref[slot] = jnp.where(lane == 0, squares, jnp.where(lane == 1, scored, 0.0))


def join(table, own, other, resid, head, chunk, n_dp, n_slots, block):
    blocks, _, cols = own.shape
    return pl.pallas_call(
        functools.partial(join_kernel, n_slots, block),
        out_shape=[
            jax.ShapeDtypeStruct((n_dp, n_slots, block, cols), jnp.bfloat16),
            jax.ShapeDtypeStruct((n_dp, n_slots, block, HD), jnp.float32),
        ],
        grid_spec=pltpu.PrefetchScalarGridSpec(
            num_scalar_prefetch=1,
            grid=(n_dp,),
            in_specs=[
                pl.BlockSpec(own.shape, lambda d, t: (0, 0, 0)),
                pl.BlockSpec(other.shape, lambda d, t: (0, 0, 0, 0)),
                pl.BlockSpec((blocks, block, cols), lambda d, t: (0, 0, chunk)),
                pl.BlockSpec((1, cols), lambda d, t: (0, chunk)),
            ],
            out_specs=[
                pl.BlockSpec((None, n_slots, block, cols), lambda d, t: (d, 0, 0, 0)),
                pl.BlockSpec((None, n_slots, block, HD), lambda d, t: (d, 0, 0, 0)),
            ],
        ),
        compiler_params=params(),
        cost_estimate=pl.CostEstimate(flops=1, bytes_accessed=1, transcendentals=0),
        name="join_partials",
    )(table, own, other, resid, head)


def place_kernel(sizes, count, order_ref, *refs):
    out_ref = refs[-1]
    step = pl.program_id(1)
    first = 0
    for chunk, size in enumerate(sizes):
        @pl.when((step >= first) & (step < first + size))
        def _(chunk=chunk):
            for k in range(count):
                out_ref[:, order_ref[k]] = refs[chunk * count + k][...]

        first += size


def place(order, arrived, sizes, width):
    n_slots, block, _ = arrived[0][0].shape
    count = len(arrived[0])
    unit = width // sum(sizes)
    rows = n_slots // 2
    firsts = [sum(sizes[:c]) for c in range(len(sizes))]

    def spec(first, size):
        return pl.BlockSpec((rows, block, unit), lambda h, c, o: (h, 0, jnp.clip(c - first, 0, size - 1)))

    return pl.pallas_call(
        functools.partial(place_kernel, sizes, count),
        out_shape=jax.ShapeDtypeStruct((n_slots, count, block, width), jnp.bfloat16),
        grid_spec=pltpu.PrefetchScalarGridSpec(
            num_scalar_prefetch=1,
            grid=(n_slots // rows, sum(sizes)),
            in_specs=[spec(f, s) for f, s in zip(firsts, sizes) for _ in range(count)],
            out_specs=pl.BlockSpec((rows, count, block, unit), lambda h, c, o: (h, 0, 0, c)),
        ),
        compiler_params=params(),
        cost_estimate=pl.CostEstimate(flops=1, bytes_accessed=1, transcendentals=0),
        name="place_rows",
    )(order, *[piece for pieces in arrived for piece in pieces])


def on_device(responses, lengths, dest_dp, dest_slot, wq, wkv, wo, norm_gain, head_vec):
    n_sec = lax.axis_size("sec")
    n_dp = lax.axis_size("dp")
    n_tp = lax.axis_size("tp")
    _, local_len, width = responses.shape
    samples = lengths.shape[0]
    n_slots = 3 * samples // (2 * n_dp)
    seq = local_len * n_tp
    block = local_len // n_dp
    my_sec, my_dp, my_tp = lax.axis_index("sec"), lax.axis_index("dp"), lax.axis_index("tp")

    mine = responses[0]
    near = [mine] + [shift(mine, "tp", n_tp, k) for k in range(1, n_tp)]
    far_mine = swap(mine, "sec", n_sec, 2)
    half = local_len // 2
    far = [far_mine]
    for k in range(1, n_tp):
        parts = [shift(far_mine[:half], "tp", n_tp, k), swap(near[k][half:], "sec", n_sec, 2)]
        far += parts if half % 16 == 0 else [jnp.concatenate(parts, axis=0)]
    near = near + [swap(v, "sec", n_sec, 1) for v in near]
    far = far + [swap(v, "sec", n_sec, 1) for v in far]

    def quarters(v):
        part = lambda k: lax.dynamic_slice_in_dim(v, lax.rem(my_dp + k, n_dp) * block, block, 0)
        return jnp.stack([part(0)] + [shift(part(k), "dp", n_dp, k) for k in range(1, n_dp)])

    resid_0, resid_2 = quarters(mine), quarters(far_mine)

    owners = lax.rem(my_tp - jnp.arange(n_tp) + n_tp, n_tp)
    positions = (owners[:, None] * local_len + jnp.arange(local_len)[None, :]).reshape(seq)
    frequency = jnp.exp(jnp.arange(HD // 2, dtype=jnp.float32) * (-2.0 * math.log(ROPE_THETA) / HD))
    angles = positions.astype(jnp.float32)[:, None] * frequency[None, :]
    cos = jnp.tile(jnp.cos(angles), (1, 2))
    sin = jnp.concatenate([-jnp.sin(angles), jnp.sin(angles)], axis=1)
    mask = (positions[:, None] >= positions[None, :]).astype(jnp.float32)

    def spread(pieces):
        ctx = attention(pieces, norm_gain, cos, sin, mask, wq, wkv, n_dp, n_tp)
        here = lambda k: lax.dynamic_index_in_dim(ctx, lax.rem(my_dp + k, n_dp), 0, keepdims=False)
        parts = [here(0)] + [shift(here(k), "dp", n_dp, k) for k in range(1, n_dp)]
        return ctx, parts

    first_ctx, first_parts = spread(near)
    resid = jnp.concatenate(
        [resid_0, swap(resid_0, "sec", n_sec, 1), resid_2, swap(resid_2, "sec", n_sec, 1)], axis=0
    )
    far, first_ctx, resid = lax.optimization_barrier((far, first_ctx, resid))
    _, second_parts = spread(far)
    q_width = wq.shape[2]
    ctx_rows = jnp.stack(first_parts + second_parts, axis=1).reshape(-1, q_width)
    owned = ctx_rows.shape[0] // n_tp

    row_dp = lax.dynamic_index_in_dim(dest_dp, my_sec, 0, keepdims=False)
    row_slot = lax.dynamic_index_in_dim(dest_slot, my_sec, 0, keepdims=False)
    sample = jnp.arange(samples)
    i_rel = my_sec ^ (sample // n_dp)
    k_rel = lax.rem(my_dp - sample % n_dp + n_dp, n_dp)
    part_at = ((i_rel // 2) * n_dp + k_rel) * 2 + i_rel % 2
    resid_at = i_rel * n_dp + k_rel
    dests = lax.rem(my_dp + jnp.arange(n_dp), n_dp)
    chosen = (row_dp[None, None, :] == dests[:, None, None]) & (
        row_slot[None, None, :] == jnp.arange(n_slots)[None, :, None]
    )
    first_pos = my_tp * local_len + my_dp * block
    live = jnp.clip(lengths - first_pos, 0, block)
    pick = lambda v: jnp.sum(jnp.where(chosen, v[None, None, :], 0), axis=-1).reshape(-1)
    table = jnp.stack([pick(part_at), pick(resid_at), pick(live)]).astype(jnp.int32)
    order = lax.rem(my_dp - jnp.arange(n_dp) + n_dp, n_dp).astype(jnp.int32)

    unit = width // sum(CHUNKS)
    starts = [unit * sum(CHUNKS[:c]) for c in range(len(CHUNKS))]
    stats, arrived, owns, sends = [], [], [], []

    def project(ctx_from):
        own, send = out_projection(ctx_from, wo, owned, starts[len(owns)], unit * CHUNKS[len(owns)])
        owns.append(own.reshape(-1, block, own.shape[-1]))
        sends.append(send.reshape(n_tp - 1, -1, block, own.shape[-1]))

    for _ in range(AHEAD):
        project(ctx_rows)
        ctx_rows, owns[-1] = lax.optimization_barrier((ctx_rows, owns[-1]))
    for chunk, size in enumerate(CHUNKS):
        other = [shift(sends[chunk][k - 1], "tp", n_tp, n_tp - k) for k in range(1, n_tp)]
        own = owns[chunk]
        last = min(chunk + AHEAD, len(CHUNKS)) - 1
        if last > chunk:
            own, sends[last] = lax.optimization_barrier((own, sends[last]))
        if chunk >= 2:
            own, arrived[chunk - 2] = lax.optimization_barrier((own, arrived[chunk - 2]))
        packed, part_stats = join(
            table, own, jnp.stack(other), resid, head_vec, starts[chunk] // (unit * size), n_dp, n_slots, block
        )
        if chunk + AHEAD < len(CHUNKS):
            packed, ctx_rows = lax.optimization_barrier((packed, ctx_rows))
            project(ctx_rows)
        stats.append(part_stats)
        arrived.append([packed[0]] + [shift(packed[k], "dp", n_dp, k) for k in range(1, n_dp)])
    arrived[-2], stats[-1] = lax.optimization_barrier((arrived[-2], stats[-1]))
    whole = place(order, arrived, CHUNKS, width)
    layer_out = jnp.transpose(whole.reshape(n_slots, local_len, width), (1, 0, 2))[None, None]

    stats = sum(v[..., :2] for v in stats)
    token_scores = stats[..., 1] * lax.rsqrt(stats[..., 0] * (1.0 / width) + NORM_EPS)
    is_live = jnp.arange(block)[None, None, :] < table[2].reshape(n_dp, n_slots, 1)
    slot_sums = jnp.sum(jnp.where(is_live, token_scores, 0.0), axis=-1)
    by_sample = jnp.sum(jnp.where(chosen, slot_sums[:, :, None], 0.0), axis=(0, 1))
    by_model = jnp.where(jnp.arange(n_sec)[:, None] == my_sec, by_sample[None, :], 0.0)
    for axis, size in (("tp", n_tp), ("dp", n_dp), ("sec", n_sec)):
        by_model = sum([shift(by_model, axis, size, k) for k in range(1, size)], by_model)
    totals = by_model
    averages = totals / lengths[None, :].astype(jnp.float32)
    owner = (dest_dp[n_sec - 1] == my_dp)[None, :] & (
        dest_slot[n_sec - 1][None, :] == jnp.arange(n_slots)[:, None]
    )
    sample_scores = jnp.sum(jnp.where(owner[:, None, :], averages[None, :, :], 0.0), axis=-1)
    return layer_out, sample_scores[None]


def solution(mesh):
    placed = (
        P(("sec", "dp"), "tp", None),
        P(),
        P(),
        P(),
        P("sec", None, "tp"),
        P("sec", None, None, "tp"),
        P("sec", "tp", None),
        P("sec", None),
        P("sec", None),
    )
    return jax.shard_map(
        on_device,
        mesh=mesh,
        in_specs=placed,
        out_specs=(P("sec", "dp", "tp", None, None), P("dp", None, None)),
        check_vma=False,
    )
```

time: 495 us -> 374 us (0.76); the launches traced: 486 us -> 373 us
  Pallas kernels: 187 us -> 130 us
  blocking collectives: 38.6 us -> 0 us
  starting transfers between devices: 77.7 us -> 53.1 us
  other arithmetic: 17.4 us -> 6.29 us
  waiting for transfers between devices: 138 us -> 149 us
  local copies, waits for them, and re-layouts: 25.5 us -> 32.8 us
    psum x1 -> x0, blocking collectives: 38.6 us -> none  [on_device(): totals = lax.psum(by_model, ('sec', 'dp', 'tp'))]
    ppermute x43 -> x41, waiting for transfers between devices: 118 us -> 149 us  [shift(): lax.ppermute(value, axis, [(j, (j + step) % size) for j in range(size)])]
    pallas_call x10 -> x3, Pallas kernels: 99.4 us -> 70.1 us  [the longest x2 56.6 us: attention(): pl.pallas_call(functools.partial(attention_kernel, n_dp, n_tp, len(pieces...]
    ppermute x43 -> x41, starting transfers between devices: 73.5 us -> 49.8 us  [shift(): lax.ppermute(value, axis, [(j, (j + step) % size) for j in range(size)])]
    pallas_call x8 -> x5, Pallas kernels: 43.4 us -> 22.9 us  [join(): pl.pallas_call(functools.partial(join_kernel, n_slots, block), out_shape=...]
    ppermute x9, waiting for transfers between devices: 19.6 us -> 0.02 us  [swap(): return lax.ppermute(value, axis, [(j, j ^ step) for j in range(size)])]
    unnamed x123 -> x83, local copies, waits for them, and re-layouts: 8.52 us -> 16.9 us
    concatenate x4 -> x0, other arithmetic: 8.14 us -> none  [the longest x1 3.66 us: on_device(): jnp.concatenate([resid_0, swap(resid_0, 'sec', n_sec, 1), resid_2, swap(r...]
  transfers between devices with their start and end apart: 52 -> 50, of which waited for: 24 -> 23; matrix products, arithmetic and copies ran while one was open for 8% -> 8% of each run, Pallas kernels for 33% -> 30%
where the time goes in v2:
time: 374 us; the launch traced here: 373 us
  waiting for transfers between devices  149 us (40%)
  Pallas kernels  130 us (35%)
  starting transfers between devices  53.1 us (14%)
  local copies, waits for them, and re-layouts  32.8 us (9%)
  other arithmetic  6.29 us (2%)
    ppermute x41, waiting for transfers between devices, shift(): lax.ppermute(value, axis, [(j, (j + step) % size) for j in range(size)])  149 us
    pallas_call x2, Pallas kernels, attention(): pl.pallas_call(functools.partial(attention_kernel, n_dp, n_tp, len(pieces...  56.6 us
    ppermute x41, starting transfers between devices, shift(): lax.ppermute(value, axis, [(j, (j + step) % size) for j in range(size)])  49.8 us
    pallas_call x5, Pallas kernels, out_projection(): pl.pallas_call(out_kernel, out_shape=[jax.ShapeDtypeStruct((mine, cols),...  37.2 us
    pallas_call x5, Pallas kernels, join(): pl.pallas_call(functools.partial(join_kernel, n_slots, block), out_shape=...  22.9 us
    unnamed x83, local copies, waits for them, and re-layouts  16.9 us
    pallas_call x1, Pallas kernels, place(): pl.pallas_call(functools.partial(place_kernel, sizes, count), out_shape=j...  13.5 us
  transfers between devices with their start and end apart: 50, of which 23 were waited for; matrix products, arithmetic and copies ran while one was open for 8% of the time, Pallas kernels for 30%

profile of v2, /device:TPU:8, one launch (start us, length us, event | category | flops | bytes accessed | tf_op | source)
XLA Modules:
  0.0 372.7 jit_solution(2516193999272157792)
XLA Ops:
  14.0 11.7 %collective-permute-done.12 = bf16[16,8192]{1,0:T(8,128)(2,1)S(1)} collective-permute-done((bf16[16,8192]{1,0:T(8,128)(2,1)}, bf16[16,8192]{1,0:T(8,128)(2,1)S(1)}, u32[]{:S(2)}, u32[]{:S(2)}) %collective-permute-start.12) | collective-permute-done | bytes 262176 | tf_op jit(solution)/shard_map/ppermute | solution.py:28
  25.7 3.9 %collective-permute-done.13 = bf16[16,8192]{1,0:T(8,128)(2,1)S(1)} collective-permute-done((bf16[16,8192]{1,0:T(8,128)(2,1)}, bf16[16,8192]{1,0:T(8,128)(2,1)S(1)}, u32[]{:S(2)}, u32[]{:S(2)}) %collective-permute-start.13) | collective-permute-done | bytes 262176 | tf_op jit(solution)/shard_map/ppermute | solution.py:28
  43.4 13.7 %collective-permute-done.17 = bf16[16,8192]{1,0:T(8,128)(2,1)S(1)} collective-permute-done((bf16[16,8192]{1,0:T(8,128)(2,1)S(1)}, bf16[16,8192]{1,0:T(8,128)(2,1)S(1)}, u32[]{:S(2)}, u32[]{:S(2)}) %collective-permute-start.17) | collective-permute-done | bytes 262176 | tf_op jit(solution)/shard_map/ppermute | solution.py:28
  63.6 28.3 %project_and_attend.2 = bf16[4,2,2,16,2048]{4,3,2,1,0:T(8,128)(2,1)} custom-call(bf16[64,8192]{1,0:T(8,128)(2,1)} %bitcast.141, bf16[64,8192]{1,0:T(8,128)(2,1)} %copy-done.2, bf16[64,8192]{1,0:T(8,128)(2,1)} %copy-done.4, bf16[64,8192]{1,0:T(8,128)(2,1)} %copy-done.6, f32[1,8192]{1,0:T(1,128)} %refs_6_.1, f32[128,128]{1,0:T(8,128)} %copy.36.refs_5_.refs_7_, ...), custom_call_target="tpu_custom_call" | custom-call | flops 1 | bytes 1 | tf_op jit(solution)/shard_map/project_and_attend/pallas_call | solution.py:119
  100.0 28.3 %project_and_attend.3 = bf16[4,2,2,16,2048]{4,3,2,1,0:T(8,128)(2,1)} custom-call(bf16[64,8192]{1,0:T(8,128)(2,1)} %copy-done.1, bf16[32,8192]{1,0:T(8,128)(2,1)} %collective-permute-done.7.refs_1_, bf16[32,8192]{1,0:T(8,128)(2,1)} %collective-permute-done.8.refs_2_, bf16[64,8192]{1,0:T(8,128)(2,1)} %copy-done.5, bf16[32,8192]{1,0:T(8,128)(2,1)} %copy-done.12, ...), custom_call_target="tpu_custom_call" | custom-call | flops 1 | bytes 1 | tf_op jit(solution)/shard_map/project_and_attend/pallas_call | solution.py:119
  129.5 3.0 collective-permute-start.21
  133.8 4.9 %collective-permute-done.20 = bf16[2,2,16,2048]{3,2,1,0:T(8,128)(2,1)S(1)} collective-permute-done((bf16[2,2,16,2048]{3,2,1,0:T(8,128)(2,1)S(1)}, bf16[2,2,16,2048]{3,2,1,0:T(8,128)(2,1)S(1)}, u32[]{:S(2)}, u32[]{:S(2)}) %collective-permute-start.20) | collective-permute-done | bytes 262176 | tf_op jit(solution)/shard_map/ppermute | solution.py:28
  138.7 13.1 %collective-permute-done.21 = bf16[2,2,16,2048]{3,2,1,0:T(8,128)(2,1)S(1)} collective-permute-done((bf16[2,2,16,2048]{3,2,1,0:T(8,128)(2,1)S(1)}, bf16[2,2,16,2048]{3,2,1,0:T(8,128)(2,1)S(1)}, u32[]{:S(2)}, u32[]{:S(2)}) %collective-permute-start.21) | collective-permute-done | bytes 262176 | tf_op jit(solution)/shard_map/ppermute | solution.py:28
  151.9 3.1 collective-permute-done.22
  156.4 5.5 %out_projection.5 = (bf16[256,1024]{1,0:T(8,128)(2,1)}, bf16[256,1024]{1,0:T(8,128)(2,1)}) custom-call(bf16[512,2048]{1,0:T(8,128)(2,1)} %bitcast.132, bf16[1,2048,8192]{2,1,0:T(8,128)(2,1)} %wo_ref.9), custom_call_target="tpu_custom_call" | custom-call | flops 1 | bytes 1 | tf_op jit(solution)/shard_map/out_projection/pallas_call | solution.py:157
  163.4 5.6 %out_projection.6 = (bf16[256,1024]{1,0:T(8,128)(2,1)}, bf16[256,1024]{1,0:T(8,128)(2,1)}) custom-call(bf16[512,2048]{1,0:T(8,128)(2,1)} %bitcast.133, bf16[1,2048,8192]{2,1,0:T(8,128)(2,1)} %wo_ref.9), custom_call_target="tpu_custom_call" | custom-call | flops 1 | bytes 1 | tf_op jit(solution)/shard_map/out_projection/pallas_call | solution.py:157
  171.1 5.9 %collective-permute-done.23 = bf16[16,16,1024]{2,1,0:T(8,128)(2,1)S(1)} collective-permute-done((bf16[16,16,1024]{2,1,0:T(8,128)(2,1)}, bf16[16,16,1024]{2,1,0:T(8,128)(2,1)S(1)}, u32[]{:S(2)}, u32[]{:S(2)}) %collective-permute-start.23) | collective-permute-done | bytes 524320 | tf_op jit(solution)/shard_map/ppermute | solution.py:28
  177.8 4.0 %join_partials.5 = (bf16[4,6,16,1024]{3,2,1,0:T(8,128)(2,1)}, f32[4,6,16,128]{3,2,1,0:T(8,128)}) custom-call(s32[3,24]{1,0:T(4,128)} %pad_add_fusion.table_ref, bf16[16,16,1024]{2,1,0:T(8,128)(2,1)} %bitcast.154, bf16[1,16,16,1024]{3,2,1,0:T(8,128)(2,1)} %bitcast.155, bf16[16,16,8192]{2,1,0:T(8,128)(2,1)} %constant_dynamic-update-slice_fusion.resid_ref, ...), custom_call_target="tpu_custom_call" | custom-call | flops 1 | bytes 1 | tf_op jit(solution)/shard_map/join_partials/pallas_call | solution.py:199
  181.8 8.6 %out_projection.7 = (bf16[256,2048]{1,0:T(8,128)(2,1)}, bf16[256,2048]{1,0:T(8,128)(2,1)}) custom-call(bf16[512,2048]{1,0:T(8,128)(2,1)} %bitcast.134, bf16[1,2048,8192]{2,1,0:T(8,128)(2,1)} %wo_ref.9), custom_call_target="tpu_custom_call" | custom-call | flops 1 | bytes 1 | tf_op jit(solution)/shard_map/out_projection/pallas_call | solution.py:157
  191.7 4.0 %join_partials.6 = (bf16[4,6,16,1024]{3,2,1,0:T(8,128)(2,1)}, f32[4,6,16,128]{3,2,1,0:T(8,128)}) custom-call(s32[3,24]{1,0:T(4,128)} %pad_add_fusion.table_ref, bf16[16,16,1024]{2,1,0:T(8,128)(2,1)} %bitcast.156, bf16[1,16,16,1024]{3,2,1,0:T(8,128)(2,1)} %bitcast.157, bf16[16,16,8192]{2,1,0:T(8,128)(2,1)} %constant_dynamic-update-slice_fusion.resid_ref, ...), custom_call_target="tpu_custom_call" | custom-call | flops 1 | bytes 1 | tf_op jit(solution)/shard_map/join_partials/pallas_call | solution.py:199
  195.7 8.8 %out_projection.8 = (bf16[256,2048]{1,0:T(8,128)(2,1)}, bf16[256,2048]{1,0:T(8,128)(2,1)}) custom-call(bf16[512,2048]{1,0:T(8,128)(2,1)} %bitcast.135, bf16[1,2048,8192]{2,1,0:T(8,128)(2,1)} %wo_ref.9), custom_call_target="tpu_custom_call" | custom-call | flops 1 | bytes 1 | tf_op jit(solution)/shard_map/out_projection/pallas_call | solution.py:157
  209.8 7.2 %collective-permute-done.25.refs_1_ = bf16[6,16,1024]{2,1,0:T(8,128)(2,1)S(1)} collective-permute-done((bf16[6,16,1024]{2,1,0:T(8,128)(2,1)S(1)}, bf16[6,16,1024]{2,1,0:T(8,128)(2,1)S(1)}, u32[]{:S(2)}, u32[]{:S(2)}) %collective-permute-start.25) | collective-permute-done | bytes 196640 | tf_op jit(solution)/shard_map/ppermute | solution.py:28
  217.0 5.2 %collective-permute-start.29 = (bf16[6,16,1024]{2,1,0:T(8,128)(2,1)S(1)}, bf16[6,16,1024]{2,1,0:T(8,128)(2,1)S(1)}, u32[]{:S(2)}, u32[]{:S(2)}) collective-permute-start(bf16[6,16,1024]{2,1,0:T(8,128)(2,1)S(1)} %get-tuple-element.167), channel_id=1, source_target_pairs={{0,2},{2,4},{4,6},{6,0},{1,3},{3,5},{5,7},{7,1},{8,10},{10,12},{12... | collective-permute-start | bytes 589832 | tf_op jit(solution)/shard_map/ppermute | solution.py:28
  222.2 8.1 %collective-permute-done.26.refs_2_ = bf16[6,16,1024]{2,1,0:T(8,128)(2,1)S(1)} collective-permute-done((bf16[6,16,1024]{2,1,0:T(8,128)(2,1)S(1)}, bf16[6,16,1024]{2,1,0:T(8,128)(2,1)S(1)}, u32[]{:S(2)}, u32[]{:S(2)}) %collective-permute-start.26) | collective-permute-done | bytes 196640 | tf_op jit(solution)/shard_map/ppermute | solution.py:28
  230.3 3.4 collective-permute-start.30
  234.8 5.0 %join_partials.7 = (bf16[4,6,16,2048]{3,2,1,0:T(8,128)(2,1)}, f32[4,6,16,128]{3,2,1,0:T(8,128)}) custom-call(s32[3,24]{1,0:T(4,128)} %pad_add_fusion.table_ref, bf16[16,16,2048]{2,1,0:T(8,128)(2,1)} %bitcast.146, bf16[1,16,16,2048]{3,2,1,0:T(8,128)(2,1)} %bitcast.147, bf16[16,16,8192]{2,1,0:T(8,128)(2,1)} %constant_dynamic-update-slice_fusion.resid_ref, ...), custom_call_target="tpu_custom_call" | custom-call | flops 1 | bytes 1 | tf_op jit(solution)/shard_map/join_partials/pallas_call | solution.py:199
  239.8 8.7 %out_projection.9 = (bf16[256,2048]{1,0:T(8,128)(2,1)}, bf16[256,2048]{1,0:T(8,128)(2,1)}) custom-call(bf16[512,2048]{1,0:T(8,128)(2,1)} %bitcast.136, bf16[1,2048,8192]{2,1,0:T(8,128)(2,1)} %wo_ref.9), custom_call_target="tpu_custom_call" | custom-call | flops 1 | bytes 1 | tf_op jit(solution)/shard_map/out_projection/pallas_call | solution.py:157
  255.6 5.0 %join_partials.8 = (bf16[4,6,16,2048]{3,2,1,0:T(8,128)(2,1)}, f32[4,6,16,128]{3,2,1,0:T(8,128)}) custom-call(s32[3,24]{1,0:T(4,128)} %pad_add_fusion.table_ref, bf16[16,16,2048]{2,1,0:T(8,128)(2,1)} %bitcast.142, bf16[1,16,16,2048]{3,2,1,0:T(8,128)(2,1)} %bitcast.143, bf16[16,16,8192]{2,1,0:T(8,128)(2,1)} %constant_dynamic-update-slice_fusion.resid_ref, ...), custom_call_target="tpu_custom_call" | custom-call | flops 1 | bytes 1 | tf_op jit(solution)/shard_map/join_partials/pallas_call | solution.py:199
  264.9 13.2 %collective-permute-done.32.refs_9_ = bf16[6,16,2048]{2,1,0:T(8,128)(2,1)S(1)} collective-permute-done((bf16[6,16,2048]{2,1,0:T(8,128)(2,1)S(1)}, bf16[6,16,2048]{2,1,0:T(8,128)(2,1)S(1)}, u32[]{:S(2)}, u32[]{:S(2)}) %collective-permute-start.32) | collective-permute-done | bytes 393248 | tf_op jit(solution)/shard_map/ppermute | solution.py:28
  278.1 16.9 %collective-permute-done.33.refs_10_ = bf16[6,16,2048]{2,1,0:T(8,128)(2,1)S(1)} collective-permute-done((bf16[6,16,2048]{2,1,0:T(8,128)(2,1)S(1)}, bf16[6,16,2048]{2,1,0:T(8,128)(2,1)S(1)}, u32[]{:S(2)}, u32[]{:S(2)}) %collective-permute-start.33) | collective-permute-done | bytes 393248 | tf_op jit(solution)/shard_map/ppermute | solution.py:28
  298.3 5.0 %join_partials.9 = (bf16[4,6,16,2048]{3,2,1,0:T(8,128)(2,1)}, f32[4,6,16,128]{3,2,1,0:T(8,128)}) custom-call(s32[3,24]{1,0:T(4,128)} %pad_add_fusion.table_ref, bf16[16,16,2048]{2,1,0:T(8,128)(2,1)} %bitcast.144, bf16[1,16,16,2048]{3,2,1,0:T(8,128)(2,1)} %bitcast.145, bf16[16,16,8192]{2,1,0:T(8,128)(2,1)} %constant_dynamic-update-slice_fusion.resid_ref, ...), custom_call_target="tpu_custom_call" | custom-call | flops 1 | bytes 1 | tf_op jit(solution)/shard_map/join_partials/pallas_call | solution.py:199
  303.3 4.3 %collective-permute-done.36.refs_13_ = bf16[6,16,2048]{2,1,0:T(8,128)(2,1)S(1)} collective-permute-done((bf16[6,16,2048]{2,1,0:T(8,128)(2,1)S(1)}, bf16[6,16,2048]{2,1,0:T(8,128)(2,1)S(1)}, u32[]{:S(2)}, u32[]{:S(2)}) %collective-permute-start.36) | collective-permute-done | bytes 393248 | tf_op jit(solution)/shard_map/ppermute | solution.py:28
  307.6 4.2 %collective-permute-done.37.refs_14_ = bf16[6,16,2048]{2,1,0:T(8,128)(2,1)S(1)} collective-permute-done((bf16[6,16,2048]{2,1,0:T(8,128)(2,1)S(1)}, bf16[6,16,2048]{2,1,0:T(8,128)(2,1)S(1)}, u32[]{:S(2)}, u32[]{:S(2)}) %collective-permute-start.37) | collective-permute-done | bytes 393248 | tf_op jit(solution)/shard_map/ppermute | solution.py:28
  317.3 3.4 collective-permute-start.45
  332.1 18.0 %collective-permute-done.40.refs_17_ = bf16[6,16,2048]{2,1,0:T(8,128)(2,1)S(1)} collective-permute-done((bf16[6,16,2048]{2,1,0:T(8,128)(2,1)}, bf16[6,16,2048]{2,1,0:T(8,128)(2,1)S(1)}, u32[]{:S(2)}, u32[]{:S(2)}) %collective-permute-start.40) | collective-permute-done | bytes 393248 | tf_op jit(solution)/shard_map/ppermute | solution.py:28
  350.1 6.1 %collective-permute-done.41.refs_18_ = bf16[6,16,2048]{2,1,0:T(8,128)(2,1)S(1)} collective-permute-done((bf16[6,16,2048]{2,1,0:T(8,128)(2,1)}, bf16[6,16,2048]{2,1,0:T(8,128)(2,1)S(1)}, u32[]{:S(2)}, u32[]{:S(2)}) %collective-permute-start.41) | collective-permute-done | bytes 393248 | tf_op jit(solution)/shard_map/ppermute | solution.py:28
  359.0 13.5 %place_rows.1 = bf16[6,4,16,8192]{3,2,1,0:T(8,128)(2,1)} custom-call(s32[4]{0:T(128)} %compare_select_fusion.6.order_ref, bf16[6,16,1024]{2,1,0:T(8,128)(2,1)} %get-tuple-element.94.refs_0_, bf16[6,16,1024]{2,1,0:T(8,128)(2,1)} %copy-done.27, bf16[6,16,1024]{2,1,0:T(8,128)(2,1)} %copy-done.28, bf16[6,16,1024]{2,1,0:T(8,128)(2,1)} %copy-done.29, ...), custom_call_target="tpu_custom_call" | custom-call | flops 1 | bytes 1 | tf_op jit(solution)/shard_map/place_rows/pallas_call | solution.py:248
  (218 shorter events, 92.0 us)
Async XLA Ops:
  0.6 33.0 %collective-permute-start.6 = (bf16[64,8192]{1,0:T(8,128)(2,1)}, bf16[64,8192]{1,0:T(8,128)(2,1)S(1)}, u32[]{:S(2)}, u32[]{:S(2)}) collective-permute-start(bf16[64,8192]{1,0:T(8,128)(2,1)} %bitcast.138), channel_id=1, source_target_pairs={{0,16},{8,24},{16,0},{24,8},{1,17},{9,25},{17,1},{25,9},{2,18},{10... | collective-permute-start | bytes 3145736 | tf_op jit(solution)/shard_map/ppermute | solution.py:24
  2.2 33.3 %collective-permute-start = (bf16[64,8192]{1,0:T(8,128)(2,1)}, bf16[64,8192]{1,0:T(8,128)(2,1)S(1)}, u32[]{:S(2)}, u32[]{:S(2)}) collective-permute-start(bf16[64,8192]{1,0:T(8,128)(2,1)} %bitcast.139), channel_id=1, source_target_pairs={{0,1},{1,0},{2,3},{3,2},{4,5},{5,4},{6,7},{7,6},{8,9},{9,8},{10,11... | collective-permute-start | bytes 3145736 | tf_op jit(solution)/shard_map/ppermute | solution.py:28
  7.4 22.2 %collective-permute-start.13 = (bf16[16,8192]{1,0:T(8,128)(2,1)}, bf16[16,8192]{1,0:T(8,128)(2,1)S(1)}, u32[]{:S(2)}, u32[]{:S(2)}) collective-permute-start(bf16[16,8192]{1,0:T(8,128)(2,1)} %get-tuple-element.161), channel_id=1, source_target_pairs={{0,4},{2,6},{4,0},{6,2},{1,5},{3,7},{5,1},{7,3},{8,12},{10,14},{12... | collective-permute-start | bytes 786440 | tf_op jit(solution)/shard_map/ppermute | solution.py:28
  8.6 22.6 %collective-permute-start.14 = (bf16[16,8192]{1,0:T(8,128)(2,1)S(1)}, bf16[16,8192]{1,0:T(8,128)(2,1)S(1)}, u32[]{:S(2)}, u32[]{:S(2)}) collective-permute-start(bf16[16,8192]{1,0:T(8,128)(2,1)S(1)} %get-tuple-element.157), channel_id=1, source_target_pairs={{0,6},{2,0},{4,2},{6,4},{1,7},{3,1},{5,3},{7,5},{8,14},{10,8},{12,... | collective-permute-start | bytes 786440 | tf_op jit(solution)/shard_map/ppermute | solution.py:28
  25.7 35.9 %collective-permute-start.1 = (bf16[64,8192]{1,0:T(8,128)(2,1)}, bf16[64,8192]{1,0:T(8,128)(2,1)S(1)}, u32[]{:S(2)}, u32[]{:S(2)}) collective-permute-start(bf16[64,8192]{1,0:T(8,128)(2,1)} %bitcast.140), channel_id=1, source_target_pairs={{0,8},{8,0},{16,24},{24,16},{1,9},{9,1},{17,25},{25,17},{2,10},{10... | collective-permute-start | bytes 3145736 | tf_op jit(solution)/shard_map/ppermute | solution.py:24
  33.7 23.3 %collective-permute-start.17 = (bf16[16,8192]{1,0:T(8,128)(2,1)S(1)}, bf16[16,8192]{1,0:T(8,128)(2,1)S(1)}, u32[]{:S(2)}, u32[]{:S(2)}) collective-permute-start(bf16[16,8192]{1,0:T(8,128)(2,1)S(1)} %get-tuple-element.155), channel_id=1, source_target_pairs={{0,4},{2,6},{4,0},{6,2},{1,5},{3,7},{5,1},{7,3},{8,12},{10,14},{12... | collective-permute-start | bytes 786440 | tf_op jit(solution)/shard_map/ppermute | solution.py:28
  35.5 23.7 %collective-permute-start.18 = (bf16[16,8192]{1,0:T(8,128)(2,1)S(1)}, bf16[16,8192]{1,0:T(8,128)(2,1)S(1)}, u32[]{:S(2)}, u32[]{:S(2)}) collective-permute-start(bf16[16,8192]{1,0:T(8,128)(2,1)S(1)} %get-tuple-element.154), channel_id=1, source_target_pairs={{0,6},{2,0},{4,2},{6,4},{1,7},{3,1},{5,3},{7,5},{8,14},{10,8},{12,... | collective-permute-start | bytes 786440 | tf_op jit(solution)/shard_map/ppermute | solution.py:28
  37.5 24.6 %collective-permute-start.7 = (bf16[32,8192]{1,0:T(8,128)(2,1)S(1)}, bf16[32,8192]{1,0:T(8,128)(2,1)}, u32[]{:S(2)}, u32[]{:S(2)}) collective-permute-start(bf16[32,8192]{1,0:T(8,128)(2,1)S(1)} %slice.124), channel_id=1, source_target_pairs={{0,1},{1,0},{2,3},{3,2},{4,5},{5,4},{6,7},{7,6},{8,9},{9,8},{10,11... | collective-permute-start | bytes 1572872 | tf_op jit(solution)/shard_map/ppermute | solution.py:28
  59.3 34.8 %collective-permute-start.19 = (bf16[4,16,8192]{2,1,0:T(8,128)(2,1)S(1)}, bf16[4,16,8192]{2,1,0:T(8,128)(2,1)S(1)}, u32[]{:S(2)}, u32[]{:S(2)}) collective-permute-start(bf16[4,16,8192]{2,1,0:T(8,128)(2,1)S(1)} %pad_maximum_fusion.1), channel_id=1, source_target_pairs={{0,8},{8,0},{16,24},{24,16},{1,9},{9,1},{17,25},{25,17},{2,10},{10... | collective-permute-start | bytes 3145736 | tf_op jit(solution)/shard_map/ppermute | solution.py:24
  61.6 37.4 %collective-permute-start.9 = (bf16[64,8192]{1,0:T(8,128)(2,1)S(1)}, bf16[64,8192]{1,0:T(8,128)(2,1)S(1)}, u32[]{:S(2)}, u32[]{:S(2)}) collective-permute-start(bf16[64,8192]{1,0:T(8,128)(2,1)S(1)} %collective-permute-done.6.refs_0_), channel_id=1, source_target_pairs={{0,8},{8,0},{16,24},{24,16},{1,9},{9,1},{17,25},{25,17},{2,10},{10... | collective-permute-start | bytes 3145736 | tf_op jit(solution)/shard_map/ppermute | solution.py:24
  62.1 34.9 %collective-permute-start.10 = (bf16[32,8192]{1,0:T(8,128)(2,1)}, bf16[32,8192]{1,0:T(8,128)(2,1)S(1)}, u32[]{:S(2)}, u32[]{:S(2)}) collective-permute-start(bf16[32,8192]{1,0:T(8,128)(2,1)} %collective-permute-done.7.refs_1_), channel_id=1, source_target_pairs={{0,8},{8,0},{16,24},{24,16},{1,9},{9,1},{17,25},{25,17},{2,10},{10... | collective-permute-start | bytes 1572872 | tf_op jit(solution)/shard_map/ppermute | solution.py:24
  62.2 36.8 %collective-permute-start.11 = (bf16[32,8192]{1,0:T(8,128)(2,1)}, bf16[32,8192]{1,0:T(8,128)(2,1)}, u32[]{:S(2)}, u32[]{:S(2)}) collective-permute-start(bf16[32,8192]{1,0:T(8,128)(2,1)} %collective-permute-done.8.refs_2_), channel_id=1, source_target_pairs={{0,8},{8,0},{16,24},{24,16},{1,9},{9,1},{17,25},{25,17},{2,10},{10... | collective-permute-start | bytes 1572872 | tf_op jit(solution)/shard_map/ppermute | solution.py:24
  93.1 39.4 %collective-permute-start.3 = (bf16[2,2,16,2048]{3,2,1,0:T(8,128)(2,1)S(1)}, bf16[2,2,16,2048]{3,2,1,0:T(8,128)(2,1)S(1)}, u32[]{:S(2)}, u32[]{:S(2)}) collective-permute-start(bf16[2,2,16,2048]{3,2,1,0:T(8,128)(2,1)S(1)} %get-tuple-element.164), channel_id=1, source_target_pairs={{0,2},{2,4},{4,6},{6,0},{1,3},{3,5},{5,7},{7,1},{8,10},{10,12},{12... | collective-permute-start | bytes 786440 | tf_op jit(solution)/shard_map/ppermute | solution.py:28
  94.2 38.6 %collective-permute-start.4 = (bf16[2,2,16,2048]{3,2,1,0:T(8,128)(2,1)S(1)}, bf16[2,2,16,2048]{3,2,1,0:T(8,128)(2,1)S(1)}, u32[]{:S(2)}, u32[]{:S(2)}) collective-permute-start(bf16[2,2,16,2048]{3,2,1,0:T(8,128)(2,1)S(1)} %get-tuple-element.163), channel_id=1, source_target_pairs={{0,4},{2,6},{4,0},{6,2},{1,5},{3,7},{5,1},{7,3},{8,12},{10,14},{12... | collective-permute-start | bytes 786440 | tf_op jit(solution)/shard_map/ppermute | solution.py:28
  97.0 35.8 %collective-permute-start.5 = (bf16[2,2,16,2048]{3,2,1,0:T(8,128)(2,1)S(1)}, bf16[2,2,16,2048]{3,2,1,0:T(8,128)(2,1)S(1)}, u32[]{:S(2)}, u32[]{:S(2)}) collective-permute-start(bf16[2,2,16,2048]{3,2,1,0:T(8,128)(2,1)S(1)} %get-tuple-element.162), channel_id=1, source_target_pairs={{0,6},{2,0},{4,2},{6,4},{1,7},{3,1},{5,3},{7,5},{8,14},{10,8},{12,... | collective-permute-start | bytes 786440 | tf_op jit(solution)/shard_map/ppermute | solution.py:28
  129.5 22.3 %collective-permute-start.21 = (bf16[2,2,16,2048]{3,2,1,0:T(8,128)(2,1)S(1)}, bf16[2,2,16,2048]{3,2,1,0:T(8,128)(2,1)S(1)}, u32[]{:S(2)}, u32[]{:S(2)}) collective-permute-start(bf16[2,2,16,2048]{3,2,1,0:T(8,128)(2,1)S(1)} %get-tuple-element.152), channel_id=1, source_target_pairs={{0,4},{2,6},{4,0},{6,2},{1,5},{3,7},{5,1},{7,3},{8,12},{10,14},{12... | collective-permute-start | bytes 786440 | tf_op jit(solution)/shard_map/ppermute | solution.py:28
  132.5 22.5 %collective-permute-start.22 = (bf16[2,2,16,2048]{3,2,1,0:T(8,128)(2,1)S(1)}, bf16[2,2,16,2048]{3,2,1,0:T(8,128)(2,1)S(1)}, u32[]{:S(2)}, u32[]{:S(2)}) collective-permute-start(bf16[2,2,16,2048]{3,2,1,0:T(8,128)(2,1)S(1)} %get-tuple-element.151), channel_id=1, source_target_pairs={{0,6},{2,0},{4,2},{6,4},{1,7},{3,1},{5,3},{7,5},{8,14},{10,8},{12,... | collective-permute-start | bytes 786440 | tf_op jit(solution)/shard_map/ppermute | solution.py:28
  169.0 21.9 %collective-permute-start.24 = (bf16[16,16,1024]{2,1,0:T(8,128)(2,1)}, bf16[16,16,1024]{2,1,0:T(8,128)(2,1)S(1)}, u32[]{:S(2)}, u32[]{:S(2)}) collective-permute-start(bf16[16,16,1024]{2,1,0:T(8,128)(2,1)} %bitcast.164), channel_id=1, source_target_pairs={{0,1},{1,0},{2,3},{3,2},{4,5},{5,4},{6,7},{7,6},{8,9},{9,8},{10,11... | collective-permute-start | bytes 1572872 | tf_op jit(solution)/shard_map/ppermute | solution.py:28
  190.4 43.3 %collective-permute-start.28 = (bf16[16,16,2048]{2,1,0:T(8,128)(2,1)}, bf16[16,16,2048]{2,1,0:T(8,128)(2,1)S(1)}, u32[]{:S(2)}, u32[]{:S(2)}) collective-permute-start(bf16[16,16,2048]{2,1,0:T(8,128)(2,1)} %bitcast.162), channel_id=1, source_target_pairs={{0,1},{1,0},{2,3},{3,2},{4,5},{5,4},{6,7},{7,6},{8,9},{9,8},{10,11... | collective-permute-start | bytes 3145736 | tf_op jit(solution)/shard_map/ppermute | solution.py:28
  204.5 50.1 %collective-permute-start.35 = (bf16[16,16,2048]{2,1,0:T(8,128)(2,1)}, bf16[16,16,2048]{2,1,0:T(8,128)(2,1)S(1)}, u32[]{:S(2)}, u32[]{:S(2)}) collective-permute-start(bf16[16,16,2048]{2,1,0:T(8,128)(2,1)} %bitcast.160), channel_id=1, source_target_pairs={{0,1},{1,0},{2,3},{3,2},{4,5},{5,4},{6,7},{7,6},{8,9},{9,8},{10,11... | collective-permute-start | bytes 3145736 | tf_op jit(solution)/shard_map/ppermute | solution.py:28
  206.7 23.6 %collective-permute-start.26 = (bf16[6,16,1024]{2,1,0:T(8,128)(2,1)S(1)}, bf16[6,16,1024]{2,1,0:T(8,128)(2,1)S(1)}, u32[]{:S(2)}, u32[]{:S(2)}) collective-permute-start(bf16[6,16,1024]{2,1,0:T(8,128)(2,1)S(1)} %get-tuple-element.170), channel_id=1, source_target_pairs={{0,4},{2,6},{4,0},{6,2},{1,5},{3,7},{5,1},{7,3},{8,12},{10,14},{12... | collective-permute-start | bytes 589832 | tf_op jit(solution)/shard_map/ppermute | solution.py:28
  207.0 26.7 %collective-permute-start.27 = (bf16[6,16,1024]{2,1,0:T(8,128)(2,1)S(1)}, bf16[6,16,1024]{2,1,0:T(8,128)(2,1)S(1)}, u32[]{:S(2)}, u32[]{:S(2)}) collective-permute-start(bf16[6,16,1024]{2,1,0:T(8,128)(2,1)S(1)} %get-tuple-element.169), channel_id=1, source_target_pairs={{0,6},{2,0},{4,2},{6,4},{1,7},{3,1},{5,3},{7,5},{8,14},{10,8},{12,... | collective-permute-start | bytes 589832 | tf_op jit(solution)/shard_map/ppermute | solution.py:28
  217.0 33.0 %collective-permute-start.29 = (bf16[6,16,1024]{2,1,0:T(8,128)(2,1)S(1)}, bf16[6,16,1024]{2,1,0:T(8,128)(2,1)S(1)}, u32[]{:S(2)}, u32[]{:S(2)}) collective-permute-start(bf16[6,16,1024]{2,1,0:T(8,128)(2,1)S(1)} %get-tuple-element.167), channel_id=1, source_target_pairs={{0,2},{2,4},{4,6},{6,0},{1,3},{3,5},{5,7},{7,1},{8,10},{10,12},{12... | collective-permute-start | bytes 589832 | tf_op jit(solution)/shard_map/ppermute | solution.py:28
  248.5 48.8 %collective-permute-start.39 = (bf16[16,16,2048]{2,1,0:T(8,128)(2,1)}, bf16[16,16,2048]{2,1,0:T(8,128)(2,1)S(1)}, u32[]{:S(2)}, u32[]{:S(2)}) collective-permute-start(bf16[16,16,2048]{2,1,0:T(8,128)(2,1)} %bitcast.161), channel_id=1, source_target_pairs={{0,1},{1,0},{2,3},{3,2},{4,5},{5,4},{6,7},{7,6},{8,9},{9,8},{10,11... | collective-permute-start | bytes 3145736 | tf_op jit(solution)/shard_map/ppermute | solution.py:28
  250.0 28.1 %collective-permute-start.32 = (bf16[6,16,2048]{2,1,0:T(8,128)(2,1)S(1)}, bf16[6,16,2048]{2,1,0:T(8,128)(2,1)S(1)}, u32[]{:S(2)}, u32[]{:S(2)}) collective-permute-start(bf16[6,16,2048]{2,1,0:T(8,128)(2,1)S(1)} %get-tuple-element.149), channel_id=1, source_target_pairs={{0,2},{2,4},{4,6},{6,0},{1,3},{3,5},{5,7},{7,1},{8,10},{10,12},{12... | collective-permute-start | bytes 1179656 | tf_op jit(solution)/shard_map/ppermute | solution.py:28
  252.0 43.0 %collective-permute-start.33 = (bf16[6,16,2048]{2,1,0:T(8,128)(2,1)S(1)}, bf16[6,16,2048]{2,1,0:T(8,128)(2,1)S(1)}, u32[]{:S(2)}, u32[]{:S(2)}) collective-permute-start(bf16[6,16,2048]{2,1,0:T(8,128)(2,1)S(1)} %get-tuple-element.148), channel_id=1, source_target_pairs={{0,4},{2,6},{4,0},{6,2},{1,5},{3,7},{5,1},{7,3},{8,12},{10,14},{12... | collective-permute-start | bytes 1179656 | tf_op jit(solution)/shard_map/ppermute | solution.py:28
  254.6 42.7 %collective-permute-start.34 = (bf16[6,16,2048]{2,1,0:T(8,128)(2,1)S(1)}, bf16[6,16,2048]{2,1,0:T(8,128)(2,1)S(1)}, u32[]{:S(2)}, u32[]{:S(2)}) collective-permute-start(bf16[6,16,2048]{2,1,0:T(8,128)(2,1)S(1)} %get-tuple-element.147), channel_id=1, source_target_pairs={{0,6},{2,0},{4,2},{6,4},{1,7},{3,1},{5,3},{7,5},{8,14},{10,8},{12,... | collective-permute-start | bytes 1179656 | tf_op jit(solution)/shard_map/ppermute | solution.py:28
  262.9 44.7 %collective-permute-start.36 = (bf16[6,16,2048]{2,1,0:T(8,128)(2,1)S(1)}, bf16[6,16,2048]{2,1,0:T(8,128)(2,1)S(1)}, u32[]{:S(2)}, u32[]{:S(2)}) collective-permute-start(bf16[6,16,2048]{2,1,0:T(8,128)(2,1)S(1)} %get-tuple-element.145), channel_id=1, source_target_pairs={{0,2},{2,4},{4,6},{6,0},{1,3},{3,5},{5,7},{7,1},{8,10},{10,12},{12... | collective-permute-start | bytes 1179656 | tf_op jit(solution)/shard_map/ppermute | solution.py:28
  278.1 33.7 %collective-permute-start.37 = (bf16[6,16,2048]{2,1,0:T(8,128)(2,1)S(1)}, bf16[6,16,2048]{2,1,0:T(8,128)(2,1)S(1)}, u32[]{:S(2)}, u32[]{:S(2)}) collective-permute-start(bf16[6,16,2048]{2,1,0:T(8,128)(2,1)S(1)} %get-tuple-element.144), channel_id=1, source_target_pairs={{0,4},{2,6},{4,0},{6,2},{1,5},{3,7},{5,1},{7,3},{8,12},{10,14},{12... | collective-permute-start | bytes 1179656 | tf_op jit(solution)/shard_map/ppermute | solution.py:28
  325.2 24.8 %collective-permute-start.40 = (bf16[6,16,2048]{2,1,0:T(8,128)(2,1)}, bf16[6,16,2048]{2,1,0:T(8,128)(2,1)S(1)}, u32[]{:S(2)}, u32[]{:S(2)}) collective-permute-start(bf16[6,16,2048]{2,1,0:T(8,128)(2,1)} %get-tuple-element.141), channel_id=1, source_target_pairs={{0,2},{2,4},{4,6},{6,0},{1,3},{3,5},{5,7},{7,1},{8,10},{10,12},{12... | collective-permute-start | bytes 1179656 | tf_op jit(solution)/shard_map/ppermute | solution.py:28
  325.4 30.8 %collective-permute-start.41 = (bf16[6,16,2048]{2,1,0:T(8,128)(2,1)}, bf16[6,16,2048]{2,1,0:T(8,128)(2,1)S(1)}, u32[]{:S(2)}, u32[]{:S(2)}) collective-permute-start(bf16[6,16,2048]{2,1,0:T(8,128)(2,1)} %get-tuple-element.140), channel_id=1, source_target_pairs={{0,4},{2,6},{4,0},{6,2},{1,5},{3,7},{5,1},{7,3},{8,12},{10,14},{12... | collective-permute-start | bytes 1179656 | tf_op jit(solution)/shard_map/ppermute | solution.py:28
  327.8 31.2 %collective-permute-start.42 = (bf16[6,16,2048]{2,1,0:T(8,128)(2,1)}, bf16[6,16,2048]{2,1,0:T(8,128)(2,1)}, u32[]{:S(2)}, u32[]{:S(2)}) collective-permute-start(bf16[6,16,2048]{2,1,0:T(8,128)(2,1)} %get-tuple-element.139), channel_id=1, source_target_pairs={{0,6},{2,0},{4,2},{6,4},{1,7},{3,1},{5,3},{7,5},{8,14},{10,8},{12,... | collective-permute-start | bytes 1179656 | tf_op jit(solution)/shard_map/ppermute | solution.py:28
  (52 other events, 1014.5 us)

commit v3 on v2

--- a/solution.py
+++ b/solution.py
@@ -13,7 +13,6 @@
 ROPE_THETA = 500000.0
 VMEM_BYTES = 56 * 1024 * 1024
 CHUNKS = (1, 1, 2, 2, 2)
-AHEAD = 2
 
 
 def params():
@@ -22,6 +21,9 @@
 
 def swap(value, axis, size, step):
     return lax.ppermute(value, axis, [(j, j ^ step) for j in range(size)])
+
+
+sync = lax.optimization_barrier
 
 
 def shift(value, axis, size, step):
@@ -175,89 +177,92 @@
     )(ctx, wo)
 
 
-def join_kernel(n_slots, block, table_ref, own_ref, other_ref, resid_ref, head_ref, packed_ref, stats_ref):
-    dest = pl.program_id(0)
+def join_kernel(n_slots, block, table_ref, near_ref, far_ref, near_other, far_other, resid_ref, pair_ref, head_ref, *out_refs):
+    packed_refs, stats_ref = out_refs[:-1], out_refs[-1]
     head = head_ref[...]
     lane = lax.broadcasted_iota(jnp.int32, (block, HD), 1)
     row = lax.broadcasted_iota(jnp.int32, (block, 1), 0)
-
-    for slot in range(n_slots):
-        entry = dest * n_slots + slot
-        part, resid, live = table_ref[0, entry], table_ref[1, entry], table_ref[2, entry]
-        added = own_ref[part].astype(jnp.float32)
-        for k in range(other_ref.shape[0]):
-            added = added + other_ref[k, part].astype(jnp.float32)
-        hidden = resid_ref[resid].astype(jnp.float32) + added
-        packed_ref[slot] = jnp.where(row < live, hidden, 0.0).astype(jnp.bfloat16)
-        squares = jnp.sum(hidden * hidden, axis=-1, keepdims=True)
-        scored = jnp.sum(hidden * head, axis=-1, keepdims=True)
-        stats_ref[slot] = jnp.where(lane == 0, squares, jnp.where(lane == 1, scored, 0.0))
-
-
-def join(table, own, other, resid, head, chunk, n_dp, n_slots, block):
-    blocks, _, cols = own.shape
-    return pl.pallas_call(
+    step = pl.program_id(0)
+    slots = packed_refs[0].shape[0]
+
+    for dest, packed_ref in enumerate(packed_refs):
+        for slot in range(slots):
+            entry = dest * n_slots + step * slots + slot
+            part, resid, live = table_ref[0, entry], table_ref[1, entry], table_ref[2, entry]
+            is_far = table_ref[4, entry] > 0
+            added = jnp.where(is_far, far_ref[part], near_ref[part]).astype(jnp.float32)
+            for k in range(near_other.shape[0]):
+                added = added + jnp.where(is_far, far_other[k, part], near_other[k, part]).astype(jnp.float32)
+            rows_in = jnp.where(table_ref[3, entry] > 0, pair_ref[resid], resid_ref[resid])
+            hidden = rows_in.astype(jnp.float32) + added
+            packed_ref[slot] = jnp.where(row < live, hidden, 0.0).astype(jnp.bfloat16)
+            squares = jnp.sum(hidden * hidden, axis=-1, keepdims=True)
+            scored = jnp.sum(hidden * head, axis=-1, keepdims=True)
+            stats_ref[dest, slot] = jnp.where(lane == 0, squares, jnp.where(lane == 1, scored, 0.0))
+
+
+def join(table, owns, others, resid, resid_pair, head, chunk, n_dp, n_slots, block):
+    cols = owns[0].shape[-1]
+    slots = n_slots // 2
+    fixed = lambda i, t: (0, 0, 0)
+    here = lambda i, t: (0, 0, chunk)
+    out = pl.pallas_call(
         functools.partial(join_kernel, n_slots, block),
-        out_shape=[
-            jax.ShapeDtypeStruct((n_dp, n_slots, block, cols), jnp.bfloat16),
-            jax.ShapeDtypeStruct((n_dp, n_slots, block, HD), jnp.float32),
-        ],
+        out_shape=[jax.ShapeDtypeStruct((n_slots, block, cols), jnp.bfloat16) for _ in range(n_dp)]
+        + [jax.ShapeDtypeStruct((n_dp, n_slots, block, HD), jnp.float32)],
         grid_spec=pltpu.PrefetchScalarGridSpec(
             num_scalar_prefetch=1,
-            grid=(n_dp,),
+            grid=(n_slots // slots,),
             in_specs=[
-                pl.BlockSpec(own.shape, lambda d, t: (0, 0, 0)),
-                pl.BlockSpec(other.shape, lambda d, t: (0, 0, 0, 0)),
-                pl.BlockSpec((blocks, block, cols), lambda d, t: (0, 0, chunk)),
-                pl.BlockSpec((1, cols), lambda d, t: (0, chunk)),
+                pl.BlockSpec(owns[0].shape, fixed),
+                pl.BlockSpec(owns[1].shape, fixed),
+                pl.BlockSpec(others[0].shape, lambda i, t: (0, 0, 0, 0)),
+                pl.BlockSpec(others[1].shape, lambda i, t: (0, 0, 0, 0)),
+                pl.BlockSpec((resid.shape[0], block, cols), here),
+                pl.BlockSpec((resid.shape[0], block, cols), here),
+                pl.BlockSpec((1, cols), lambda i, t: (0, chunk)),
             ],
-            out_specs=[
-                pl.BlockSpec((None, n_slots, block, cols), lambda d, t: (d, 0, 0, 0)),
-                pl.BlockSpec((None, n_slots, block, HD), lambda d, t: (d, 0, 0, 0)),
-            ],
+            out_specs=[pl.BlockSpec((slots, block, cols), lambda i, t: (i, 0, 0)) for _ in range(n_dp)]
+            + [pl.BlockSpec((n_dp, slots, block, HD), lambda i, t: (0, i, 0, 0))],
         ),
         compiler_params=params(),
         cost_estimate=pl.CostEstimate(flops=1, bytes_accessed=1, transcendentals=0),
         name="join_partials",
-    )(table, own, other, resid, head)
-
-
-def place_kernel(sizes, count, order_ref, *refs):
+    )(table, *owns, *others, resid, resid_pair, head)
+    return list(out[:-1]), out[-1]
+
+
+def place_kernel(count, order_ref, *refs):
     out_ref = refs[-1]
-    step = pl.program_id(1)
-    first = 0
-    for chunk, size in enumerate(sizes):
-        @pl.when((step >= first) & (step < first + size))
-        def _(chunk=chunk):
-            for k in range(count):
-                out_ref[:, order_ref[k]] = refs[chunk * count + k][...]
-
-        first += size
-
-
-def place(order, arrived, sizes, width):
-    n_slots, block, _ = arrived[0][0].shape
-    count = len(arrived[0])
-    unit = width // sum(sizes)
-    rows = n_slots // 2
-    firsts = [sum(sizes[:c]) for c in range(len(sizes))]
-
-    def spec(first, size):
-        return pl.BlockSpec((rows, block, unit), lambda h, c, o: (h, 0, jnp.clip(c - first, 0, size - 1)))
-
+    for k in range(count):
+        out_ref[:, order_ref[k]] = refs[k][...]
+
+
+def place(order, pieces, whole, chunk, width):
+    n_slots, block, cols = pieces[0].shape
+    count = len(pieces)
+    rows = n_slots // 3
+    specs = [pl.BlockSpec((rows, block, cols), lambda i, o: (i, 0, 0)) for _ in pieces]
+    operands = list(pieces)
+    aliases = {}
+    if whole is not None:
+        specs.append(pl.BlockSpec(memory_space=pl.ANY))
+        operands.append(whole)
+        aliases = {1 + count: 0}
     return pl.pallas_call(
-        functools.partial(place_kernel, sizes, count),
+        functools.partial(place_kernel, count),
         out_shape=jax.ShapeDtypeStruct((n_slots, count, block, width), jnp.bfloat16),
         grid_spec=pltpu.PrefetchScalarGridSpec(
             num_scalar_prefetch=1,
-            grid=(n_slots // rows, sum(sizes)),
-            in_specs=[spec(f, s) for f, s in zip(firsts, sizes) for _ in range(count)],
-            out_specs=pl.BlockSpec((rows, count, block, unit), lambda h, c, o: (h, 0, 0, c)),
+            grid=(n_slots // rows,),
+            in_specs=specs,
+            out_specs=pl.BlockSpec((rows, count, block, cols), lambda i, o: (i, 0, 0, chunk)),
         ),
+        input_output_aliases=aliases,
         compiler_params=params(),
         cost_estimate=pl.CostEstimate(flops=1, bytes_accessed=1, transcendentals=0),
         name="place_rows",
-    )(order, *[piece for pieces in arrived for piece in pieces])
+    )(order, *operands)
 
 
 def on_device(responses, lengths, dest_dp, dest_slot, wq, wkv, wo, norm_gain, head_vec):
@@ -271,23 +276,6 @@
     block = local_len // n_dp
     my_sec, my_dp, my_tp = lax.axis_index("sec"), lax.axis_index("dp"), lax.axis_index("tp")
 
-    mine = responses[0]
-    near = [mine] + [shift(mine, "tp", n_tp, k) for k in range(1, n_tp)]
-    far_mine = swap(mine, "sec", n_sec, 2)
-    half = local_len // 2
-    far = [far_mine]
-    for k in range(1, n_tp):
-        parts = [shift(far_mine[:half], "tp", n_tp, k), swap(near[k][half:], "sec", n_sec, 2)]
-        far += parts if half % 16 == 0 else [jnp.concatenate(parts, axis=0)]
-    near = near + [swap(v, "sec", n_sec, 1) for v in near]
-    far = far + [swap(v, "sec", n_sec, 1) for v in far]
-
-    def quarters(v):
-        part = lambda k: lax.dynamic_slice_in_dim(v, lax.rem(my_dp + k, n_dp) * block, block, 0)
-        return jnp.stack([part(0)] + [shift(part(k), "dp", n_dp, k) for k in range(1, n_dp)])
-
-    resid_0, resid_2 = quarters(mine), quarters(far_mine)
-
     owners = lax.rem(my_tp - jnp.arange(n_tp) + n_tp, n_tp)
     positions = (owners[:, None] * local_len + jnp.arange(local_len)[None, :]).reshape(seq)
     frequency = jnp.exp(jnp.arange(HD // 2, dtype=jnp.float32) * (-2.0 * math.log(ROPE_THETA) / HD))
@@ -296,29 +284,48 @@
     sin = jnp.concatenate([-jnp.sin(angles), jnp.sin(angles)], axis=1)
     mask = (positions[:, None] >= positions[None, :]).astype(jnp.float32)
 
-    def spread(pieces):
-        ctx = attention(pieces, norm_gain, cos, sin, mask, wq, wkv, n_dp, n_tp)
+    mine = responses[0]
+    quarter = lambda k: lax.dynamic_slice_in_dim(mine, lax.rem(my_dp + k, n_dp) * block, block, 0)
+    resid = [quarter(0)] + [shift(quarter(k), "dp", n_dp, k) for k in range(1, n_dp)]
+    near = [mine] + [shift(mine, "tp", n_tp, k) for k in range(1, n_tp)]
+    far_mine = swap(mine, "sec", n_sec, 2)
+    near, far_mine, resid, cos, sin, mask = sync((near, far_mine, resid, cos, sin, mask))
+
+    half = local_len // 2
+    far = [far_mine]
+    for k in range(1, n_tp):
+        parts = [shift(far_mine[:half], "tp", n_tp, k), swap(near[k][half:], "sec", n_sec, 2)]
+        far += parts if half % 16 == 0 else [jnp.concatenate(parts, axis=0)]
+    near_pair = [swap(v, "sec", n_sec, 1) for v in near]
+    resid = jnp.stack(resid)
+    far, near, near_pair, resid = sync((far, near, near_pair, resid))
+
+    attend = lambda pieces: attention(pieces, norm_gain, cos, sin, mask, wq, wkv, n_dp, n_tp)
+
+    def spread(ctx):
         here = lambda k: lax.dynamic_index_in_dim(ctx, lax.rem(my_dp + k, n_dp), 0, keepdims=False)
-        parts = [here(0)] + [shift(here(k), "dp", n_dp, k) for k in range(1, n_dp)]
-        return ctx, parts
-
-    first_ctx, first_parts = spread(near)
-    resid = jnp.concatenate(
-        [resid_0, swap(resid_0, "sec", n_sec, 1), resid_2, swap(resid_2, "sec", n_sec, 1)], axis=0
-    )
-    far, first_ctx, resid = lax.optimization_barrier((far, first_ctx, resid))
-    _, second_parts = spread(far)
-    q_width = wq.shape[2]
-    ctx_rows = jnp.stack(first_parts + second_parts, axis=1).reshape(-1, q_width)
-    owned = ctx_rows.shape[0] // n_tp
+        return [here(0)] + [shift(here(k), "dp", n_dp, k) for k in range(1, n_dp)]
+
+    def gathered(parts):
+        return jnp.stack(parts, axis=1).reshape(-1, wq.shape[2])
+
+    near_ctx = attend(near + near_pair)
+    far_pair = [swap(v, "sec", n_sec, 1) for v in far]
+    resid_far = swap(resid, "sec", n_sec, 2)
+    near_ctx, far, far_pair, resid, resid_far = sync((near_ctx, far, far_pair, resid, resid_far))
+    near_rows = spread(near_ctx)
+    resid = jnp.concatenate([resid, resid_far], axis=0)
+    resid_pair = swap(resid, "sec", n_sec, 1)
+    far_ctx = attend(far + far_pair)
+    near_rows, far_ctx, resid, resid_pair = sync((near_rows, far_ctx, resid, resid_pair))
 
     row_dp = lax.dynamic_index_in_dim(dest_dp, my_sec, 0, keepdims=False)
     row_slot = lax.dynamic_index_in_dim(dest_slot, my_sec, 0, keepdims=False)
     sample = jnp.arange(samples)
     i_rel = my_sec ^ (sample // n_dp)
     k_rel = lax.rem(my_dp - sample % n_dp + n_dp, n_dp)
-    part_at = ((i_rel // 2) * n_dp + k_rel) * 2 + i_rel % 2
-    resid_at = i_rel * n_dp + k_rel
+    part_at = k_rel * 2 + i_rel % 2
+    resid_at = (i_rel // 2) * n_dp + k_rel
     dests = lax.rem(my_dp + jnp.arange(n_dp), n_dp)
     chosen = (row_dp[None, None, :] == dests[:, None, None]) & (
         row_slot[None, None, :] == jnp.arange(n_slots)[None, :, None]
@@ -326,39 +333,68 @@
     first_pos = my_tp * local_len + my_dp * block
     live = jnp.clip(lengths - first_pos, 0, block)
     pick = lambda v: jnp.sum(jnp.where(chosen, v[None, None, :], 0), axis=-1).reshape(-1)
-    table = jnp.stack([pick(part_at), pick(resid_at), pick(live)]).astype(jnp.int32)
+    table = jnp.stack([pick(part_at), pick(resid_at), pick(live), pick(i_rel % 2), pick(i_rel // 2)]).astype(jnp.int32)
     order = lax.rem(my_dp - jnp.arange(n_dp) + n_dp, n_dp).astype(jnp.int32)
 
     unit = width // sum(CHUNKS)
     starts = [unit * sum(CHUNKS[:c]) for c in range(len(CHUNKS))]
-    stats, arrived, owns, sends = [], [], [], []
-
-    def project(ctx_from):
-        own, send = out_projection(ctx_from, wo, owned, starts[len(owns)], unit * CHUNKS[len(owns)])
-        owns.append(own.reshape(-1, block, own.shape[-1]))
-        sends.append(send.reshape(n_tp - 1, -1, block, own.shape[-1]))
-
-    for _ in range(AHEAD):
-        project(ctx_rows)
-        ctx_rows, owns[-1] = lax.optimization_barrier((ctx_rows, owns[-1]))
-    for chunk, size in enumerate(CHUNKS):
-        other = [shift(sends[chunk][k - 1], "tp", n_tp, n_tp - k) for k in range(1, n_tp)]
-        own = owns[chunk]
-        last = min(chunk + AHEAD, len(CHUNKS)) - 1
-        if last > chunk:
-            own, sends[last] = lax.optimization_barrier((own, sends[last]))
-        if chunk >= 2:
-            own, arrived[chunk - 2] = lax.optimization_barrier((own, arrived[chunk - 2]))
-        packed, part_stats = join(
-            table, own, jnp.stack(other), resid, head_vec, starts[chunk] // (unit * size), n_dp, n_slots, block
+    count = len(CHUNKS)
+
+    def project(chunk, ctx_rows):
+        owned = ctx_rows.shape[0] // n_tp
+        own, send = out_projection(ctx_rows, wo, owned, starts[chunk], unit * CHUNKS[chunk])
+        own = own.reshape(-1, block, own.shape[-1])
+        return own, send.reshape(n_tp - 1, -1, block, own.shape[-1])
+
+    def exchange(projected):
+        send = projected[1]
+        return jnp.stack([shift(send[k - 1], "tp", n_tp, n_tp - k) for k in range(1, n_tp)])
+
+    def finish(chunk, owns, others):
+        return join(
+            table, owns, others, resid, resid_pair, head_vec, starts[chunk] // (unit * CHUNKS[chunk]),
+            n_dp, n_slots, block,
         )
-        if chunk + AHEAD < len(CHUNKS):
-            packed, ctx_rows = lax.optimization_barrier((packed, ctx_rows))
-            project(ctx_rows)
-        stats.append(part_stats)
-        arrived.append([packed[0]] + [shift(packed[k], "dp", n_dp, k) for k in range(1, n_dp)])
-    arrived[-2], stats[-1] = lax.optimization_barrier((arrived[-2], stats[-1]))
-    whole = place(order, arrived, CHUNKS, width)
+
+    def put(whole, chunk, pieces):
+        return place(order, pieces, whole, starts[chunk] // (unit * CHUNKS[chunk]), width)
+
+    far_rows = spread(far_ctx)
+    near_rows = gathered(near_rows)
+    first = [project(c, near_rows) for c in range(2)]
+    first, near_rows = sync((first, near_rows))
+    near_others = [exchange(p) for p in first]
+    near_projected = first + [project(c, near_rows) for c in range(2, count)]
+    far_rows, near_others, near_projected = sync((far_rows, near_others, near_projected))
+
+    far_rows = gathered(far_rows)
+    first = project(0, far_rows)
+    first, far_rows = sync((first, far_rows))
+    far_others = [exchange(first)]
+    far_projected = [first, project(1, far_rows)]
+    far_others, far_projected, far_rows = sync((far_others, far_projected, far_rows))
+    packed, part = finish(0, [near_projected[0][0], first[0]], [near_others[0], far_others[0]])
+    packed, far_projected, far_rows = sync((packed, far_projected, far_rows))
+
+    stats, whole, pieces = [part], None, None
+    for chunk in range(count):
+        moved = [packed[0]] + [shift(packed[k], "dp", n_dp, k) for k in range(1, n_dp)]
+        if pieces is not None:
+            whole = put(whole, chunk - 1, pieces)
+        ahead = chunk + 1
+        if ahead < count:
+            far_others.append(exchange(far_projected[ahead]))
+            if ahead + 1 < count:
+                near_others.append(exchange(near_projected[ahead + 1]))
+                far_projected.append(project(ahead + 1, far_rows))
+            owns = [near_projected[ahead][0], far_projected[ahead][0]]
+            packed, part = finish(ahead, owns, [near_others[ahead], far_others[ahead]])
+            stats.append(part)
+            moved, packed, whole, far_rows, far_projected, near_others[-1] = sync(
+                (moved, packed, whole, far_rows, far_projected, near_others[-1])
+            )
+        pieces = moved
+    whole = put(whole, count - 1, pieces)
     layer_out = jnp.transpose(whole.reshape(n_slots, local_len, width), (1, 0, 2))[None, None]
 
     stats = sum(v[..., :2] for v in stats)

time: 374 us -> 327 us (0.87)
  waiting for transfers between devices: 149 us -> 95.8 us
  Pallas kernels: 130 us -> 154 us
  local copies, waits for them, and re-layouts: 32.8 us -> 14.4 us
    ppermute x41 -> x43, waiting for transfers between devices: 149 us -> 95.5 us  [shift(): lax.ppermute(value, axis, [(j, (j + step) % size) for j in range(size)])]
    pallas_call x5 -> x10, Pallas kernels: 37.2 us -> 55.6 us  [out_projection(): pl.pallas_call(out_kernel, out_shape=[jax.ShapeDtypeStruct((mine, cols),...]
    unnamed x83 -> x89, local copies, waits for them, and re-layouts: 16.9 us -> 7.07 us
    squeeze x5 -> x0, local copies, waits for them, and re-layouts: 7.26 us -> none  [on_device(): packed[k]]
    pallas_call x1 -> x5, Pallas kernels: 13.5 us -> 19.4 us  [place(): pl.pallas_call(functools.partial(place_kernel, count), out_shape=jax.Shap...]
    ppermute x41 -> x43, starting transfers between devices: 49.8 us -> 47.2 us  [shift(): lax.ppermute(value, axis, [(j, (j + step) % size) for j in range(size)])]
  transfers between devices with their start and end apart: 50 -> 52, of which waited for: 23 -> 20; matrix products, arithmetic and copies ran while one was open for 8% -> 4% of each run, Pallas kernels for 30% -> 42%
where the time goes in v3:
time: 327 us; the launch traced here: 325 us
  Pallas kernels  154 us (47%)
  waiting for transfers between devices  95.8 us (29%)
  starting transfers between devices  51.5 us (16%)
  local copies, waits for them, and re-layouts  14.4 us (4%)
  other arithmetic  8.24 us (3%)
    ppermute x43, waiting for transfers between devices, shift(): lax.ppermute(value, axis, [(j, (j + step) % size) for j in range(size)])  95.5 us
    pallas_call x2, Pallas kernels, attention(): pl.pallas_call(functools.partial(attention_kernel, n_dp, n_tp, len(pieces...  56.8 us
    pallas_call x10, Pallas kernels, out_projection(): pl.pallas_call(out_kernel, out_shape=[jax.ShapeDtypeStruct((mine, cols),...  55.6 us
    ppermute x43, starting transfers between devices, shift(): lax.ppermute(value, axis, [(j, (j + step) % size) for j in range(size)])  47.2 us
    pallas_call x5, Pallas kernels, join(): pl.pallas_call(functools.partial(join_kernel, n_slots, block), out_shape=...  21.8 us
    pallas_call x5, Pallas kernels, place(): pl.pallas_call(functools.partial(place_kernel, count), out_shape=jax.Shap...  19.4 us
    unnamed x89, local copies, waits for them, and re-layouts  7.07 us
  transfers between devices with their start and end apart: 52, of which 20 were waited for; matrix products, arithmetic and copies ran while one was open for 4% of the time, Pallas kernels for 42%

profile of v3, /device:TPU:8, one launch (start us, length us, event | category | flops | bytes accessed | tf_op | source)
XLA Modules:
  0.0 324.7 jit_solution(4942912824235335482)
XLA Ops:
  11.7 12.9 %collective-permute-done.2 = bf16[16,8192]{1,0:T(8,128)(2,1)} collective-permute-done((bf16[16,8192]{1,0:T(8,128)(2,1)S(1)}, bf16[16,8192]{1,0:T(8,128)(2,1)}, u32[]{:S(2)}, u32[]{:S(2)}) %collective-permute-start.2) | collective-permute-done | bytes 262176 | tf_op jit(solution)/shard_map/ppermute | solution.py:30
  24.6 3.9 %collective-permute-done.3 = bf16[16,8192]{1,0:T(8,128)(2,1)} collective-permute-done((bf16[16,8192]{1,0:T(8,128)(2,1)S(1)}, bf16[16,8192]{1,0:T(8,128)(2,1)}, u32[]{:S(2)}, u32[]{:S(2)}) %collective-permute-start.3) | collective-permute-done | bytes 262176 | tf_op jit(solution)/shard_map/ppermute | solution.py:30
  33.4 11.7 %collective-permute-done.5.refs_1_ = bf16[32,8192]{1,0:T(8,128)(2,1)} collective-permute-done((bf16[32,8192]{1,0:T(8,128)(2,1)S(1)}, bf16[32,8192]{1,0:T(8,128)(2,1)}, u32[]{:S(2)}, u32[]{:S(2)}) %collective-permute-start.5) | collective-permute-done | bytes 524320 | tf_op jit(solution)/shard_map/ppermute | solution.py:30
  48.6 28.5 %project_and_attend.2 = bf16[4,2,2,16,2048]{4,3,2,1,0:T(8,128)(2,1)} custom-call(bf16[64,8192]{1,0:T(8,128)(2,1)} %bitcast.115, bf16[64,8192]{1,0:T(8,128)(2,1)} %copy-done.3, bf16[64,8192]{1,0:T(8,128)(2,1)} %copy-done.4, bf16[64,8192]{1,0:T(8,128)(2,1)} %copy-done.5, f32[1,8192]{1,0:T(1,128)} %refs_6_.1, f32[128,128]{1,0:T(8,128)} %copy.46.refs_5_.refs_7_, ...), custom_call_target="tpu_custom_call" | custom-call | flops 1 | bytes 1 | tf_op jit(solution)/shard_map/project_and_attend/pallas_call | solution.py:121
  84.1 28.4 %project_and_attend.3 = bf16[4,2,2,16,2048]{4,3,2,1,0:T(8,128)(2,1)} custom-call(bf16[64,8192]{1,0:T(8,128)(2,1)} %copy-done.2, bf16[32,8192]{1,0:T(8,128)(2,1)} %collective-permute-done.5.refs_1_, bf16[32,8192]{1,0:T(8,128)(2,1)} %collective-permute-done.6.refs_2_, bf16[64,8192]{1,0:T(8,128)(2,1)} %collective-permute-done.9.refs_3_, ...), custom_call_target="tpu_custom_call" | custom-call | flops 1 | bytes 1 | tf_op jit(solution)/shard_map/project_and_attend/pallas_call | solution.py:121
  113.7 4.0 %out_projection.10 = (bf16[128,1024]{1,0:T(8,128)(2,1)}, bf16[128,1024]{1,0:T(8,128)(2,1)}) custom-call(bf16[256,2048]{1,0:T(8,128)(2,1)} %bitcast.107, bf16[1,2048,8192]{2,1,0:T(8,128)(2,1)} %wo_ref.19), custom_call_target="tpu_custom_call" | custom-call | flops 1 | bytes 1 | tf_op jit(solution)/shard_map/out_projection/pallas_call | solution.py:159
  117.7 4.2 %out_projection.11 = (bf16[128,1024]{1,0:T(8,128)(2,1)}, bf16[128,1024]{1,0:T(8,128)(2,1)}) custom-call(bf16[256,2048]{1,0:T(8,128)(2,1)} %bitcast.108, bf16[1,2048,8192]{2,1,0:T(8,128)(2,1)} %wo_ref.19), custom_call_target="tpu_custom_call" | custom-call | flops 1 | bytes 1 | tf_op jit(solution)/shard_map/out_projection/pallas_call | solution.py:159
  124.1 3.1 collective-permute-start.18
  127.4 6.6 %out_projection.12 = (bf16[128,2048]{1,0:T(8,128)(2,1)}, bf16[128,2048]{1,0:T(8,128)(2,1)}) custom-call(bf16[256,2048]{1,0:T(8,128)(2,1)} %bitcast.109, bf16[1,2048,8192]{2,1,0:T(8,128)(2,1)} %wo_ref.19), custom_call_target="tpu_custom_call" | custom-call | flops 1 | bytes 1 | tf_op jit(solution)/shard_map/out_projection/pallas_call | solution.py:159
  134.0 6.5 %out_projection.13 = (bf16[128,2048]{1,0:T(8,128)(2,1)}, bf16[128,2048]{1,0:T(8,128)(2,1)}) custom-call(bf16[256,2048]{1,0:T(8,128)(2,1)} %bitcast.110, bf16[1,2048,8192]{2,1,0:T(8,128)(2,1)} %wo_ref.19), custom_call_target="tpu_custom_call" | custom-call | flops 1 | bytes 1 | tf_op jit(solution)/shard_map/out_projection/pallas_call | solution.py:159
  140.5 6.6 %out_projection.14 = (bf16[128,2048]{1,0:T(8,128)(2,1)}, bf16[128,2048]{1,0:T(8,128)(2,1)}) custom-call(bf16[256,2048]{1,0:T(8,128)(2,1)} %bitcast.111, bf16[1,2048,8192]{2,1,0:T(8,128)(2,1)} %wo_ref.19), custom_call_target="tpu_custom_call" | custom-call | flops 1 | bytes 1 | tf_op jit(solution)/shard_map/out_projection/pallas_call | solution.py:159
  150.5 4.0 %out_projection.15 = (bf16[128,1024]{1,0:T(8,128)(2,1)}, bf16[128,1024]{1,0:T(8,128)(2,1)}) custom-call(bf16[256,2048]{1,0:T(8,128)(2,1)} %bitcast.102, bf16[1,2048,8192]{2,1,0:T(8,128)(2,1)} %wo_ref.19), custom_call_target="tpu_custom_call" | custom-call | flops 1 | bytes 1 | tf_op jit(solution)/shard_map/out_projection/pallas_call | solution.py:159
  158.8 4.0 %out_projection.16 = (bf16[128,1024]{1,0:T(8,128)(2,1)}, bf16[128,1024]{1,0:T(8,128)(2,1)}) custom-call(bf16[256,2048]{1,0:T(8,128)(2,1)} %bitcast.103, bf16[1,2048,8192]{2,1,0:T(8,128)(2,1)} %wo_ref.19), custom_call_target="tpu_custom_call" | custom-call | flops 1 | bytes 1 | tf_op jit(solution)/shard_map/out_projection/pallas_call | solution.py:159
  164.8 3.6 %join_partials.5 = (bf16[6,16,1024]{2,1,0:T(8,128)(2,1)}, bf16[6,16,1024]{2,1,0:T(8,128)(2,1)}, bf16[6,16,1024]{2,1,0:T(8,128)(2,1)}, bf16[6,16,1024]{2,1,0:T(8,128)(2,1)}, f32[4,6,16,128]{3,2,1,0:T(8,128)}) custom-call(s32[5,24]{1,0:T(8,128)} %stack.78.table_ref, bf16[8,16,1024]{2,1,0:T(8,128)(2,1)} %bitcast.133, bf16[8,16,1024]{2,1,0:T(8,128)(2,1)} %bitcast.135, ...), custom_call_target="tpu_custom_call" | custom-call | flops 1 | bytes 1 | tf_op jit(solution)/shard_map/join_partials/pallas_call | solution.py:209
  172.1 6.6 %out_projection.17 = (bf16[128,2048]{1,0:T(8,128)(2,1)}, bf16[128,2048]{1,0:T(8,128)(2,1)}) custom-call(bf16[256,2048]{1,0:T(8,128)(2,1)} %bitcast.104, bf16[1,2048,8192]{2,1,0:T(8,128)(2,1)} %wo_ref.19), custom_call_target="tpu_custom_call" | custom-call | flops 1 | bytes 1 | tf_op jit(solution)/shard_map/out_projection/pallas_call | solution.py:159
  180.3 3.6 %join_partials.6 = (bf16[6,16,1024]{2,1,0:T(8,128)(2,1)}, bf16[6,16,1024]{2,1,0:T(8,128)(2,1)}, bf16[6,16,1024]{2,1,0:T(8,128)(2,1)}, bf16[6,16,1024]{2,1,0:T(8,128)(2,1)}, f32[4,6,16,128]{3,2,1,0:T(8,128)}) custom-call(s32[5,24]{1,0:T(8,128)} %stack.78.table_ref, bf16[8,16,1024]{2,1,0:T(8,128)(2,1)} %bitcast.131, bf16[8,16,1024]{2,1,0:T(8,128)(2,1)} %bitcast.137, ...), custom_call_target="tpu_custom_call" | custom-call | flops 1 | bytes 1 | tf_op jit(solution)/shard_map/join_partials/pallas_call | solution.py:209
  193.1 6.5 %out_projection.18 = (bf16[128,2048]{1,0:T(8,128)(2,1)}, bf16[128,2048]{1,0:T(8,128)(2,1)}) custom-call(bf16[256,2048]{1,0:T(8,128)(2,1)} %bitcast.105, bf16[1,2048,8192]{2,1,0:T(8,128)(2,1)} %wo_ref.19), custom_call_target="tpu_custom_call" | custom-call | flops 1 | bytes 1 | tf_op jit(solution)/shard_map/out_projection/pallas_call | solution.py:159
  199.7 3.6 %place_rows.5.refs_4_ = bf16[6,4,16,8192]{3,2,1,0:T(8,128)(2,1)} custom-call(s32[4]{0:T(128)} %compare_select_fusion.6.order_ref, bf16[6,16,1024]{2,1,0:T(8,128)(2,1)} %get-tuple-element.258.refs_0_, bf16[6,16,1024]{2,1,0:T(8,128)(2,1)} %copy-done.25, bf16[6,16,1024]{2,1,0:T(8,128)(2,1)} %copy-done.26, bf16[6,16,1024]{2,1,0:T(8,128)(2,1)} %copy-done.27), custom_call_target="tpu_custom_call" | custom-call | flops 1 | bytes 1 | tf_op jit(solution)/shard_map/place_rows/pallas_call | solution.py:252
  204.2 4.8 %join_partials.7 = (bf16[6,16,2048]{2,1,0:T(8,128)(2,1)}, bf16[6,16,2048]{2,1,0:T(8,128)(2,1)}, bf16[6,16,2048]{2,1,0:T(8,128)(2,1)}, bf16[6,16,2048]{2,1,0:T(8,128)(2,1)}, f32[4,6,16,128]{3,2,1,0:T(8,128)}) custom-call(s32[5,24]{1,0:T(8,128)} %stack.78.table_ref, bf16[8,16,2048]{2,1,0:T(8,128)(2,1)} %bitcast.121, bf16[8,16,2048]{2,1,0:T(8,128)(2,1)} %bitcast.127, ...), custom_call_target="tpu_custom_call" | custom-call | flops 1 | bytes 1 | tf_op jit(solution)/shard_map/join_partials/pallas_call | solution.py:209
  214.7 6.6 %out_projection.19 = (bf16[128,2048]{1,0:T(8,128)(2,1)}, bf16[128,2048]{1,0:T(8,128)(2,1)}) custom-call(bf16[256,2048]{1,0:T(8,128)(2,1)} %bitcast.106, bf16[1,2048,8192]{2,1,0:T(8,128)(2,1)} %wo_ref.19), custom_call_target="tpu_custom_call" | custom-call | flops 1 | bytes 1 | tf_op jit(solution)/shard_map/out_projection/pallas_call | solution.py:159
  221.3 3.5 %place_rows.6.refs_4_ = bf16[6,4,16,8192]{3,2,1,0:T(8,128)(2,1)} custom-call(s32[4]{0:T(128)} %compare_select_fusion.6.order_ref, bf16[6,16,1024]{2,1,0:T(8,128)(2,1)} %get-tuple-element.278.refs_0_, bf16[6,16,1024]{2,1,0:T(8,128)(2,1)} %copy-done.32, bf16[6,16,1024]{2,1,0:T(8,128)(2,1)} %copy-done.33, ...), custom_call_target="tpu_custom_call", output_to_operand_aliasing={{}: (5, {})} | custom-call | flops 1 | bytes 1 | tf_op jit(solution)/shard_map/place_rows/pallas_call | solution.py:252
  226.3 4.9 %join_partials.8 = (bf16[6,16,2048]{2,1,0:T(8,128)(2,1)}, bf16[6,16,2048]{2,1,0:T(8,128)(2,1)}, bf16[6,16,2048]{2,1,0:T(8,128)(2,1)}, bf16[6,16,2048]{2,1,0:T(8,128)(2,1)}, f32[4,6,16,128]{3,2,1,0:T(8,128)}) custom-call(s32[5,24]{1,0:T(8,128)} %stack.78.table_ref, bf16[8,16,2048]{2,1,0:T(8,128)(2,1)} %bitcast.120, bf16[8,16,2048]{2,1,0:T(8,128)(2,1)} %bitcast.126, ...), custom_call_target="tpu_custom_call" | custom-call | flops 1 | bytes 1 | tf_op jit(solution)/shard_map/join_partials/pallas_call | solution.py:209
  233.9 5.5 %collective-permute-done.33.refs_1_ = bf16[6,16,2048]{2,1,0:T(8,128)(2,1)S(1)} collective-permute-done((bf16[6,16,2048]{2,1,0:T(8,128)(2,1)}, bf16[6,16,2048]{2,1,0:T(8,128)(2,1)S(1)}, u32[]{:S(2)}, u32[]{:S(2)}) %collective-permute-start.33) | collective-permute-done | bytes 393248 | tf_op jit(solution)/shard_map/ppermute | solution.py:30
  239.4 5.3 %collective-permute-done.34.refs_2_ = bf16[6,16,2048]{2,1,0:T(8,128)(2,1)S(1)} collective-permute-done((bf16[6,16,2048]{2,1,0:T(8,128)(2,1)}, bf16[6,16,2048]{2,1,0:T(8,128)(2,1)S(1)}, u32[]{:S(2)}, u32[]{:S(2)}) %collective-permute-start.34) | collective-permute-done | bytes 393248 | tf_op jit(solution)/shard_map/ppermute | solution.py:30
  250.7 4.1 %place_rows.7.refs_4_ = bf16[6,4,16,8192]{3,2,1,0:T(8,128)(2,1)} custom-call(s32[4]{0:T(128)} %compare_select_fusion.6.order_ref, bf16[6,16,2048]{2,1,0:T(8,128)(2,1)} %get-tuple-element.299.refs_0_, bf16[6,16,2048]{2,1,0:T(8,128)(2,1)} %copy-done.18, bf16[6,16,2048]{2,1,0:T(8,128)(2,1)} %copy-done.19, ...), custom_call_target="tpu_custom_call", output_to_operand_aliasing={{}: (5, {})} | custom-call | flops 1 | bytes 1 | tf_op jit(solution)/shard_map/place_rows/pallas_call | solution.py:252
  254.8 4.6 %collective-permute-done.41 = bf16[8,16,2048]{2,1,0:T(8,128)(2,1)S(1)} collective-permute-done((bf16[8,16,2048]{2,1,0:T(8,128)(2,1)S(1)}, bf16[8,16,2048]{2,1,0:T(8,128)(2,1)S(1)}, u32[]{:S(2)}, u32[]{:S(2)}) %collective-permute-start.41) | collective-permute-done | bytes 524320 | tf_op jit(solution)/shard_map/ppermute | solution.py:30
  260.2 4.8 %join_partials.9 = (bf16[6,16,2048]{2,1,0:T(8,128)(2,1)}, bf16[6,16,2048]{2,1,0:T(8,128)(2,1)}, bf16[6,16,2048]{2,1,0:T(8,128)(2,1)}, bf16[6,16,2048]{2,1,0:T(8,128)(2,1)}, f32[4,6,16,128]{3,2,1,0:T(8,128)}) custom-call(s32[5,24]{1,0:T(8,128)} %stack.78.table_ref, bf16[8,16,2048]{2,1,0:T(8,128)(2,1)} %bitcast.119, bf16[8,16,2048]{2,1,0:T(8,128)(2,1)} %bitcast.125, ...), custom_call_target="tpu_custom_call" | custom-call | flops 1 | bytes 1 | tf_op jit(solution)/shard_map/join_partials/pallas_call | solution.py:209
  267.1 13.1 %collective-permute-done.39.refs_2_ = bf16[6,16,2048]{2,1,0:T(8,128)(2,1)S(1)} collective-permute-done((bf16[6,16,2048]{2,1,0:T(8,128)(2,1)}, bf16[6,16,2048]{2,1,0:T(8,128)(2,1)S(1)}, u32[]{:S(2)}, u32[]{:S(2)}) %collective-permute-start.39) | collective-permute-done | bytes 393248 | tf_op jit(solution)/shard_map/ppermute | solution.py:30
  280.3 3.8 %collective-permute-start.42 = (bf16[6,16,2048]{2,1,0:T(8,128)(2,1)}, bf16[6,16,2048]{2,1,0:T(8,128)(2,1)S(1)}, u32[]{:S(2)}, u32[]{:S(2)}) collective-permute-start(bf16[6,16,2048]{2,1,0:T(8,128)(2,1)} %get-tuple-element.305), channel_id=1, source_target_pairs={{0,2},{2,4},{4,6},{6,0},{1,3},{3,5},{5,7},{7,1},{8,10},{10,12},{12... | collective-permute-start | bytes 1179656 | tf_op jit(solution)/shard_map/ppermute | solution.py:30
  288.6 22.4 %collective-permute-done.47 = f32[4,16]{1,0:T(4,128)S(1)} collective-permute-done((f32[4,16]{1,0:T(4,128)S(1)}, f32[4,16]{1,0:T(4,128)S(1)}, u32[]{:S(2)}, u32[]{:S(2)}) %collective-permute-start.47) | collective-permute-done | bytes 288 | tf_op jit(solution)/shard_map/ppermute | solution.py:30
  314.1 4.1 %place_rows.8.refs_4_ = bf16[6,4,16,8192]{3,2,1,0:T(8,128)(2,1)} custom-call(s32[4]{0:T(128)} %compare_select_fusion.6.order_ref, bf16[6,16,2048]{2,1,0:T(8,128)(2,1)} %get-tuple-element.308.refs_0_, bf16[6,16,2048]{2,1,0:T(8,128)(2,1)} %copy-done.12, bf16[6,16,2048]{2,1,0:T(8,128)(2,1)} %copy-done.13, ...), custom_call_target="tpu_custom_call", output_to_operand_aliasing={{}: (5, {})} | custom-call | flops 1 | bytes 1 | tf_op jit(solution)/shard_map/place_rows/pallas_call | solution.py:252
  320.6 4.1 %place_rows.9 = bf16[6,4,16,8192]{3,2,1,0:T(8,128)(2,1)} custom-call(s32[4]{0:T(128)} %compare_select_fusion.6.order_ref, bf16[6,16,2048]{2,1,0:T(8,128)(2,1)} %get-tuple-element.304.refs_0_, bf16[6,16,2048]{2,1,0:T(8,128)(2,1)} %copy-done.15, bf16[6,16,2048]{2,1,0:T(8,128)(2,1)} %copy-done.16, ...), custom_call_target="tpu_custom_call", output_to_operand_aliasing={{}: (5, {})} | custom-call | flops 1 | bytes 1 | tf_op jit(solution)/shard_map/place_rows/pallas_call | solution.py:252
  (236 shorter events, 83.5 us)
Async XLA Ops:
  0.6 29.7 %collective-permute-start = (bf16[64,8192]{1,0:T(8,128)(2,1)}, bf16[64,8192]{1,0:T(8,128)(2,1)S(1)}, u32[]{:S(2)}, u32[]{:S(2)}) collective-permute-start(bf16[64,8192]{1,0:T(8,128)(2,1)} %bitcast.112), channel_id=1, source_target_pairs={{0,1},{1,0},{2,3},{3,2},{4,5},{5,4},{6,7},{7,6},{8,9},{9,8},{10,11... | collective-permute-start | bytes 3145736 | tf_op jit(solution)/shard_map/ppermute | solution.py:30
  2.2 28.1 %collective-permute-start.1 = (bf16[64,8192]{1,0:T(8,128)(2,1)}, bf16[64,8192]{1,0:T(8,128)(2,1)S(1)}, u32[]{:S(2)}, u32[]{:S(2)}) collective-permute-start(bf16[64,8192]{1,0:T(8,128)(2,1)} %bitcast.113), channel_id=1, source_target_pairs={{0,16},{8,24},{16,0},{24,8},{1,17},{9,25},{17,1},{25,9},{2,18},{10... | collective-permute-start | bytes 3145736 | tf_op jit(solution)/shard_map/ppermute | solution.py:23
  6.6 21.9 %collective-permute-start.3 = (bf16[16,8192]{1,0:T(8,128)(2,1)S(1)}, bf16[16,8192]{1,0:T(8,128)(2,1)}, u32[]{:S(2)}, u32[]{:S(2)}) collective-permute-start(bf16[16,8192]{1,0:T(8,128)(2,1)S(1)} %get-tuple-element.334), channel_id=1, source_target_pairs={{0,4},{2,6},{4,0},{6,2},{1,5},{3,7},{5,1},{7,3},{8,12},{10,14},{12... | collective-permute-start | bytes 786440 | tf_op jit(solution)/shard_map/ppermute | solution.py:30
  7.8 22.5 %collective-permute-start.4 = (bf16[16,8192]{1,0:T(8,128)(2,1)S(1)}, bf16[16,8192]{1,0:T(8,128)(2,1)}, u32[]{:S(2)}, u32[]{:S(2)}) collective-permute-start(bf16[16,8192]{1,0:T(8,128)(2,1)S(1)} %get-tuple-element.331), channel_id=1, source_target_pairs={{0,6},{2,0},{4,2},{6,4},{1,7},{3,1},{5,3},{7,5},{8,14},{10,8},{12,... | collective-permute-start | bytes 786440 | tf_op jit(solution)/shard_map/ppermute | solution.py:30
  46.3 30.7 %collective-permute-start.12 = (bf16[4,16,8192]{2,1,0:T(8,128)(2,1)S(1)}, bf16[4,16,8192]{2,1,0:T(8,128)(2,1)}, u32[]{:S(2)}, u32[]{:S(2)}) collective-permute-start(bf16[4,16,8192]{2,1,0:T(8,128)(2,1)S(1)} %pad_maximum_fusion), channel_id=1, source_target_pairs={{0,16},{8,24},{16,0},{24,8},{1,17},{9,25},{17,1},{25,9},{2,18},{10... | collective-permute-start | bytes 3145736 | tf_op jit(solution)/shard_map/ppermute | solution.py:23
  47.3 29.7 %collective-permute-start.9 = (bf16[64,8192]{1,0:T(8,128)(2,1)S(1)}, bf16[64,8192]{1,0:T(8,128)(2,1)}, u32[]{:S(2)}, u32[]{:S(2)}) collective-permute-start(bf16[64,8192]{1,0:T(8,128)(2,1)S(1)} %collective-permute-done.1.refs_0_), channel_id=1, source_target_pairs={{0,8},{8,0},{16,24},{24,16},{1,9},{9,1},{17,25},{25,17},{2,10},{10... | collective-permute-start | bytes 3145736 | tf_op jit(solution)/shard_map/ppermute | solution.py:23
  47.3 29.7 %collective-permute-start.10 = (bf16[32,8192]{1,0:T(8,128)(2,1)}, bf16[32,8192]{1,0:T(8,128)(2,1)}, u32[]{:S(2)}, u32[]{:S(2)}) collective-permute-start(bf16[32,8192]{1,0:T(8,128)(2,1)} %collective-permute-done.5.refs_1_), channel_id=1, source_target_pairs={{0,8},{8,0},{16,24},{24,16},{1,9},{9,1},{17,25},{25,17},{2,10},{10... | collective-permute-start | bytes 1572872 | tf_op jit(solution)/shard_map/ppermute | solution.py:23
  47.8 29.2 %collective-permute-start.11 = (bf16[32,8192]{1,0:T(8,128)(2,1)}, bf16[32,8192]{1,0:T(8,128)(2,1)}, u32[]{:S(2)}, u32[]{:S(2)}) collective-permute-start(bf16[32,8192]{1,0:T(8,128)(2,1)} %collective-permute-done.6.refs_2_), channel_id=1, source_target_pairs={{0,8},{8,0},{16,24},{24,16},{1,9},{9,1},{17,25},{25,17},{2,10},{10... | collective-permute-start | bytes 1572872 | tf_op jit(solution)/shard_map/ppermute | solution.py:23
  78.5 34.1 %collective-permute-start.16 = (bf16[8,16,8192]{2,1,0:T(8,128)(2,1)S(1)}, bf16[8,16,8192]{2,1,0:T(8,128)(2,1)}, u32[]{:S(2)}, u32[]{:S(2)}) collective-permute-start(bf16[8,16,8192]{2,1,0:T(8,128)(2,1)S(1)} %constant_dynamic-update-slice_fusion.resid_ref), channel_id=1, source_target_pairs={{0,8},{8,0},{16,24},{24,16},{1,9},{9,1},{17,25},{25,17},{2,10},{10... | collective-permute-start | bytes 6291464 | tf_op jit(solution)/shard_map/ppermute | solution.py:23
  80.5 32.1 %collective-permute-start.13 = (bf16[2,2,16,2048]{3,2,1,0:T(8,128)(2,1)S(1)}, bf16[2,2,16,2048]{3,2,1,0:T(8,128)(2,1)S(1)}, u32[]{:S(2)}, u32[]{:S(2)}) collective-permute-start(bf16[2,2,16,2048]{3,2,1,0:T(8,128)(2,1)S(1)} %get-tuple-element.329), channel_id=1, source_target_pairs={{0,2},{2,4},{4,6},{6,0},{1,3},{3,5},{5,7},{7,1},{8,10},{10,12},{12... | collective-permute-start | bytes 786440 | tf_op jit(solution)/shard_map/ppermute | solution.py:30
  80.5 32.0 %collective-permute-start.14 = (bf16[2,2,16,2048]{3,2,1,0:T(8,128)(2,1)S(1)}, bf16[2,2,16,2048]{3,2,1,0:T(8,128)(2,1)S(1)}, u32[]{:S(2)}, u32[]{:S(2)}) collective-permute-start(bf16[2,2,16,2048]{3,2,1,0:T(8,128)(2,1)S(1)} %get-tuple-element.328), channel_id=1, source_target_pairs={{0,4},{2,6},{4,0},{6,2},{1,5},{3,7},{5,1},{7,3},{8,12},{10,14},{12... | collective-permute-start | bytes 786440 | tf_op jit(solution)/shard_map/ppermute | solution.py:30
  82.2 30.4 %collective-permute-start.15 = (bf16[2,2,16,2048]{3,2,1,0:T(8,128)(2,1)S(1)}, bf16[2,2,16,2048]{3,2,1,0:T(8,128)(2,1)S(1)}, u32[]{:S(2)}, u32[]{:S(2)}) collective-permute-start(bf16[2,2,16,2048]{3,2,1,0:T(8,128)(2,1)S(1)} %get-tuple-element.327), channel_id=1, source_target_pairs={{0,6},{2,0},{4,2},{6,4},{1,7},{3,1},{5,3},{7,5},{8,14},{10,8},{12,... | collective-permute-start | bytes 786440 | tf_op jit(solution)/shard_map/ppermute | solution.py:30
  121.8 25.3 %collective-permute-start.20 = (bf16[8,16,1024]{2,1,0:T(8,128)(2,1)S(1)}, bf16[8,16,1024]{2,1,0:T(8,128)(2,1)S(1)}, u32[]{:S(2)}, u32[]{:S(2)}) collective-permute-start(bf16[8,16,1024]{2,1,0:T(8,128)(2,1)S(1)} %bitcast.154), channel_id=1, source_target_pairs={{0,1},{1,0},{2,3},{3,2},{4,5},{5,4},{6,7},{7,6},{8,9},{9,8},{10,11... | collective-permute-start | bytes 786440 | tf_op jit(solution)/shard_map/ppermute | solution.py:30
  123.3 23.8 %collective-permute-start.21 = (bf16[8,16,1024]{2,1,0:T(8,128)(2,1)}, bf16[8,16,1024]{2,1,0:T(8,128)(2,1)S(1)}, u32[]{:S(2)}, u32[]{:S(2)}) collective-permute-start(bf16[8,16,1024]{2,1,0:T(8,128)(2,1)} %bitcast.153), channel_id=1, source_target_pairs={{0,1},{1,0},{2,3},{3,2},{4,5},{5,4},{6,7},{7,6},{8,9},{9,8},{10,11... | collective-permute-start | bytes 786440 | tf_op jit(solution)/shard_map/ppermute | solution.py:30
  123.9 23.2 %collective-permute-start.17 = (bf16[2,2,16,2048]{3,2,1,0:T(8,128)(2,1)S(1)}, bf16[2,2,16,2048]{3,2,1,0:T(8,128)(2,1)S(1)}, u32[]{:S(2)}, u32[]{:S(2)}) collective-permute-start(bf16[2,2,16,2048]{3,2,1,0:T(8,128)(2,1)S(1)} %get-tuple-element.325), channel_id=1, source_target_pairs={{0,2},{2,4},{4,6},{6,0},{1,3},{3,5},{5,7},{7,1},{8,10},{10,12},{12... | collective-permute-start | bytes 786440 | tf_op jit(solution)/shard_map/ppermute | solution.py:30
  124.1 23.1 %collective-permute-start.18 = (bf16[2,2,16,2048]{3,2,1,0:T(8,128)(2,1)S(1)}, bf16[2,2,16,2048]{3,2,1,0:T(8,128)(2,1)S(1)}, u32[]{:S(2)}, u32[]{:S(2)}) collective-permute-start(bf16[2,2,16,2048]{3,2,1,0:T(8,128)(2,1)S(1)} %get-tuple-element.324), channel_id=1, source_target_pairs={{0,4},{2,6},{4,0},{6,2},{1,5},{3,7},{5,1},{7,3},{8,12},{10,14},{12... | collective-permute-start | bytes 786440 | tf_op jit(solution)/shard_map/ppermute | solution.py:30
  127.2 22.2 %collective-permute-start.19 = (bf16[2,2,16,2048]{3,2,1,0:T(8,128)(2,1)S(1)}, bf16[2,2,16,2048]{3,2,1,0:T(8,128)(2,1)S(1)}, u32[]{:S(2)}, u32[]{:S(2)}) collective-permute-start(bf16[2,2,16,2048]{3,2,1,0:T(8,128)(2,1)S(1)} %get-tuple-element.323), channel_id=1, source_target_pairs={{0,6},{2,0},{4,2},{6,4},{1,7},{3,1},{5,3},{7,5},{8,14},{10,8},{12,... | collective-permute-start | bytes 786440 | tf_op jit(solution)/shard_map/ppermute | solution.py:30
  156.2 29.9 %collective-permute-start.27 = (bf16[8,16,2048]{2,1,0:T(8,128)(2,1)S(1)}, bf16[8,16,2048]{2,1,0:T(8,128)(2,1)S(1)}, u32[]{:S(2)}, u32[]{:S(2)}) collective-permute-start(bf16[8,16,2048]{2,1,0:T(8,128)(2,1)S(1)} %bitcast.149), channel_id=1, source_target_pairs={{0,1},{1,0},{2,3},{3,2},{4,5},{5,4},{6,7},{7,6},{8,9},{9,8},{10,11... | collective-permute-start | bytes 1572872 | tf_op jit(solution)/shard_map/ppermute | solution.py:30
  186.6 23.9 %collective-permute-start.32 = (bf16[8,16,2048]{2,1,0:T(8,128)(2,1)S(1)}, bf16[8,16,2048]{2,1,0:T(8,128)(2,1)S(1)}, u32[]{:S(2)}, u32[]{:S(2)}) collective-permute-start(bf16[8,16,2048]{2,1,0:T(8,128)(2,1)S(1)} %bitcast.148), channel_id=1, source_target_pairs={{0,1},{1,0},{2,3},{3,2},{4,5},{5,4},{6,7},{7,6},{8,9},{9,8},{10,11... | collective-permute-start | bytes 1572872 | tf_op jit(solution)/shard_map/ppermute | solution.py:30
  188.2 22.4 %collective-permute-start.28 = (bf16[6,16,1024]{2,1,0:T(8,128)(2,1)}, bf16[6,16,1024]{2,1,0:T(8,128)(2,1)S(1)}, u32[]{:S(2)}, u32[]{:S(2)}) collective-permute-start(bf16[6,16,1024]{2,1,0:T(8,128)(2,1)} %get-tuple-element.247), channel_id=1, source_target_pairs={{0,2},{2,4},{4,6},{6,0},{1,3},{3,5},{5,7},{7,1},{8,10},{10,12},{12... | collective-permute-start | bytes 589832 | tf_op jit(solution)/shard_map/ppermute | solution.py:30
  188.2 22.4 %collective-permute-start.29 = (bf16[6,16,1024]{2,1,0:T(8,128)(2,1)}, bf16[6,16,1024]{2,1,0:T(8,128)(2,1)S(1)}, u32[]{:S(2)}, u32[]{:S(2)}) collective-permute-start(bf16[6,16,1024]{2,1,0:T(8,128)(2,1)} %get-tuple-element.248), channel_id=1, source_target_pairs={{0,4},{2,6},{4,0},{6,2},{1,5},{3,7},{5,1},{7,3},{8,12},{10,14},{12... | collective-permute-start | bytes 589832 | tf_op jit(solution)/shard_map/ppermute | solution.py:30
  211.1 22.8 %collective-permute-start.37 = (bf16[8,16,2048]{2,1,0:T(8,128)(2,1)S(1)}, bf16[8,16,2048]{2,1,0:T(8,128)(2,1)S(1)}, u32[]{:S(2)}, u32[]{:S(2)}) collective-permute-start(bf16[8,16,2048]{2,1,0:T(8,128)(2,1)S(1)} %bitcast.147), channel_id=1, source_target_pairs={{0,1},{1,0},{2,3},{3,2},{4,5},{5,4},{6,7},{7,6},{8,9},{9,8},{10,11... | collective-permute-start | bytes 1572872 | tf_op jit(solution)/shard_map/ppermute | solution.py:30
  212.7 26.7 %collective-permute-start.33 = (bf16[6,16,2048]{2,1,0:T(8,128)(2,1)}, bf16[6,16,2048]{2,1,0:T(8,128)(2,1)S(1)}, u32[]{:S(2)}, u32[]{:S(2)}) collective-permute-start(bf16[6,16,2048]{2,1,0:T(8,128)(2,1)} %get-tuple-element.267), channel_id=1, source_target_pairs={{0,2},{2,4},{4,6},{6,0},{1,3},{3,5},{5,7},{7,1},{8,10},{10,12},{12... | collective-permute-start | bytes 1179656 | tf_op jit(solution)/shard_map/ppermute | solution.py:30
  212.7 32.1 %collective-permute-start.34 = (bf16[6,16,2048]{2,1,0:T(8,128)(2,1)}, bf16[6,16,2048]{2,1,0:T(8,128)(2,1)S(1)}, u32[]{:S(2)}, u32[]{:S(2)}) collective-permute-start(bf16[6,16,2048]{2,1,0:T(8,128)(2,1)} %get-tuple-element.268), channel_id=1, source_target_pairs={{0,4},{2,6},{4,0},{6,2},{1,5},{3,7},{5,1},{7,3},{8,12},{10,14},{12... | collective-permute-start | bytes 1179656 | tf_op jit(solution)/shard_map/ppermute | solution.py:30
  213.5 32.0 %collective-permute-start.35 = (bf16[6,16,2048]{2,1,0:T(8,128)(2,1)}, bf16[6,16,2048]{2,1,0:T(8,128)(2,1)S(1)}, u32[]{:S(2)}, u32[]{:S(2)}) collective-permute-start(bf16[6,16,2048]{2,1,0:T(8,128)(2,1)} %get-tuple-element.269), channel_id=1, source_target_pairs={{0,6},{2,0},{4,2},{6,4},{1,7},{3,1},{5,3},{7,5},{8,14},{10,8},{12,... | collective-permute-start | bytes 1179656 | tf_op jit(solution)/shard_map/ppermute | solution.py:30
  246.1 34.1 %collective-permute-start.39 = (bf16[6,16,2048]{2,1,0:T(8,128)(2,1)}, bf16[6,16,2048]{2,1,0:T(8,128)(2,1)S(1)}, u32[]{:S(2)}, u32[]{:S(2)}) collective-permute-start(bf16[6,16,2048]{2,1,0:T(8,128)(2,1)} %get-tuple-element.289), channel_id=1, source_target_pairs={{0,4},{2,6},{4,0},{6,2},{1,5},{3,7},{5,1},{7,3},{8,12},{10,14},{12... | collective-permute-start | bytes 1179656 | tf_op jit(solution)/shard_map/ppermute | solution.py:30
  248.7 31.5 %collective-permute-start.40 = (bf16[6,16,2048]{2,1,0:T(8,128)(2,1)}, bf16[6,16,2048]{2,1,0:T(8,128)(2,1)S(1)}, u32[]{:S(2)}, u32[]{:S(2)}) collective-permute-start(bf16[6,16,2048]{2,1,0:T(8,128)(2,1)} %get-tuple-element.290), channel_id=1, source_target_pairs={{0,6},{2,0},{4,2},{6,4},{1,7},{3,1},{5,3},{7,5},{8,14},{10,8},{12,... | collective-permute-start | bytes 1179656 | tf_op jit(solution)/shard_map/ppermute | solution.py:30
  280.3 38.6 %collective-permute-start.42 = (bf16[6,16,2048]{2,1,0:T(8,128)(2,1)}, bf16[6,16,2048]{2,1,0:T(8,128)(2,1)S(1)}, u32[]{:S(2)}, u32[]{:S(2)}) collective-permute-start(bf16[6,16,2048]{2,1,0:T(8,128)(2,1)} %get-tuple-element.305), channel_id=1, source_target_pairs={{0,2},{2,4},{4,6},{6,0},{1,3},{3,5},{5,7},{7,1},{8,10},{10,12},{12... | collective-permute-start | bytes 1179656 | tf_op jit(solution)/shard_map/ppermute | solution.py:30
  284.2 26.8 %collective-permute-start.47 = (f32[4,16]{1,0:T(4,128)S(1)}, f32[4,16]{1,0:T(4,128)S(1)}, u32[]{:S(2)}, u32[]{:S(2)}) collective-permute-start(f32[4,16]{1,0:T(4,128)S(1)} %fusion.26), channel_id=1, source_target_pairs={{0,4},{2,6},{4,0},{6,2},{1,5},{3,7},{5,1},{7,3},{8,12},{10,14},{12... | collective-permute-start | bytes 776 | tf_op jit(solution)/shard_map/ppermute | solution.py:30
  284.7 26.3 %collective-permute-start.48 = (f32[4,16]{1,0:T(4,128)S(1)}, f32[4,16]{1,0:T(4,128)S(1)}, u32[]{:S(2)}, u32[]{:S(2)}) collective-permute-start(f32[4,16]{1,0:T(4,128)S(1)} %fusion.26), channel_id=1, source_target_pairs={{0,6},{2,0},{4,2},{6,4},{1,7},{3,1},{5,3},{7,5},{8,14},{10,8},{12,... | collective-permute-start | bytes 776 | tf_op jit(solution)/shard_map/ppermute | solution.py:30
  285.7 33.3 %collective-permute-start.43 = (bf16[6,16,2048]{2,1,0:T(8,128)(2,1)}, bf16[6,16,2048]{2,1,0:T(8,128)(2,1)S(1)}, u32[]{:S(2)}, u32[]{:S(2)}) collective-permute-start(bf16[6,16,2048]{2,1,0:T(8,128)(2,1)} %get-tuple-element.306), channel_id=1, source_target_pairs={{0,4},{2,6},{4,0},{6,2},{1,5},{3,7},{5,1},{7,3},{8,12},{10,14},{12... | collective-permute-start | bytes 1179656 | tf_op jit(solution)/shard_map/ppermute | solution.py:30
  287.1 31.9 %collective-permute-start.44 = (bf16[6,16,2048]{2,1,0:T(8,128)(2,1)}, bf16[6,16,2048]{2,1,0:T(8,128)(2,1)S(1)}, u32[]{:S(2)}, u32[]{:S(2)}) collective-permute-start(bf16[6,16,2048]{2,1,0:T(8,128)(2,1)} %get-tuple-element.307), channel_id=1, source_target_pairs={{0,6},{2,0},{4,2},{6,4},{1,7},{3,1},{5,3},{7,5},{8,14},{10,8},{12,... | collective-permute-start | bytes 1179656 | tf_op jit(solution)/shard_map/ppermute | solution.py:30
  (64 other events, 832.9 us)

commit v4 on v3

--- a/solution.py
+++ b/solution.py
@@ -11,7 +11,7 @@
 HD = 128
 NORM_EPS = 1e-05
 ROPE_THETA = 500000.0
-VMEM_BYTES = 56 * 1024 * 1024
+VMEM_BYTES = 40 * 1024 * 1024
 CHUNKS = (1, 1, 2, 2, 2)
 
 
@@ -30,9 +30,15 @@
     return lax.ppermute(value, axis, [(j, (j + step) % size) for j in range(size)])
 
 
-def attention_kernel(n_dp, n_tp, n_pieces, *refs):
+def attention_kernel(n_dp, n_tp, n_pieces, n_done, with_prior, *refs):
     x_refs, refs = refs[:n_pieces], refs[n_pieces:]
-    (gain_ref, cos_ref, sin_ref, mask_ref, wq_ref, wkv_ref, out_ref, normed, acc_q, acc_k, acc_v) = refs
+    gain_ref, cos_ref, sin_ref, mask_ref, wq_ref, wkv_ref = refs[:6]
+    refs = refs[6:]
+    normed, acc_q, acc_k, acc_v = refs[-4:]
+    refs = list(refs[:-4])
+    prior_ref = refs.pop(0) if with_prior else None
+    out_ref = refs.pop(0) if with_prior else None
+    kept_ref = refs.pop(0) if refs else None
     group, step = pl.program_id(0), pl.program_id(1)
     steps, rows, depth = normed.shape
     seq = mask_ref.shape[0]
@@ -75,38 +81,53 @@
 
     @pl.when(step == steps - 1)
     def _():
-        cos, sin = cos_ref[...], sin_ref[...]
-        causal = jnp.concatenate([mask_ref[...]] * (acc_q.shape[1] // acc_k.shape[1]), axis=0) > 0.0
-        block = seq // (n_dp * n_tp)
-        kv_here = acc_k.shape[1] // HD
-        per_kv = acc_q.shape[1] // acc_k.shape[1]
-
-        def rope(v):
-            return (v * cos + pltpu.roll(v, HD // 2, 1) * sin).astype(jnp.bfloat16)
-
-        for s in range(rows // seq):
-            at = slice(s * seq, (s + 1) * seq)
-            for j in range(kv_here):
-                cols = slice(j * HD, (j + 1) * HD)
-                keys = rope(acc_k[at, cols])
-                values = acc_v[at, cols].astype(jnp.bfloat16)
-                heads = range(j * per_kv, (j + 1) * per_kv)
-                queries = jnp.concatenate([rope(acc_q[at, h * HD : (h + 1) * HD]) for h in heads], axis=0)
-                scores = lax.dot_general(
-                    queries, keys, (((1,), (1,)), ((), ())), preferred_element_type=jnp.float32
-                ) * (1.0 / math.sqrt(HD))
-                scores = jnp.where(causal, scores, -1e30)
-                expo = jnp.exp(scores - jnp.max(scores, axis=-1, keepdims=True))
-                weights = (expo / jnp.sum(expo, axis=-1, keepdims=True)).astype(jnp.bfloat16)
-                context = jnp.dot(weights, values, preferred_element_type=jnp.float32).astype(jnp.bfloat16)
-                for n, h in enumerate(heads):
-                    for t in range(n_tp):
-                        for z in range(n_dp):
-                            start = n * seq + (t * n_dp + z) * block
-                            out_ref[z, t, s, :, h * HD : (h + 1) * HD] = context[start : start + block]
-
-
-def attention(pieces, gain, cos, sin, mask, wq, wkv, n_dp, n_tp):
+        local = seq // n_tp
+        q_width, kv_width = acc_q.shape[1], acc_k.shape[1]
+        per_kv = q_width // kv_width
+
+        def rope(v, first):
+            at = slice(first, first + v.shape[0])
+            return (v * cos_ref[at] + pltpu.roll(v, HD // 2, 1) * sin_ref[at]).astype(jnp.bfloat16)
+
+        if kept_ref is not None:
+            for start in range(n_done, rows, local):
+                at, to = slice(start, start + local), slice(start - n_done, start - n_done + local)
+                for c in range(0, q_width, HD):
+                    kept_ref[to, c : c + HD] = rope(acc_q[at, c : c + HD], 0)
+                for c in range(0, kv_width, HD):
+                    kept_ref[to, q_width + c : q_width + c + HD] = rope(acc_k[at, c : c + HD], 0)
+                kept_ref[to, q_width + kv_width :] = acc_v[at].astype(jnp.bfloat16)
+
+        if out_ref is not None:
+            causal = jnp.concatenate([mask_ref[...]] * per_kv, axis=0) > 0.0
+            block = seq // (n_dp * n_tp)
+            more = seq - local
+            for s in range(n_done // more):
+                old, new = slice(s * local, (s + 1) * local), slice(s * more, (s + 1) * more)
+                for j in range(kv_width // HD):
+                    cols = slice(j * HD, (j + 1) * HD)
+                    joined = lambda first, last: jnp.concatenate([first, last], axis=0)
+                    kept = lambda start: prior_ref[old, start : start + HD]
+                    keys = joined(kept(q_width + j * HD), rope(acc_k[new, cols], local))
+                    values = joined(kept(q_width + kv_width + j * HD), acc_v[new, cols].astype(jnp.bfloat16))
+                    heads = range(j * per_kv, (j + 1) * per_kv)
+                    queries = [joined(kept(h * HD), rope(acc_q[new, h * HD : (h + 1) * HD], local)) for h in heads]
+                    queries = jnp.concatenate(queries, axis=0)
+                    scores = lax.dot_general(
+                        queries, keys, (((1,), (1,)), ((), ())), preferred_element_type=jnp.float32
+                    ) * (1.0 / math.sqrt(HD))
+                    scores = jnp.where(causal, scores, -1e30)
+                    expo = jnp.exp(scores - jnp.max(scores, axis=-1, keepdims=True))
+                    weights = (expo / jnp.sum(expo, axis=-1, keepdims=True)).astype(jnp.bfloat16)
+                    context = jnp.dot(weights, values, preferred_element_type=jnp.float32).astype(jnp.bfloat16)
+                    for n, h in enumerate(heads):
+                        for t in range(n_tp):
+                            for z in range(n_dp):
+                                start = n * seq + (t * n_dp + z) * block
+                                out_ref[z, t, s, :, h * HD : (h + 1) * HD] = context[start : start + block]
+
+
+def attention(pieces, prior, n_done, gain, cos, sin, mask, wq, wkv, n_dp, n_tp):
     rows, width = sum(p.shape[0] for p in pieces), pieces[0].shape[1]
     seq = mask.shape[0]
     q_width, kv_width = wq.shape[2], wkv.shape[3]
@@ -115,23 +136,34 @@
     q_block = q_width // groups
     steps = 2
     depth = width // steps
-    samples = rows // seq
+    samples = n_done // (seq - seq // n_tp)
     block = seq // (n_dp * n_tp)
+    packed = q_block + 2 * kv_block
     fixed = lambda g, k: (0, 0)
+    in_specs = [pl.BlockSpec(p.shape, fixed, pipeline_mode=pl.Buffered(1)) for p in pieces] + [
+        pl.BlockSpec((1, width), fixed),
+        pl.BlockSpec((seq, HD), fixed),
+        pl.BlockSpec((seq, HD), fixed),
+        pl.BlockSpec((seq, seq), fixed),
+        pl.BlockSpec((None, depth, q_block), lambda g, k: (0, k, g)),
+        pl.BlockSpec((None, 2, depth, kv_block), lambda g, k: (0, 0, k, g)),
+    ]
+    operands = [*pieces, gain, cos, sin, mask, wq, wkv]
+    out_shape, out_specs = [], []
+    if prior is not None:
+        operands.append(prior)
+        in_specs.append(pl.BlockSpec((None, prior.shape[1], packed), lambda g, k: (g, 0, 0)))
+        out_shape.append(jax.ShapeDtypeStruct((n_dp, n_tp, samples, block, q_width), jnp.bfloat16))
+        out_specs.append(pl.BlockSpec((n_dp, n_tp, samples, block, q_block), lambda g, k: (0, 0, 0, 0, g)))
+    if n_done < rows:
+        out_shape.append(jax.ShapeDtypeStruct((groups, rows - n_done, packed), jnp.bfloat16))
+        out_specs.append(pl.BlockSpec((None, rows - n_done, packed), lambda g, k: (g, 0, 0)))
     return pl.pallas_call(
-        functools.partial(attention_kernel, n_dp, n_tp, len(pieces)),
-        out_shape=jax.ShapeDtypeStruct((n_dp, n_tp, samples, block, q_width), jnp.bfloat16),
+        functools.partial(attention_kernel, n_dp, n_tp, len(pieces), n_done, prior is not None),
+        out_shape=out_shape,
         grid=(groups, steps),
-        in_specs=[pl.BlockSpec(p.shape, fixed) for p in pieces]
-        + [
-            pl.BlockSpec((1, width), fixed),
-            pl.BlockSpec((seq, HD), fixed),
-            pl.BlockSpec((seq, HD), fixed),
-            pl.BlockSpec((seq, seq), fixed),
-            pl.BlockSpec((None, depth, q_block), lambda g, k: (0, k, g)),
-            pl.BlockSpec((None, 2, depth, kv_block), lambda g, k: (0, 0, k, g)),
-        ],
-        out_specs=pl.BlockSpec((n_dp, n_tp, samples, block, q_block), lambda g, k: (0, 0, 0, 0, g)),
+        in_specs=in_specs,
+        out_specs=out_specs,
         scratch_shapes=[
             pltpu.VMEM((steps, rows, depth), jnp.bfloat16),
             pltpu.VMEM((rows, q_block), jnp.float32),
@@ -141,7 +173,7 @@
         compiler_params=params(),
         cost_estimate=pl.CostEstimate(flops=1, bytes_accessed=1, transcendentals=0),
         name="project_and_attend",
-    )(*pieces, gain, cos, sin, mask, wq, wkv)
+    )(*operands)
 
 
 def out_kernel(ctx_ref, wo_ref, own_ref, send_ref):
@@ -284,49 +316,58 @@
     sin = jnp.concatenate([-jnp.sin(angles), jnp.sin(angles)], axis=1)
     mask = (positions[:, None] >= positions[None, :]).astype(jnp.float32)
 
+    attend = lambda pieces, prior, n_done: attention(
+        pieces, prior, n_done, norm_gain, cos, sin, mask, wq, wkv, n_dp, n_tp
+    )
+
+    def spread(ctx, steps):
+        here = lambda k: lax.dynamic_index_in_dim(ctx, my_dp ^ k, 0, keepdims=False)
+        return [swap(here(k), "dp", n_dp, k) if k else here(k) for k in steps]
+
+    def gathered(parts):
+        return jnp.stack(parts, axis=1).reshape(-1, wq.shape[2])
+
     mine = responses[0]
-    quarter = lambda k: lax.dynamic_slice_in_dim(mine, lax.rem(my_dp + k, n_dp) * block, block, 0)
-    resid = [quarter(0)] + [shift(quarter(k), "dp", n_dp, k) for k in range(1, n_dp)]
-    near = [mine] + [shift(mine, "tp", n_tp, k) for k in range(1, n_tp)]
+    near = [shift(mine, "tp", n_tp, k) for k in range(1, n_tp)]
     far_mine = swap(mine, "sec", n_sec, 2)
-    near, far_mine, resid, cos, sin, mask = sync((near, far_mine, resid, cos, sin, mask))
+    mine_pair = swap(mine, "sec", n_sec, 1)
+    mine, mine_pair, cos, sin, mask = sync((mine, mine_pair, cos, sin, mask))
+    quarter = lambda k: lax.dynamic_slice_in_dim(mine, (my_dp ^ k) * block, block, 0)
+    resid = [quarter(0)] + [swap(quarter(k), "dp", n_dp, k) for k in range(1, n_dp)]
+    (kept,) = attend([mine, mine_pair], None, 0)
+    near, far_mine, resid, kept = sync((near, far_mine, resid, kept))
 
     half = local_len // 2
-    far = [far_mine]
+    far = []
     for k in range(1, n_tp):
-        parts = [shift(far_mine[:half], "tp", n_tp, k), swap(near[k][half:], "sec", n_sec, 2)]
+        parts = [shift(far_mine[:half], "tp", n_tp, k), swap(near[k - 1][half:], "sec", n_sec, 2)]
         far += parts if half % 16 == 0 else [jnp.concatenate(parts, axis=0)]
     near_pair = [swap(v, "sec", n_sec, 1) for v in near]
+    far_mine_pair = swap(far_mine, "sec", n_sec, 1)
+    near, near_pair, far_mine, far_mine_pair, kept, resid = sync(
+        (near, near_pair, far_mine, far_mine_pair, kept, resid)
+    )
+
+    more = 2 * (seq - local_len)
     resid = jnp.stack(resid)
-    far, near, near_pair, resid = sync((far, near, near_pair, resid))
-
-    attend = lambda pieces: attention(pieces, norm_gain, cos, sin, mask, wq, wkv, n_dp, n_tp)
-
-    def spread(ctx):
-        here = lambda k: lax.dynamic_index_in_dim(ctx, lax.rem(my_dp + k, n_dp), 0, keepdims=False)
-        return [here(0)] + [shift(here(k), "dp", n_dp, k) for k in range(1, n_dp)]
-
-    def gathered(parts):
-        return jnp.stack(parts, axis=1).reshape(-1, wq.shape[2])
-
-    near_ctx = attend(near + near_pair)
+    resid_far = swap(resid, "sec", n_sec, 2)
+    near_ctx, kept = attend(near + near_pair + [far_mine, far_mine_pair], kept, more)
+    near_ctx, kept, far, resid, resid_far = sync((near_ctx, kept, far, resid, resid_far))
+
+    near_rows = spread(near_ctx, range(n_dp))
     far_pair = [swap(v, "sec", n_sec, 1) for v in far]
-    resid_far = swap(resid, "sec", n_sec, 2)
-    near_ctx, far, far_pair, resid, resid_far = sync((near_ctx, far, far_pair, resid, resid_far))
-    near_rows = spread(near_ctx)
-    resid = jnp.concatenate([resid, resid_far], axis=0)
-    resid_pair = swap(resid, "sec", n_sec, 1)
-    far_ctx = attend(far + far_pair)
-    near_rows, far_ctx, resid, resid_pair = sync((near_rows, far_ctx, resid, resid_pair))
+    far, far_pair, kept = sync((far, far_pair, kept))
+    (far_ctx,) = attend(far + far_pair, kept, more)
+    near_rows, far_ctx, resid, resid_far = sync((near_rows, far_ctx, resid, resid_far))
 
     row_dp = lax.dynamic_index_in_dim(dest_dp, my_sec, 0, keepdims=False)
     row_slot = lax.dynamic_index_in_dim(dest_slot, my_sec, 0, keepdims=False)
     sample = jnp.arange(samples)
     i_rel = my_sec ^ (sample // n_dp)
-    k_rel = lax.rem(my_dp - sample % n_dp + n_dp, n_dp)
+    k_rel = my_dp ^ (sample % n_dp)
     part_at = k_rel * 2 + i_rel % 2
     resid_at = (i_rel // 2) * n_dp + k_rel
-    dests = lax.rem(my_dp + jnp.arange(n_dp), n_dp)
+    dests = my_dp ^ jnp.arange(n_dp)
     chosen = (row_dp[None, None, :] == dests[:, None, None]) & (
         row_slot[None, None, :] == jnp.arange(n_slots)[None, :, None]
     )
@@ -334,7 +375,7 @@
     live = jnp.clip(lengths - first_pos, 0, block)
     pick = lambda v: jnp.sum(jnp.where(chosen, v[None, None, :], 0), axis=-1).reshape(-1)
     table = jnp.stack([pick(part_at), pick(resid_at), pick(live), pick(i_rel % 2), pick(i_rel // 2)]).astype(jnp.int32)
-    order = lax.rem(my_dp - jnp.arange(n_dp) + n_dp, n_dp).astype(jnp.int32)
+    order = dests.astype(jnp.int32)
 
     unit = width // sum(CHUNKS)
     starts = [unit * sum(CHUNKS[:c]) for c in range(len(CHUNKS))]
@@ -359,13 +400,22 @@
     def put(whole, chunk, pieces):
         return place(order, pieces, whole, starts[chunk] // (unit * CHUNKS[chunk]), width)
 
-    far_rows = spread(far_ctx)
+    far_across = spread(far_ctx, range(n_dp // 2, n_dp // 2 + 1))
     near_rows = gathered(near_rows)
-    first = [project(c, near_rows) for c in range(2)]
-    first, near_rows = sync((first, near_rows))
-    near_others = [exchange(p) for p in first]
-    near_projected = first + [project(c, near_rows) for c in range(2, count)]
-    far_rows, near_others, near_projected = sync((far_rows, near_others, near_projected))
+    near_projected = [project(c, near_rows) for c in range(2)]
+    resid = jnp.concatenate([resid, resid_far], axis=0)
+    far_across, near_projected, near_rows, far_ctx, resid = sync(
+        (far_across, near_projected, near_rows, far_ctx, resid)
+    )
+    others = [k for k in range(n_dp) if k != n_dp // 2]
+    far_rows = spread(far_ctx, others)
+    far_rows.insert(n_dp // 2, far_across[0])
+    near_others = [exchange(p) for p in near_projected]
+    resid_pair = swap(resid, "sec", n_sec, 1)
+    near_projected += [project(c, near_rows) for c in range(2, count - 1)]
+    far_rows, near_others, near_projected, near_rows, resid_pair = sync(
+        (far_rows, near_others, near_projected, near_rows, resid_pair)
+    )
 
     far_rows = gathered(far_rows)
     first = project(0, far_rows)
@@ -378,15 +428,20 @@
 
     stats, whole, pieces = [part], None, None
     for chunk in range(count):
-        moved = [packed[0]] + [shift(packed[k], "dp", n_dp, k) for k in range(1, n_dp)]
+        moved = [packed[0]] + [swap(packed[k], "dp", n_dp, k) for k in range(1, n_dp)]
         if pieces is not None:
             whole = put(whole, chunk - 1, pieces)
         ahead = chunk + 1
         if ahead < count:
             far_others.append(exchange(far_projected[ahead]))
+            if len(near_others) == ahead:
+                near_others.append(exchange(near_projected[ahead]))
+            elif ahead + 1 < count - 1:
+                near_others.append(exchange(near_projected[ahead + 1]))
             if ahead + 1 < count:
-                near_others.append(exchange(near_projected[ahead + 1]))
                 far_projected.append(project(ahead + 1, far_rows))
+                if ahead + 1 == count - 1:
+                    near_projected.append(project(ahead + 1, near_rows))
             owns = [near_projected[ahead][0], far_projected[ahead][0]]
             packed, part = finish(ahead, owns, [near_others[ahead], far_others[ahead]])
             stats.append(part)

time: 327 us -> 312 us (0.954)
  Pallas kernels: 154 us -> 141 us
  local copies, waits for them, and re-layouts: 14.4 us -> 18.1 us
  other arithmetic: 8.24 us -> 4.73 us
  waiting for transfers between devices: 95.8 us -> 92.5 us
    ppermute x43 -> x19, waiting for transfers between devices: 95.5 us -> 22 us  [shift(): lax.ppermute(value, axis, [(j, (j + step) % size) for j in range(size)])]
    ppermute x9 -> x33, waiting for transfers between devices: 0.25 us -> 70.5 us  [swap(): return lax.ppermute(value, axis, [(j, j ^ step) for j in range(size)])]
    ppermute x9 -> x33, starting transfers between devices: 4.22 us -> 38.2 us  [swap(): return lax.ppermute(value, axis, [(j, j ^ step) for j in range(size)])]
    ppermute x43 -> x19, starting transfers between devices: 47.2 us -> 14.6 us  [shift(): lax.ppermute(value, axis, [(j, (j + step) % size) for j in range(size)])]
    pallas_call x2 -> x3, Pallas kernels: 56.8 us -> 66 us  [attention(): pl.pallas_call(functools.partial(attention_kernel, n_dp, n_tp, len(pieces...]
    pallas_call x10, Pallas kernels: 55.6 us -> 47.4 us  [out_projection(): pl.pallas_call(out_kernel, out_shape=[jax.ShapeDtypeStruct((mine, cols),...]
    pallas_call x5, Pallas kernels: 19.4 us -> 12.2 us  [place(): pl.pallas_call(functools.partial(place_kernel, count), out_shape=jax.Shap...]
    pallas_call x5, Pallas kernels: 21.8 us -> 15.6 us  [join(): pl.pallas_call(functools.partial(join_kernel, n_slots, block), out_shape=...]
  transfers between devices with their start and end apart: 52 -> 52, of which waited for: 20 -> 20; matrix products, arithmetic and copies ran while one was open for 4% -> 3% of each run, Pallas kernels for 42% -> 43%
where the time goes in v4:
time: 312 us; the launch traced here: 311 us
  Pallas kernels  141 us (45%)
  waiting for transfers between devices  92.5 us (30%)
  starting transfers between devices  52.9 us (17%)
  local copies, waits for them, and re-layouts  18.1 us (6%)
  other arithmetic  4.73 us (2%)
    ppermute x33, waiting for transfers between devices, swap(): return lax.ppermute(value, axis, [(j, j ^ step) for j in range(size)])  70.5 us
    pallas_call x3, Pallas kernels, attention(): pl.pallas_call(functools.partial(attention_kernel, n_dp, n_tp, len(pieces...  66 us
    pallas_call x10, Pallas kernels, out_projection(): pl.pallas_call(out_kernel, out_shape=[jax.ShapeDtypeStruct((mine, cols),...  47.4 us
    ppermute x33, starting transfers between devices, swap(): return lax.ppermute(value, axis, [(j, j ^ step) for j in range(size)])  38.2 us
    ppermute x19, waiting for transfers between devices, shift(): lax.ppermute(value, axis, [(j, (j + step) % size) for j in range(size)])  22 us
    pallas_call x5, Pallas kernels, join(): pl.pallas_call(functools.partial(join_kernel, n_slots, block), out_shape=...  15.6 us
    ppermute x19, starting transfers between devices, shift(): lax.ppermute(value, axis, [(j, (j + step) % size) for j in range(size)])  14.6 us
    pallas_call x5, Pallas kernels, place(): pl.pallas_call(functools.partial(place_kernel, count), out_shape=jax.Shap...  12.2 us
  transfers between devices with their start and end apart: 52, of which 20 were waited for; matrix products, arithmetic and copies ran while one was open for 3% of the time, Pallas kernels for 43%

profile of v4, /device:TPU:8, one launch (start us, length us, event | category | flops | bytes accessed | tf_op | source)
XLA Modules:
  0.0 310.7 jit_solution(17072247570239770082)
XLA Ops:
  12.3 19.0 %project_and_attend.3.refs_10_ = bf16[2,128,1536]{2,1,0:T(8,128)(2,1)S(1)} custom-call(bf16[64,8192]{1,0:T(8,128)(2,1)S(1)} %bitcast.106, bf16[64,8192]{1,0:T(8,128)(2,1)S(1)} %collective-permute-done.2.refs_1_, f32[1,8192]{1,0:T(1,128)S(1)} %copy-done.12, f32[128,128]{1,0:T(8,128)S(1)} %copy.49.refs_3_.refs_5_, ...), custom_call_target="tpu_custom_call" | custom-call | flops 1 | bytes 1 | tf_op jit(solution)/shard_map/project_and_attend/pallas_call | solution.py:161
  41.7 26.6 %project_and_attend.4 = (bf16[4,2,2,16,2048]{4,3,2,1,0:T(8,128)(2,1)S(1)}, bf16[2,128,1536]{2,1,0:T(8,128)(2,1)S(1)}) custom-call(bf16[64,8192]{1,0:T(8,128)(2,1)S(1)} %collective-permute-done.refs_0_, bf16[64,8192]{1,0:T(8,128)(2,1)S(1)} %collective-permute-done.6.refs_1_, bf16[64,8192]{1,0:T(8,128)(2,1)S(1)} %collective-permute-done.1.refs_2_, ...), custom_call_target="tpu_custom_call" | custom-call | flops 1 | bytes 1 | tf_op jit(solution)/shard_map/project_and_attend/pallas_call | solution.py:161
  69.1 6.2 %collective-permute-done.9.refs_1_ = bf16[32,8192]{1,0:T(8,128)(2,1)} collective-permute-done((bf16[32,8192]{1,0:T(8,128)(2,1)S(1)}, bf16[32,8192]{1,0:T(8,128)(2,1)}, u32[]{:S(2)}, u32[]{:S(2)}) %collective-permute-start.9) | collective-permute-done | bytes 524320 | tf_op jit(solution)/shard_map/ppermute | solution.py:23
  77.0 3.0 collective-permute-start.12
  81.6 20.5 %project_and_attend.5 = bf16[4,2,2,16,2048]{4,3,2,1,0:T(8,128)(2,1)S(1)} custom-call(bf16[32,8192]{1,0:T(8,128)(2,1)} %collective-permute-done.8.refs_0_, bf16[32,8192]{1,0:T(8,128)(2,1)} %collective-permute-done.9.refs_1_, bf16[32,8192]{1,0:T(8,128)(2,1)S(1)} %collective-permute-done.14.refs_2_, bf16[32,8192]{1,0:T(8,128)(2,1)S(1)} %collective-permute-done.15.refs_3_, ...), custom_call_target="tpu_custom_call" | custom-call | flops 1 | bytes 1 | tf_op jit(solution)/shard_map/project_and_attend/pallas_call | solution.py:161
  105.1 3.1 out_projection.10
  108.9 3.2 %out_projection.11 = (bf16[128,1024]{1,0:T(8,128)(2,1)S(1)}, bf16[128,1024]{1,0:T(8,128)(2,1)S(1)}) custom-call(bf16[256,2048]{1,0:T(8,128)(2,1)S(1)} %bitcast.93, bf16[1,2048,8192]{2,1,0:T(8,128)(2,1)} %wo_ref.19), custom_call_target="tpu_custom_call" | custom-call | flops 1 | bytes 1 | tf_op jit(solution)/shard_map/out_projection/pallas_call | solution.py:191
  112.2 3.2 %collective-permute-done.16 = bf16[2,2,16,2048]{3,2,1,0:T(8,128)(2,1)S(1)} collective-permute-done((bf16[2,2,16,2048]{3,2,1,0:T(8,128)(2,1)S(1)}, bf16[2,2,16,2048]{3,2,1,0:T(8,128)(2,1)S(1)}, u32[]{:S(2)}, u32[]{:S(2)}) %collective-permute-start.16) | collective-permute-done | bytes 262176 | tf_op jit(solution)/shard_map/ppermute | solution.py:23
  124.2 6.2 %out_projection.12 = (bf16[128,2048]{1,0:T(8,128)(2,1)S(1)}, bf16[128,2048]{1,0:T(8,128)(2,1)}) custom-call(bf16[256,2048]{1,0:T(8,128)(2,1)S(1)} %bitcast.94, bf16[1,2048,8192]{2,1,0:T(8,128)(2,1)} %wo_ref.19), custom_call_target="tpu_custom_call" | custom-call | flops 1 | bytes 1 | tf_op jit(solution)/shard_map/out_projection/pallas_call | solution.py:191
  131.2 5.6 %out_projection.13 = (bf16[128,2048]{1,0:T(8,128)(2,1)S(1)}, bf16[128,2048]{1,0:T(8,128)(2,1)S(1)}) custom-call(bf16[256,2048]{1,0:T(8,128)(2,1)S(1)} %bitcast.95, bf16[1,2048,8192]{2,1,0:T(8,128)(2,1)} %wo_ref.19), custom_call_target="tpu_custom_call" | custom-call | flops 1 | bytes 1 | tf_op jit(solution)/shard_map/out_projection/pallas_call | solution.py:191
  139.6 4.1 %out_projection.14 = (bf16[128,1024]{1,0:T(8,128)(2,1)S(1)}, bf16[128,1024]{1,0:T(8,128)(2,1)}) custom-call(bf16[256,2048]{1,0:T(8,128)(2,1)S(1)} %bitcast.97, bf16[1,2048,8192]{2,1,0:T(8,128)(2,1)} %wo_ref.19), custom_call_target="tpu_custom_call" | custom-call | flops 1 | bytes 1 | tf_op jit(solution)/shard_map/out_projection/pallas_call | solution.py:191
  149.2 3.2 %out_projection.15 = (bf16[128,1024]{1,0:T(8,128)(2,1)S(1)}, bf16[128,1024]{1,0:T(8,128)(2,1)S(1)}) custom-call(bf16[256,2048]{1,0:T(8,128)(2,1)S(1)} %bitcast.98, bf16[1,2048,8192]{2,1,0:T(8,128)(2,1)} %wo_ref.19), custom_call_target="tpu_custom_call" | custom-call | flops 1 | bytes 1 | tf_op jit(solution)/shard_map/out_projection/pallas_call | solution.py:191
  160.7 5.5 %out_projection.16 = (bf16[128,2048]{1,0:T(8,128)(2,1)S(1)}, bf16[128,2048]{1,0:T(8,128)(2,1)S(1)}) custom-call(bf16[256,2048]{1,0:T(8,128)(2,1)S(1)} %bitcast.99, bf16[1,2048,8192]{2,1,0:T(8,128)(2,1)} %wo_ref.19), custom_call_target="tpu_custom_call" | custom-call | flops 1 | bytes 1 | tf_op jit(solution)/shard_map/out_projection/pallas_call | solution.py:191
  171.6 3.3 %collective-permute-done.25.refs_3_ = bf16[6,16,1024]{2,1,0:T(8,128)(2,1)S(1)} collective-permute-done((bf16[6,16,1024]{2,1,0:T(8,128)(2,1)S(1)}, bf16[6,16,1024]{2,1,0:T(8,128)(2,1)S(1)}, u32[]{:S(2)}, u32[]{:S(2)}) %collective-permute-start.25) | collective-permute-done | bytes 196640 | tf_op jit(solution)/shard_map/ppermute | solution.py:23
  180.4 5.5 %out_projection.17 = (bf16[128,2048]{1,0:T(8,128)(2,1)S(1)}, bf16[128,2048]{1,0:T(8,128)(2,1)S(1)}) custom-call(bf16[256,2048]{1,0:T(8,128)(2,1)S(1)} %bitcast.100, bf16[1,2048,8192]{2,1,0:T(8,128)(2,1)} %wo_ref.19), custom_call_target="tpu_custom_call" | custom-call | flops 1 | bytes 1 | tf_op jit(solution)/shard_map/out_projection/pallas_call | solution.py:191
  189.7 3.3 %join_partials.7 = (bf16[6,16,2048]{2,1,0:T(8,128)(2,1)S(1)}, bf16[6,16,2048]{2,1,0:T(8,128)(2,1)S(1)}, bf16[6,16,2048]{2,1,0:T(8,128)(2,1)S(1)}, bf16[6,16,2048]{2,1,0:T(8,128)(2,1)S(1)}, f32[4,6,16,128]{3,2,1,0:T(8,128)S(1)}) custom-call(s32[5,24]{1,0:T(8,128)S(1)} %stack.78.table_ref, bf16[8,16,2048]{2,1,0:T(8,128)(2,1)S(1)} %bitcast.108, ...), custom_call_target="tpu_custom_call" | custom-call | flops 1 | bytes 1 | tf_op jit(solution)/shard_map/join_partials/pallas_call | solution.py:241
  193.0 5.4 %collective-permute-done.32 = bf16[8,16,2048]{2,1,0:T(8,128)(2,1)S(1)} collective-permute-done((bf16[8,16,2048]{2,1,0:T(8,128)(2,1)S(1)}, bf16[8,16,2048]{2,1,0:T(8,128)(2,1)S(1)}, u32[]{:S(2)}, u32[]{:S(2)}) %collective-permute-start.32) | collective-permute-done | bytes 524320 | tf_op jit(solution)/shard_map/ppermute | solution.py:30
  203.5 5.5 %out_projection.19 = (bf16[128,2048]{1,0:T(8,128)(2,1)S(1)}, bf16[128,2048]{1,0:T(8,128)(2,1)S(1)}) custom-call(bf16[256,2048]{1,0:T(8,128)(2,1)S(1)} %bitcast.96, bf16[1,2048,8192]{2,1,0:T(8,128)(2,1)} %wo_ref.19), custom_call_target="tpu_custom_call" | custom-call | flops 1 | bytes 1 | tf_op jit(solution)/shard_map/out_projection/pallas_call | solution.py:191
  209.6 5.5 %out_projection.18 = (bf16[128,2048]{1,0:T(8,128)(2,1)S(1)}, bf16[128,2048]{1,0:T(8,128)(2,1)S(1)}) custom-call(bf16[256,2048]{1,0:T(8,128)(2,1)S(1)} %bitcast.101, bf16[1,2048,8192]{2,1,0:T(8,128)(2,1)} %wo_ref.19), custom_call_target="tpu_custom_call" | custom-call | flops 1 | bytes 1 | tf_op jit(solution)/shard_map/out_projection/pallas_call | solution.py:191
  217.2 4.0 %join_partials.8 = (bf16[6,16,2048]{2,1,0:T(8,128)(2,1)S(1)}, bf16[6,16,2048]{2,1,0:T(8,128)(2,1)}, bf16[6,16,2048]{2,1,0:T(8,128)(2,1)}, bf16[6,16,2048]{2,1,0:T(8,128)(2,1)}, f32[4,6,16,128]{3,2,1,0:T(8,128)S(1)}) custom-call(s32[5,24]{1,0:T(8,128)S(1)} %stack.78.table_ref, bf16[8,16,2048]{2,1,0:T(8,128)(2,1)S(1)} %bitcast.107, ...), custom_call_target="tpu_custom_call" | custom-call | flops 1 | bytes 1 | tf_op jit(solution)/shard_map/join_partials/pallas_call | solution.py:241
  221.1 6.2 %collective-permute-done.34.refs_2_ = bf16[6,16,2048]{2,1,0:T(8,128)(2,1)S(1)} collective-permute-done((bf16[6,16,2048]{2,1,0:T(8,128)(2,1)S(1)}, bf16[6,16,2048]{2,1,0:T(8,128)(2,1)S(1)}, u32[]{:S(2)}, u32[]{:S(2)}) %collective-permute-start.34) | collective-permute-done | bytes 393248 | tf_op jit(solution)/shard_map/ppermute | solution.py:23
  227.3 7.6 %collective-permute-done.35.refs_3_ = bf16[6,16,2048]{2,1,0:T(8,128)(2,1)S(1)} collective-permute-done((bf16[6,16,2048]{2,1,0:T(8,128)(2,1)S(1)}, bf16[6,16,2048]{2,1,0:T(8,128)(2,1)S(1)}, u32[]{:S(2)}, u32[]{:S(2)}) %collective-permute-start.35) | collective-permute-done | bytes 393248 | tf_op jit(solution)/shard_map/ppermute | solution.py:23
  241.1 5.5 %collective-permute-done.41 = bf16[8,16,2048]{2,1,0:T(8,128)(2,1)S(1)} collective-permute-done((bf16[8,16,2048]{2,1,0:T(8,128)(2,1)S(1)}, bf16[8,16,2048]{2,1,0:T(8,128)(2,1)S(1)}, u32[]{:S(2)}, u32[]{:S(2)}) %collective-permute-start.41) | collective-permute-done | bytes 524320 | tf_op jit(solution)/shard_map/ppermute | solution.py:30
  246.6 3.2 %join_partials.9 = (bf16[6,16,2048]{2,1,0:T(8,128)(2,1)S(1)}, bf16[6,16,2048]{2,1,0:T(8,128)(2,1)S(1)}, bf16[6,16,2048]{2,1,0:T(8,128)(2,1)S(1)}, bf16[6,16,2048]{2,1,0:T(8,128)(2,1)S(1)}, f32[4,6,16,128]{3,2,1,0:T(8,128)S(1)}) custom-call(s32[5,24]{1,0:T(8,128)S(1)} %stack.78.table_ref, bf16[8,16,2048]{2,1,0:T(8,128)(2,1)S(1)} %bitcast.110, ...), custom_call_target="tpu_custom_call" | custom-call | flops 1 | bytes 1 | tf_op jit(solution)/shard_map/join_partials/pallas_call | solution.py:241
  251.9 11.3 %collective-permute-done.38.refs_2_ = bf16[6,16,2048]{2,1,0:T(8,128)(2,1)} collective-permute-done((bf16[6,16,2048]{2,1,0:T(8,128)(2,1)}, bf16[6,16,2048]{2,1,0:T(8,128)(2,1)}, u32[]{:S(2)}, u32[]{:S(2)}) %collective-permute-start.38) | collective-permute-done | bytes 393248 | tf_op jit(solution)/shard_map/ppermute | solution.py:23
  263.1 7.7 %collective-permute-done.39.refs_3_ = bf16[6,16,2048]{2,1,0:T(8,128)(2,1)} collective-permute-done((bf16[6,16,2048]{2,1,0:T(8,128)(2,1)}, bf16[6,16,2048]{2,1,0:T(8,128)(2,1)}, u32[]{:S(2)}, u32[]{:S(2)}) %collective-permute-start.39) | collective-permute-done | bytes 393248 | tf_op jit(solution)/shard_map/ppermute | solution.py:23
  273.0 2.9 collective-permute-start.43
  276.0 2.9 collective-permute-start.44
  278.8 3.6 %collective-permute-done.47 = f32[4,16]{1,0:T(4,128)S(1)} collective-permute-done((f32[4,16]{1,0:T(4,128)S(1)}, f32[4,16]{1,0:T(4,128)S(1)}, u32[]{:S(2)}, u32[]{:S(2)}) %collective-permute-start.47) | collective-permute-done | bytes 288 | tf_op jit(solution)/shard_map/ppermute | solution.py:30
  285.6 3.7 %place_rows.8.refs_4_ = bf16[6,4,16,8192]{3,2,1,0:T(8,128)(2,1)} custom-call(s32[4]{0:T(128)S(1)} %iota_xor_fusion.order_ref, bf16[6,16,2048]{2,1,0:T(8,128)(2,1)S(1)} %get-tuple-element.326.refs_0_, bf16[6,16,2048]{2,1,0:T(8,128)(2,1)S(1)} %collective-permute-done.37.refs_1_, ...), custom_call_target="tpu_custom_call", output_to_operand_aliasing={{}: (5, {})} | custom-call | flops 1 | bytes 1 | tf_op jit(solution)/shard_map/place_rows/pallas_call | solution.py:284
  290.1 11.1 %collective-permute-done.43.refs_2_ = bf16[6,16,2048]{2,1,0:T(8,128)(2,1)S(1)} collective-permute-done((bf16[6,16,2048]{2,1,0:T(8,128)(2,1)}, bf16[6,16,2048]{2,1,0:T(8,128)(2,1)S(1)}, u32[]{:S(2)}, u32[]{:S(2)}) %collective-permute-start.43) | collective-permute-done | bytes 393248 | tf_op jit(solution)/shard_map/ppermute | solution.py:23
  301.2 7.3 %collective-permute-done.44.refs_3_ = bf16[6,16,2048]{2,1,0:T(8,128)(2,1)S(1)} collective-permute-done((bf16[6,16,2048]{2,1,0:T(8,128)(2,1)}, bf16[6,16,2048]{2,1,0:T(8,128)(2,1)S(1)}, u32[]{:S(2)}, u32[]{:S(2)}) %collective-permute-start.44) | collective-permute-done | bytes 393248 | tf_op jit(solution)/shard_map/ppermute | solution.py:23
  (220 shorter events, 94.8 us)
Async XLA Ops:
  0.7 30.6 %collective-permute-start = (bf16[64,8192]{1,0:T(8,128)(2,1)}, bf16[64,8192]{1,0:T(8,128)(2,1)S(1)}, u32[]{:S(2)}, u32[]{:S(2)}) collective-permute-start(bf16[64,8192]{1,0:T(8,128)(2,1)} %bitcast.103), channel_id=1, source_target_pairs={{0,1},{1,0},{2,3},{3,2},{4,5},{5,4},{6,7},{7,6},{8,9},{9,8},{10,11... | collective-permute-start | bytes 3145736 | tf_op jit(solution)/shard_map/ppermute | solution.py:30
  2.3 29.0 %collective-permute-start.1 = (bf16[64,8192]{1,0:T(8,128)(2,1)}, bf16[64,8192]{1,0:T(8,128)(2,1)S(1)}, u32[]{:S(2)}, u32[]{:S(2)}) collective-permute-start(bf16[64,8192]{1,0:T(8,128)(2,1)} %bitcast.104), channel_id=1, source_target_pairs={{0,16},{8,24},{16,0},{24,8},{1,17},{9,25},{17,1},{25,9},{2,18},{10... | collective-permute-start | bytes 3145736 | tf_op jit(solution)/shard_map/ppermute | solution.py:23
  6.8 24.6 %collective-permute-start.3 = (bf16[16,8192]{1,0:T(8,128)(2,1)}, bf16[16,8192]{1,0:T(8,128)(2,1)}, u32[]{:S(2)}, u32[]{:S(2)}) collective-permute-start(bf16[16,8192]{1,0:T(8,128)(2,1)} %get-tuple-element.350), channel_id=1, source_target_pairs={{0,2},{2,0},{4,6},{6,4},{1,3},{3,1},{5,7},{7,5},{8,10},{10,8},{12,... | collective-permute-start | bytes 786440 | tf_op jit(solution)/shard_map/ppermute | solution.py:23
  7.2 24.1 %collective-permute-start.4 = (bf16[16,8192]{1,0:T(8,128)(2,1)}, bf16[16,8192]{1,0:T(8,128)(2,1)}, u32[]{:S(2)}, u32[]{:S(2)}) collective-permute-start(bf16[16,8192]{1,0:T(8,128)(2,1)} %get-tuple-element.349), channel_id=1, source_target_pairs={{0,4},{2,6},{4,0},{6,2},{1,5},{3,7},{5,1},{7,3},{8,12},{10,14},{12... | collective-permute-start | bytes 786440 | tf_op jit(solution)/shard_map/ppermute | solution.py:23
  9.8 23.5 %collective-permute-start.5 = (bf16[16,8192]{1,0:T(8,128)(2,1)}, bf16[16,8192]{1,0:T(8,128)(2,1)}, u32[]{:S(2)}, u32[]{:S(2)}) collective-permute-start(bf16[16,8192]{1,0:T(8,128)(2,1)} %get-tuple-element.348), channel_id=1, source_target_pairs={{0,6},{2,4},{4,2},{6,0},{1,7},{3,5},{5,3},{7,1},{8,14},{10,12},{12... | collective-permute-start | bytes 786440 | tf_op jit(solution)/shard_map/ppermute | solution.py:23
  38.7 36.6 %collective-permute-start.10 = (bf16[4,16,8192]{2,1,0:T(8,128)(2,1)S(1)}, bf16[4,16,8192]{2,1,0:T(8,128)(2,1)S(1)}, u32[]{:S(2)}, u32[]{:S(2)}) collective-permute-start(bf16[4,16,8192]{2,1,0:T(8,128)(2,1)S(1)} %pad_maximum_fusion.1), channel_id=1, source_target_pairs={{0,16},{8,24},{16,0},{24,8},{1,17},{9,25},{17,1},{25,9},{2,18},{10... | collective-permute-start | bytes 3145736 | tf_op jit(solution)/shard_map/ppermute | solution.py:23
  39.5 29.6 %collective-permute-start.8 = (bf16[32,8192]{1,0:T(8,128)(2,1)S(1)}, bf16[32,8192]{1,0:T(8,128)(2,1)}, u32[]{:S(2)}, u32[]{:S(2)}) collective-permute-start(bf16[32,8192]{1,0:T(8,128)(2,1)S(1)} %slice.33), channel_id=1, source_target_pairs={{0,1},{1,0},{2,3},{3,2},{4,5},{5,4},{6,7},{7,6},{8,9},{9,8},{10,11... | collective-permute-start | bytes 1572872 | tf_op jit(solution)/shard_map/ppermute | solution.py:30
  41.1 34.2 %collective-permute-start.9 = (bf16[32,8192]{1,0:T(8,128)(2,1)S(1)}, bf16[32,8192]{1,0:T(8,128)(2,1)}, u32[]{:S(2)}, u32[]{:S(2)}) collective-permute-start(bf16[32,8192]{1,0:T(8,128)(2,1)S(1)} %slice.34), channel_id=1, source_target_pairs={{0,16},{8,24},{16,0},{24,8},{1,17},{9,25},{17,1},{25,9},{2,18},{10... | collective-permute-start | bytes 1572872 | tf_op jit(solution)/shard_map/ppermute | solution.py:23
  76.9 25.2 %collective-permute-start.11 = (bf16[2,2,16,2048]{3,2,1,0:T(8,128)(2,1)S(1)}, bf16[2,2,16,2048]{3,2,1,0:T(8,128)(2,1)S(1)}, u32[]{:S(2)}, u32[]{:S(2)}) collective-permute-start(bf16[2,2,16,2048]{3,2,1,0:T(8,128)(2,1)S(1)} %get-tuple-element.346), channel_id=1, source_target_pairs={{0,2},{2,0},{4,6},{6,4},{1,3},{3,1},{5,7},{7,5},{8,10},{10,8},{12,... | collective-permute-start | bytes 786440 | tf_op jit(solution)/shard_map/ppermute | solution.py:23
  77.0 25.2 %collective-permute-start.12 = (bf16[2,2,16,2048]{3,2,1,0:T(8,128)(2,1)S(1)}, bf16[2,2,16,2048]{3,2,1,0:T(8,128)(2,1)S(1)}, u32[]{:S(2)}, u32[]{:S(2)}) collective-permute-start(bf16[2,2,16,2048]{3,2,1,0:T(8,128)(2,1)S(1)} %get-tuple-element.345), channel_id=1, source_target_pairs={{0,4},{2,6},{4,0},{6,2},{1,5},{3,7},{5,1},{7,3},{8,12},{10,14},{12... | collective-permute-start | bytes 786440 | tf_op jit(solution)/shard_map/ppermute | solution.py:23
  80.0 23.3 %collective-permute-start.13 = (bf16[2,2,16,2048]{3,2,1,0:T(8,128)(2,1)S(1)}, bf16[2,2,16,2048]{3,2,1,0:T(8,128)(2,1)S(1)}, u32[]{:S(2)}, u32[]{:S(2)}) collective-permute-start(bf16[2,2,16,2048]{3,2,1,0:T(8,128)(2,1)S(1)} %get-tuple-element.344), channel_id=1, source_target_pairs={{0,6},{2,4},{4,2},{6,0},{1,7},{3,5},{5,3},{7,1},{8,14},{10,12},{12... | collective-permute-start | bytes 786440 | tf_op jit(solution)/shard_map/ppermute | solution.py:23
  116.0 22.4 %collective-permute-start.21 = (bf16[8,16,8192]{2,1,0:T(8,128)(2,1)S(1)}, bf16[8,16,8192]{2,1,0:T(8,128)(2,1)}, u32[]{:S(2)}, u32[]{:S(2)}) collective-permute-start(bf16[8,16,8192]{2,1,0:T(8,128)(2,1)S(1)} %pad_maximum_fusion.resid_ref), channel_id=1, source_target_pairs={{0,8},{8,0},{16,24},{24,16},{1,9},{9,1},{17,25},{25,17},{2,10},{10... | collective-permute-start | bytes 6291464 | tf_op jit(solution)/shard_map/ppermute | solution.py:23
  118.1 20.2 %collective-permute-start.17 = (bf16[2,2,16,2048]{3,2,1,0:T(8,128)(2,1)}, bf16[2,2,16,2048]{3,2,1,0:T(8,128)(2,1)}, u32[]{:S(2)}, u32[]{:S(2)}) collective-permute-start(bf16[2,2,16,2048]{3,2,1,0:T(8,128)(2,1)} %get-tuple-element.342), channel_id=1, source_target_pairs={{0,2},{2,0},{4,6},{6,4},{1,3},{3,1},{5,7},{7,5},{8,10},{10,8},{12,... | collective-permute-start | bytes 786440 | tf_op jit(solution)/shard_map/ppermute | solution.py:23
  120.2 18.1 %collective-permute-start.18 = (bf16[2,2,16,2048]{3,2,1,0:T(8,128)(2,1)}, bf16[2,2,16,2048]{3,2,1,0:T(8,128)(2,1)}, u32[]{:S(2)}, u32[]{:S(2)}) collective-permute-start(bf16[2,2,16,2048]{3,2,1,0:T(8,128)(2,1)} %get-tuple-element.341), channel_id=1, source_target_pairs={{0,6},{2,4},{4,2},{6,0},{1,7},{3,5},{5,3},{7,1},{8,14},{10,12},{12... | collective-permute-start | bytes 786440 | tf_op jit(solution)/shard_map/ppermute | solution.py:23
  122.1 16.3 %collective-permute-start.19 = (bf16[8,16,1024]{2,1,0:T(8,128)(2,1)}, bf16[8,16,1024]{2,1,0:T(8,128)(2,1)}, u32[]{:S(2)}, u32[]{:S(2)}) collective-permute-start(bf16[8,16,1024]{2,1,0:T(8,128)(2,1)} %bitcast.129), channel_id=1, source_target_pairs={{0,1},{1,0},{2,3},{3,2},{4,5},{5,4},{6,7},{7,6},{8,9},{9,8},{10,11... | collective-permute-start | bytes 786440 | tf_op jit(solution)/shard_map/ppermute | solution.py:30
  144.9 30.0 %collective-permute-start.27 = (bf16[8,16,2048]{2,1,0:T(8,128)(2,1)}, bf16[8,16,2048]{2,1,0:T(8,128)(2,1)}, u32[]{:S(2)}, u32[]{:S(2)}) collective-permute-start(bf16[8,16,2048]{2,1,0:T(8,128)(2,1)} %bitcast.48), channel_id=1, source_target_pairs={{0,1},{1,0},{2,3},{3,2},{4,5},{5,4},{6,7},{7,6},{8,9},{9,8},{10,11... | collective-permute-start | bytes 1572872 | tf_op jit(solution)/shard_map/ppermute | solution.py:30
  176.4 22.0 %collective-permute-start.32 = (bf16[8,16,2048]{2,1,0:T(8,128)(2,1)S(1)}, bf16[8,16,2048]{2,1,0:T(8,128)(2,1)S(1)}, u32[]{:S(2)}, u32[]{:S(2)}) collective-permute-start(bf16[8,16,2048]{2,1,0:T(8,128)(2,1)S(1)} %bitcast.123), channel_id=1, source_target_pairs={{0,1},{1,0},{2,3},{3,2},{4,5},{5,4},{6,7},{7,6},{8,9},{9,8},{10,11... | collective-permute-start | bytes 1572872 | tf_op jit(solution)/shard_map/ppermute | solution.py:30
  176.9 21.5 %collective-permute-start.28 = (bf16[6,16,1024]{2,1,0:T(8,128)(2,1)S(1)}, bf16[6,16,1024]{2,1,0:T(8,128)(2,1)S(1)}, u32[]{:S(2)}, u32[]{:S(2)}) collective-permute-start(bf16[6,16,1024]{2,1,0:T(8,128)(2,1)S(1)} %get-tuple-element.265), channel_id=1, source_target_pairs={{0,2},{2,0},{4,6},{6,4},{1,3},{3,1},{5,7},{7,5},{8,10},{10,8},{12,... | collective-permute-start | bytes 589832 | tf_op jit(solution)/shard_map/ppermute | solution.py:23
  176.9 21.5 %collective-permute-start.29 = (bf16[6,16,1024]{2,1,0:T(8,128)(2,1)S(1)}, bf16[6,16,1024]{2,1,0:T(8,128)(2,1)S(1)}, u32[]{:S(2)}, u32[]{:S(2)}) collective-permute-start(bf16[6,16,1024]{2,1,0:T(8,128)(2,1)S(1)} %get-tuple-element.266), channel_id=1, source_target_pairs={{0,4},{2,6},{4,0},{6,2},{1,5},{3,7},{5,1},{7,3},{8,12},{10,14},{12... | collective-permute-start | bytes 589832 | tf_op jit(solution)/shard_map/ppermute | solution.py:23
  178.8 19.6 %collective-permute-start.30 = (bf16[6,16,1024]{2,1,0:T(8,128)(2,1)S(1)}, bf16[6,16,1024]{2,1,0:T(8,128)(2,1)S(1)}, u32[]{:S(2)}, u32[]{:S(2)}) collective-permute-start(bf16[6,16,1024]{2,1,0:T(8,128)(2,1)S(1)} %get-tuple-element.267), channel_id=1, source_target_pairs={{0,6},{2,4},{4,2},{6,0},{1,7},{3,5},{5,3},{7,1},{8,14},{10,12},{12... | collective-permute-start | bytes 589832 | tf_op jit(solution)/shard_map/ppermute | solution.py:23
  198.4 18.8 %collective-permute-start.36 = (bf16[8,16,2048]{2,1,0:T(8,128)(2,1)S(1)}, bf16[8,16,2048]{2,1,0:T(8,128)(2,1)S(1)}, u32[]{:S(2)}, u32[]{:S(2)}) collective-permute-start(bf16[8,16,2048]{2,1,0:T(8,128)(2,1)S(1)} %bitcast.124), channel_id=1, source_target_pairs={{0,1},{1,0},{2,3},{3,2},{4,5},{5,4},{6,7},{7,6},{8,9},{9,8},{10,11... | collective-permute-start | bytes 1572872 | tf_op jit(solution)/shard_map/ppermute | solution.py:30
  200.0 21.1 %collective-permute-start.33 = (bf16[6,16,2048]{2,1,0:T(8,128)(2,1)S(1)}, bf16[6,16,2048]{2,1,0:T(8,128)(2,1)S(1)}, u32[]{:S(2)}, u32[]{:S(2)}) collective-permute-start(bf16[6,16,2048]{2,1,0:T(8,128)(2,1)S(1)} %get-tuple-element.285), channel_id=1, source_target_pairs={{0,2},{2,0},{4,6},{6,4},{1,3},{3,1},{5,7},{7,5},{8,10},{10,8},{12,... | collective-permute-start | bytes 1179656 | tf_op jit(solution)/shard_map/ppermute | solution.py:23
  200.1 27.3 %collective-permute-start.34 = (bf16[6,16,2048]{2,1,0:T(8,128)(2,1)S(1)}, bf16[6,16,2048]{2,1,0:T(8,128)(2,1)S(1)}, u32[]{:S(2)}, u32[]{:S(2)}) collective-permute-start(bf16[6,16,2048]{2,1,0:T(8,128)(2,1)S(1)} %get-tuple-element.286), channel_id=1, source_target_pairs={{0,4},{2,6},{4,0},{6,2},{1,5},{3,7},{5,1},{7,3},{8,12},{10,14},{12... | collective-permute-start | bytes 1179656 | tf_op jit(solution)/shard_map/ppermute | solution.py:23
  201.5 33.5 %collective-permute-start.35 = (bf16[6,16,2048]{2,1,0:T(8,128)(2,1)S(1)}, bf16[6,16,2048]{2,1,0:T(8,128)(2,1)S(1)}, u32[]{:S(2)}, u32[]{:S(2)}) collective-permute-start(bf16[6,16,2048]{2,1,0:T(8,128)(2,1)S(1)} %get-tuple-element.287), channel_id=1, source_target_pairs={{0,6},{2,4},{4,2},{6,0},{1,7},{3,5},{5,3},{7,1},{8,14},{10,12},{12... | collective-permute-start | bytes 1179656 | tf_op jit(solution)/shard_map/ppermute | solution.py:23
  209.1 32.0 %collective-permute-start.40 = (bf16[8,16,2048]{2,1,0:T(8,128)(2,1)S(1)}, bf16[8,16,2048]{2,1,0:T(8,128)(2,1)S(1)}, u32[]{:S(2)}, u32[]{:S(2)}) collective-permute-start(bf16[8,16,2048]{2,1,0:T(8,128)(2,1)S(1)} %bitcast.125), channel_id=1, source_target_pairs={{0,1},{1,0},{2,3},{3,2},{4,5},{5,4},{6,7},{7,6},{8,9},{9,8},{10,11... | collective-permute-start | bytes 1572872 | tf_op jit(solution)/shard_map/ppermute | solution.py:30
  235.3 16.6 %collective-permute-start.37 = (bf16[6,16,2048]{2,1,0:T(8,128)(2,1)}, bf16[6,16,2048]{2,1,0:T(8,128)(2,1)S(1)}, u32[]{:S(2)}, u32[]{:S(2)}) collective-permute-start(bf16[6,16,2048]{2,1,0:T(8,128)(2,1)} %get-tuple-element.305), channel_id=1, source_target_pairs={{0,2},{2,0},{4,6},{6,4},{1,3},{3,1},{5,7},{7,5},{8,10},{10,8},{12,... | collective-permute-start | bytes 1179656 | tf_op jit(solution)/shard_map/ppermute | solution.py:23
  235.4 27.7 %collective-permute-start.38 = (bf16[6,16,2048]{2,1,0:T(8,128)(2,1)}, bf16[6,16,2048]{2,1,0:T(8,128)(2,1)}, u32[]{:S(2)}, u32[]{:S(2)}) collective-permute-start(bf16[6,16,2048]{2,1,0:T(8,128)(2,1)} %get-tuple-element.306), channel_id=1, source_target_pairs={{0,4},{2,6},{4,0},{6,2},{1,5},{3,7},{5,1},{7,3},{8,12},{10,14},{12... | collective-permute-start | bytes 1179656 | tf_op jit(solution)/shard_map/ppermute | solution.py:23
  236.4 34.5 %collective-permute-start.39 = (bf16[6,16,2048]{2,1,0:T(8,128)(2,1)}, bf16[6,16,2048]{2,1,0:T(8,128)(2,1)}, u32[]{:S(2)}, u32[]{:S(2)}) collective-permute-start(bf16[6,16,2048]{2,1,0:T(8,128)(2,1)} %get-tuple-element.307), channel_id=1, source_target_pairs={{0,6},{2,4},{4,2},{6,0},{1,7},{3,5},{5,3},{7,1},{8,14},{10,12},{12... | collective-permute-start | bytes 1179656 | tf_op jit(solution)/shard_map/ppermute | solution.py:23
  251.4 19.5 %collective-permute-start.45 = (f32[4,16]{1,0:T(4,128)S(1)}, f32[4,16]{1,0:T(4,128)S(1)}, u32[]{:S(2)}, u32[]{:S(2)}) collective-permute-start(f32[4,16]{1,0:T(4,128)S(1)} %broadcast_select_fusion), channel_id=1, source_target_pairs={{0,1},{1,0},{2,3},{3,2},{4,5},{5,4},{6,7},{7,6},{8,9},{9,8},{10,11... | collective-permute-start | bytes 776 | tf_op jit(solution)/shard_map/ppermute | solution.py:30
  271.0 19.1 %collective-permute-start.42 = (bf16[6,16,2048]{2,1,0:T(8,128)(2,1)}, bf16[6,16,2048]{2,1,0:T(8,128)(2,1)S(1)}, u32[]{:S(2)}, u32[]{:S(2)}) collective-permute-start(bf16[6,16,2048]{2,1,0:T(8,128)(2,1)} %copy-done.22), channel_id=1, source_target_pairs={{0,2},{2,0},{4,6},{6,4},{1,3},{3,1},{5,7},{7,5},{8,10},{10,8},{12,... | collective-permute-start | bytes 1179656 | tf_op jit(solution)/shard_map/ppermute | solution.py:23
  273.0 28.1 %collective-permute-start.43 = (bf16[6,16,2048]{2,1,0:T(8,128)(2,1)}, bf16[6,16,2048]{2,1,0:T(8,128)(2,1)S(1)}, u32[]{:S(2)}, u32[]{:S(2)}) collective-permute-start(bf16[6,16,2048]{2,1,0:T(8,128)(2,1)} %copy-done.21), channel_id=1, source_target_pairs={{0,4},{2,6},{4,0},{6,2},{1,5},{3,7},{5,1},{7,3},{8,12},{10,14},{12... | collective-permute-start | bytes 1179656 | tf_op jit(solution)/shard_map/ppermute | solution.py:23
  276.0 32.5 %collective-permute-start.44 = (bf16[6,16,2048]{2,1,0:T(8,128)(2,1)}, bf16[6,16,2048]{2,1,0:T(8,128)(2,1)S(1)}, u32[]{:S(2)}, u32[]{:S(2)}) collective-permute-start(bf16[6,16,2048]{2,1,0:T(8,128)(2,1)} %copy-done.20), channel_id=1, source_target_pairs={{0,6},{2,4},{4,2},{6,0},{1,7},{3,5},{5,3},{7,1},{8,14},{10,12},{12... | collective-permute-start | bytes 1179656 | tf_op jit(solution)/shard_map/ppermute | solution.py:23
  (56 other events, 429.1 us)

commit v5 on v4

--- a/solution.py
+++ b/solution.py
@@ -13,6 +13,7 @@
 ROPE_THETA = 500000.0
 VMEM_BYTES = 40 * 1024 * 1024
 CHUNKS = (1, 1, 2, 2, 2)
+SPLIT = 3
 
 
 def params():
@@ -234,7 +235,8 @@
 
 
 def join(table, owns, others, resid, resid_pair, head, chunk, n_dp, n_slots, block):
-    cols = owns[0].shape[-1]
+    cols = owns[0][0].shape[-1]
+    blocks = resid.shape[0]
     slots = n_slots // 2
     fixed = lambda i, t: (0, 0, 0)
     here = lambda i, t: (0, 0, chunk)
@@ -246,10 +248,8 @@
             num_scalar_prefetch=1,
             grid=(n_slots // slots,),
             in_specs=[
-                pl.BlockSpec(owns[0].shape, fixed),
-                pl.BlockSpec(owns[1].shape, fixed),
-                pl.BlockSpec(others[0].shape, lambda i, t: (0, 0, 0, 0)),
-                pl.BlockSpec(others[1].shape, lambda i, t: (0, 0, 0, 0)),
+                *[pl.BlockSpec((blocks, block, cols), lambda i, t, at=at: (at, 0, 0)) for _, at in owns],
+                *[pl.BlockSpec((v.shape[0], blocks, block, cols), lambda i, t, at=at: (0, at, 0, 0)) for v, at in others],
                 pl.BlockSpec((resid.shape[0], block, cols), here),
                 pl.BlockSpec((resid.shape[0], block, cols), here),
                 pl.BlockSpec((1, cols), lambda i, t: (0, chunk)),
@@ -260,7 +260,7 @@
         compiler_params=params(),
         cost_estimate=pl.CostEstimate(flops=1, bytes_accessed=1, transcendentals=0),
         name="join_partials",
-    )(table, *owns, *others, resid, resid_pair, head)
+    )(table, *[v for v, _ in owns], *[v for v, _ in others], resid, resid_pair, head)
     return list(out[:-1]), out[-1]
 
 
@@ -320,9 +320,11 @@
         pieces, prior, n_done, norm_gain, cos, sin, mask, wq, wkv, n_dp, n_tp
     )
 
-    def spread(ctx, steps):
-        here = lambda k: lax.dynamic_index_in_dim(ctx, my_dp ^ k, 0, keepdims=False)
-        return [swap(here(k), "dp", n_dp, k) if k else here(k) for k in steps]
+    def by_step(ctx):
+        return [lax.dynamic_index_in_dim(ctx, my_dp ^ k, 0, keepdims=False) for k in range(n_dp)]
+
+    def spread(parts):
+        return [parts[0]] + [swap(parts[k], "dp", n_dp, k) for k in range(1, n_dp)]
 
     def gathered(parts):
         return jnp.stack(parts, axis=1).reshape(-1, wq.shape[2])
@@ -344,21 +346,22 @@
         far += parts if half % 16 == 0 else [jnp.concatenate(parts, axis=0)]
     near_pair = [swap(v, "sec", n_sec, 1) for v in near]
     far_mine_pair = swap(far_mine, "sec", n_sec, 1)
+    resid = jnp.stack(resid)
     near, near_pair, far_mine, far_mine_pair, kept, resid = sync(
         (near, near_pair, far_mine, far_mine_pair, kept, resid)
     )
 
     more = 2 * (seq - local_len)
-    resid = jnp.stack(resid)
+    near_ctx, kept = attend(near + near_pair + [far_mine, far_mine_pair], kept, more)
+    near_ctx, kept, far = sync((near_ctx, kept, far))
+
+    near_rows = spread(by_step(near_ctx))
+    far_pair = [swap(v, "sec", n_sec, 1) for v in far]
+    far, far_pair, kept, resid = sync((far, far_pair, kept, resid))
     resid_far = swap(resid, "sec", n_sec, 2)
-    near_ctx, kept = attend(near + near_pair + [far_mine, far_mine_pair], kept, more)
-    near_ctx, kept, far, resid, resid_far = sync((near_ctx, kept, far, resid, resid_far))
-
-    near_rows = spread(near_ctx, range(n_dp))
-    far_pair = [swap(v, "sec", n_sec, 1) for v in far]
-    far, far_pair, kept = sync((far, far_pair, kept))
     (far_ctx,) = attend(far + far_pair, kept, more)
-    near_rows, far_ctx, resid, resid_far = sync((near_rows, far_ctx, resid, resid_far))
+    across = lax.dynamic_index_in_dim(far_ctx, my_dp ^ 2, 0, keepdims=False)
+    near_rows, far_ctx, across = sync((near_rows, far_ctx, across))
 
     row_dp = lax.dynamic_index_in_dim(dest_dp, my_sec, 0, keepdims=False)
     row_slot = lax.dynamic_index_in_dim(dest_slot, my_sec, 0, keepdims=False)
@@ -400,53 +403,61 @@
     def put(whole, chunk, pieces):
         return place(order, pieces, whole, starts[chunk] // (unit * CHUNKS[chunk]), width)
 
-    far_across = spread(far_ctx, range(n_dp // 2, n_dp // 2 + 1))
-    near_rows = gathered(near_rows)
+    far_across = swap(across, "dp", n_dp, 2)
+    far_rows, near_rows = by_step(far_ctx), gathered(near_rows)
+    resid = jnp.concatenate([resid, resid_far], axis=0)
+    far_rows, near_rows, resid = sync((far_rows, near_rows, resid))
     near_projected = [project(c, near_rows) for c in range(2)]
-    resid = jnp.concatenate([resid, resid_far], axis=0)
-    far_across, near_projected, near_rows, far_ctx, resid = sync(
-        (far_across, near_projected, near_rows, far_ctx, resid)
-    )
-    others = [k for k in range(n_dp) if k != n_dp // 2]
-    far_rows = spread(far_ctx, others)
-    far_rows.insert(n_dp // 2, far_across[0])
+    far_rows, far_across, near_projected, near_rows, resid = sync(
+        (far_rows, far_across, near_projected, near_rows, resid)
+    )
+    far_rows = [far_across if k == 2 else swap(v, "dp", n_dp, k) if k else v for k, v in enumerate(far_rows)]
     near_others = [exchange(p) for p in near_projected]
     resid_pair = swap(resid, "sec", n_sec, 1)
-    near_projected += [project(c, near_rows) for c in range(2, count - 1)]
+    near_projected += [project(c, near_rows) for c in range(2, SPLIT)]
     far_rows, near_others, near_projected, near_rows, resid_pair = sync(
         (far_rows, near_others, near_projected, near_rows, resid_pair)
     )
 
     far_rows = gathered(far_rows)
-    first = project(0, far_rows)
-    first, far_rows = sync((first, far_rows))
-    far_others = [exchange(first)]
-    far_projected = [first, project(1, far_rows)]
+    far_projected = [project(0, far_rows)]
+    far_projected, far_rows = sync((far_projected, far_rows))
+    far_others = [exchange(far_projected[0])]
+    far_projected.append(project(1, far_rows))
     far_others, far_projected, far_rows = sync((far_others, far_projected, far_rows))
-    packed, part = finish(0, [near_projected[0][0], first[0]], [near_others[0], far_others[0]])
+
+    def halves(near, far):
+        return [(near, 0), (far, 0)]
+
+    packed, part = finish(
+        0, halves(near_projected[0][0], far_projected[0][0]), halves(near_others[0], far_others[0])
+    )
     packed, far_projected, far_rows = sync((packed, far_projected, far_rows))
 
-    stats, whole, pieces = [part], None, None
+    stats, whole, pieces, projected = [part], None, None, None
+    all_rows = jnp.concatenate([v.reshape(n_tp, -1, v.shape[-1]) for v in (near_rows, far_rows)], axis=1)
+    all_rows = all_rows.reshape(-1, wq.shape[2])
     for chunk in range(count):
         moved = [packed[0]] + [swap(packed[k], "dp", n_dp, k) for k in range(1, n_dp)]
         if pieces is not None:
             whole = put(whole, chunk - 1, pieces)
         ahead = chunk + 1
         if ahead < count:
-            far_others.append(exchange(far_projected[ahead]))
-            if len(near_others) == ahead:
-                near_others.append(exchange(near_projected[ahead]))
-            elif ahead + 1 < count - 1:
+            if ahead < SPLIT:
+                owns = halves(near_projected[ahead][0], far_projected[ahead][0])
+                others = halves(near_others[ahead], exchange(far_projected[ahead]))
+            else:
+                other = exchange(projected)
+                owns, others = [(projected[0], 0), (projected[0], 1)], [(other, 0), (other, 1)]
+            if ahead + 1 < SPLIT:
                 near_others.append(exchange(near_projected[ahead + 1]))
-            if ahead + 1 < count:
                 far_projected.append(project(ahead + 1, far_rows))
-                if ahead + 1 == count - 1:
-                    near_projected.append(project(ahead + 1, near_rows))
-            owns = [near_projected[ahead][0], far_projected[ahead][0]]
-            packed, part = finish(ahead, owns, [near_others[ahead], far_others[ahead]])
+            elif ahead + 1 < count:
+                projected = project(ahead + 1, all_rows)
+            packed, part = finish(ahead, owns, others)
             stats.append(part)
-            moved, packed, whole, far_rows, far_projected, near_others[-1] = sync(
-                (moved, packed, whole, far_rows, far_projected, near_others[-1])
+            moved, packed, whole, all_rows, far_projected, near_others, projected = sync(
+                (moved, packed, whole, all_rows, far_projected, near_others, projected)
             )
         pieces = moved
     whole = put(whole, count - 1, pieces)

time: 312 us -> 297 us (0.952)
  waiting for transfers between devices: 92.5 us -> 82.8 us
  Pallas kernels: 141 us -> 133 us
    ppermute x33, waiting for transfers between devices: 70.5 us -> 46 us  [swap(): return lax.ppermute(value, axis, [(j, j ^ step) for j in range(size)])]
    ppermute x19 -> x17, waiting for transfers between devices: 22 us -> 36.9 us  [shift(): lax.ppermute(value, axis, [(j, (j + step) % size) for j in range(size)])]
    pallas_call x10 -> x8, Pallas kernels: 47.4 us -> 39.6 us  [out_projection(): pl.pallas_call(out_kernel, out_shape=[jax.ShapeDtypeStruct((mine, cols),...]
    ppermute x19 -> x17, starting transfers between devices: 14.6 us -> 18.1 us  [shift(): lax.ppermute(value, axis, [(j, (j + step) % size) for j in range(size)])]
    unnamed x72 -> x62, local copies, waits for them, and re-layouts: 11.7 us -> 12.9 us
  transfers between devices with their start and end apart: 52 -> 50, of which waited for: 20 -> 19; matrix products, arithmetic and copies ran while one was open for 3% -> 4% of each run, Pallas kernels for 43% -> 43%
where the time goes in v5:
time: 297 us; the launch traced here: 296 us
  Pallas kernels  133 us (45%)
  waiting for transfers between devices  82.8 us (28%)
  starting transfers between devices  53.7 us (18%)
  local copies, waits for them, and re-layouts  18.2 us (6%)
  other arithmetic  7.42 us (2%)
    pallas_call x3, Pallas kernels, attention(): pl.pallas_call(functools.partial(attention_kernel, n_dp, n_tp, len(pieces...  65.7 us
    ppermute x33, waiting for transfers between devices, swap(): return lax.ppermute(value, axis, [(j, j ^ step) for j in range(size)])  46 us
    pallas_call x8, Pallas kernels, out_projection(): pl.pallas_call(out_kernel, out_shape=[jax.ShapeDtypeStruct((mine, cols),...  39.6 us
    ppermute x17, waiting for transfers between devices, shift(): lax.ppermute(value, axis, [(j, (j + step) % size) for j in range(size)])  36.9 us
    ppermute x33, starting transfers between devices, swap(): return lax.ppermute(value, axis, [(j, j ^ step) for j in range(size)])  35.6 us
    ppermute x17, starting transfers between devices, shift(): lax.ppermute(value, axis, [(j, (j + step) % size) for j in range(size)])  18.1 us
    pallas_call x5, Pallas kernels, join(): pl.pallas_call(functools.partial(join_kernel, n_slots, block), out_shape=...  15.4 us
    unnamed x62, local copies, waits for them, and re-layouts  12.9 us
  transfers between devices with their start and end apart: 50, of which 19 were waited for; matrix products, arithmetic and copies ran while one was open for 4% of the time, Pallas kernels for 43%

profile of v5, /device:TPU:8, one launch (start us, length us, event | category | flops | bytes accessed | tf_op | source)
XLA Modules:
  0.0 296.4 jit_solution(7684640088968195773)
XLA Ops:
  7.2 2.6 collective-permute-start.4
  12.3 19.0 %project_and_attend.3.refs_10_ = bf16[2,128,1536]{2,1,0:T(8,128)(2,1)S(1)} custom-call(bf16[64,8192]{1,0:T(8,128)(2,1)S(1)} %bitcast.102, bf16[64,8192]{1,0:T(8,128)(2,1)S(1)} %collective-permute-done.2.refs_1_, f32[1,8192]{1,0:T(1,128)S(1)} %copy-done.13, f32[128,128]{1,0:T(8,128)S(1)} %copy.49.refs_3_.refs_5_, ...), custom_call_target="tpu_custom_call" | custom-call | flops 1 | bytes 1 | tf_op jit(solution)/shard_map/project_and_attend/pallas_call | solution.py:162
  38.4 26.6 %project_and_attend.4 = (bf16[4,2,2,16,2048]{4,3,2,1,0:T(8,128)(2,1)S(1)}, bf16[2,128,1536]{2,1,0:T(8,128)(2,1)S(1)}) custom-call(bf16[64,8192]{1,0:T(8,128)(2,1)S(1)} %collective-permute-done.refs_0_, bf16[64,8192]{1,0:T(8,128)(2,1)S(1)} %collective-permute-done.6.refs_1_, bf16[64,8192]{1,0:T(8,128)(2,1)S(1)} %collective-permute-done.1.refs_2_, ...), custom_call_target="tpu_custom_call" | custom-call | flops 1 | bytes 1 | tf_op jit(solution)/shard_map/project_and_attend/pallas_call | solution.py:162
  69.5 3.0 %collective-permute-start.11 = (bf16[2,2,16,2048]{3,2,1,0:T(8,128)(2,1)S(1)}, bf16[2,2,16,2048]{3,2,1,0:T(8,128)(2,1)S(1)}, u32[]{:S(2)}, u32[]{:S(2)}) collective-permute-start(bf16[2,2,16,2048]{3,2,1,0:T(8,128)(2,1)S(1)} %get-tuple-element.337), channel_id=1, source_target_pairs={{0,4},{2,6},{4,0},{6,2},{1,5},{3,7},{5,1},{7,3},{8,12},{10,14},{12... | collective-permute-start | bytes 786440 | tf_op jit(solution)/shard_map/ppermute | solution.py:24
  76.1 20.2 %project_and_attend.5 = bf16[4,2,2,16,2048]{4,3,2,1,0:T(8,128)(2,1)S(1)} custom-call(bf16[32,8192]{1,0:T(8,128)(2,1)S(1)} %copy-done.8, bf16[32,8192]{1,0:T(8,128)(2,1)S(1)} %copy-done.10, bf16[32,8192]{1,0:T(8,128)(2,1)S(1)} %collective-permute-done.13.refs_2_, bf16[32,8192]{1,0:T(8,128)(2,1)S(1)} %collective-permute-done.14.refs_3_, ...), custom_call_target="tpu_custom_call" | custom-call | flops 1 | bytes 1 | tf_op jit(solution)/shard_map/project_and_attend/pallas_call | solution.py:162
  96.4 2.4 collective-permute-start.16
  101.6 3.1 %out_projection.8 = (bf16[128,1024]{1,0:T(8,128)(2,1)S(1)}, bf16[128,1024]{1,0:T(8,128)(2,1)S(1)}) custom-call(bf16[256,2048]{1,0:T(8,128)(2,1)S(1)} %bitcast.88, bf16[1,2048,8192]{2,1,0:T(8,128)(2,1)} %wo_ref.15), custom_call_target="tpu_custom_call" | custom-call | flops 1 | bytes 1 | tf_op jit(solution)/shard_map/out_projection/pallas_call | solution.py:192
  105.4 3.2 %out_projection.9 = (bf16[128,1024]{1,0:T(8,128)(2,1)S(1)}, bf16[128,1024]{1,0:T(8,128)(2,1)S(1)}) custom-call(bf16[256,2048]{1,0:T(8,128)(2,1)S(1)} %bitcast.89, bf16[1,2048,8192]{2,1,0:T(8,128)(2,1)} %wo_ref.15), custom_call_target="tpu_custom_call" | custom-call | flops 1 | bytes 1 | tf_op jit(solution)/shard_map/out_projection/pallas_call | solution.py:192
  110.1 2.4 collective-permute-start.17
  116.3 6.3 %out_projection.10 = (bf16[128,2048]{1,0:T(8,128)(2,1)S(1)}, bf16[128,2048]{1,0:T(8,128)(2,1)}) custom-call(bf16[256,2048]{1,0:T(8,128)(2,1)S(1)} %bitcast.90, bf16[1,2048,8192]{2,1,0:T(8,128)(2,1)} %wo_ref.15), custom_call_target="tpu_custom_call" | custom-call | flops 1 | bytes 1 | tf_op jit(solution)/shard_map/out_projection/pallas_call | solution.py:192
  123.4 3.5 %collective-permute-done.18 = bf16[2,2,16,2048]{3,2,1,0:T(8,128)(2,1)} collective-permute-done((bf16[2,2,16,2048]{3,2,1,0:T(8,128)(2,1)}, bf16[2,2,16,2048]{3,2,1,0:T(8,128)(2,1)}, u32[]{:S(2)}, u32[]{:S(2)}) %collective-permute-start.18) | collective-permute-done | bytes 262176 | tf_op jit(solution)/shard_map/ppermute | solution.py:24
  129.4 4.1 %out_projection.11 = (bf16[128,1024]{1,0:T(8,128)(2,1)S(1)}, bf16[128,1024]{1,0:T(8,128)(2,1)}) custom-call(bf16[256,2048]{1,0:T(8,128)(2,1)S(1)} %bitcast.92, bf16[1,2048,8192]{2,1,0:T(8,128)(2,1)} %wo_ref.15), custom_call_target="tpu_custom_call" | custom-call | flops 1 | bytes 1 | tf_op jit(solution)/shard_map/out_projection/pallas_call | solution.py:192
  139.0 3.1 %out_projection.12 = (bf16[128,1024]{1,0:T(8,128)(2,1)S(1)}, bf16[128,1024]{1,0:T(8,128)(2,1)S(1)}) custom-call(bf16[256,2048]{1,0:T(8,128)(2,1)S(1)} %bitcast.93, bf16[1,2048,8192]{2,1,0:T(8,128)(2,1)} %wo_ref.15), custom_call_target="tpu_custom_call" | custom-call | flops 1 | bytes 1 | tf_op jit(solution)/shard_map/out_projection/pallas_call | solution.py:192
  143.8 2.6 join_partials.5
  151.4 5.6 %out_projection.13 = (bf16[128,2048]{1,0:T(8,128)(2,1)S(1)}, bf16[128,2048]{1,0:T(8,128)(2,1)S(1)}) custom-call(bf16[256,2048]{1,0:T(8,128)(2,1)S(1)} %bitcast.94, bf16[1,2048,8192]{2,1,0:T(8,128)(2,1)} %wo_ref.15), custom_call_target="tpu_custom_call" | custom-call | flops 1 | bytes 1 | tf_op jit(solution)/shard_map/out_projection/pallas_call | solution.py:192
  158.6 2.5 join_partials.6
  161.2 3.0 %collective-permute-done.25.refs_3_ = bf16[6,16,1024]{2,1,0:T(8,128)(2,1)S(1)} collective-permute-done((bf16[6,16,1024]{2,1,0:T(8,128)(2,1)S(1)}, bf16[6,16,1024]{2,1,0:T(8,128)(2,1)S(1)}, u32[]{:S(2)}, u32[]{:S(2)}) %collective-permute-start.25) | collective-permute-done | bytes 196640 | tf_op jit(solution)/shard_map/ppermute | solution.py:24
  169.1 7.1 %out_projection.14 = (bf16[256,2048]{1,0:T(8,128)(2,1)S(1)}, bf16[256,2048]{1,0:T(8,128)(2,1)S(1)}) custom-call(bf16[512,2048]{1,0:T(8,128)(2,1)S(1)} %bitcast.96, bf16[1,2048,8192]{2,1,0:T(8,128)(2,1)} %wo_ref.15), custom_call_target="tpu_custom_call" | custom-call | flops 1 | bytes 1 | tf_op jit(solution)/shard_map/out_projection/pallas_call | solution.py:192
  178.2 3.3 %join_partials.7 = (bf16[6,16,2048]{2,1,0:T(8,128)(2,1)S(1)}, bf16[6,16,2048]{2,1,0:T(8,128)(2,1)S(1)}, bf16[6,16,2048]{2,1,0:T(8,128)(2,1)S(1)}, bf16[6,16,2048]{2,1,0:T(8,128)(2,1)S(1)}, f32[4,6,16,128]{3,2,1,0:T(8,128)S(1)}) custom-call(s32[5,24]{1,0:T(8,128)S(1)} %stack.72.table_ref, bf16[8,16,2048]{2,1,0:T(8,128)(2,1)S(1)} %bitcast.111, ...), custom_call_target="tpu_custom_call" | custom-call | flops 1 | bytes 1 | tf_op jit(solution)/shard_map/join_partials/pallas_call | solution.py:243
  181.5 2.6 collective-permute-done.30.refs_3_
  188.3 7.1 %out_projection.15 = (bf16[256,2048]{1,0:T(8,128)(2,1)S(1)}, bf16[256,2048]{1,0:T(8,128)(2,1)S(1)}) custom-call(bf16[512,2048]{1,0:T(8,128)(2,1)S(1)} %bitcast.97, bf16[1,2048,8192]{2,1,0:T(8,128)(2,1)} %wo_ref.15), custom_call_target="tpu_custom_call" | custom-call | flops 1 | bytes 1 | tf_op jit(solution)/shard_map/out_projection/pallas_call | solution.py:192
  197.5 10.1 %collective-permute-done.35 = bf16[16,16,2048]{2,1,0:T(8,128)(2,1)S(1)} collective-permute-done((bf16[16,16,2048]{2,1,0:T(8,128)(2,1)S(1)}, bf16[16,16,2048]{2,1,0:T(8,128)(2,1)S(1)}, u32[]{:S(2)}, u32[]{:S(2)}) %collective-permute-start.35) | collective-permute-done | bytes 1048608 | tf_op jit(solution)/shard_map/ppermute | solution.py:31
  207.6 3.9 %join_partials.8 = (bf16[6,16,2048]{2,1,0:T(8,128)(2,1)S(1)}, bf16[6,16,2048]{2,1,0:T(8,128)(2,1)}, bf16[6,16,2048]{2,1,0:T(8,128)(2,1)}, bf16[6,16,2048]{2,1,0:T(8,128)(2,1)}, f32[4,6,16,128]{3,2,1,0:T(8,128)S(1)}) custom-call(s32[5,24]{1,0:T(8,128)S(1)} %stack.72.table_ref, bf16[16,16,2048]{2,1,0:T(8,128)(2,1)S(1)} %bitcast.105, ...), custom_call_target="tpu_custom_call" | custom-call | flops 1 | bytes 1 | tf_op jit(solution)/shard_map/join_partials/pallas_call | solution.py:243
  213.1 7.4 %collective-permute-done.34.refs_3_ = bf16[6,16,2048]{2,1,0:T(8,128)(2,1)S(1)} collective-permute-done((bf16[6,16,2048]{2,1,0:T(8,128)(2,1)S(1)}, bf16[6,16,2048]{2,1,0:T(8,128)(2,1)S(1)}, u32[]{:S(2)}, u32[]{:S(2)}) %collective-permute-start.34) | collective-permute-done | bytes 393248 | tf_op jit(solution)/shard_map/ppermute | solution.py:24
  227.6 15.4 %collective-permute-done.39 = bf16[16,16,2048]{2,1,0:T(8,128)(2,1)S(1)} collective-permute-done((bf16[16,16,2048]{2,1,0:T(8,128)(2,1)S(1)}, bf16[16,16,2048]{2,1,0:T(8,128)(2,1)S(1)}, u32[]{:S(2)}, u32[]{:S(2)}) %collective-permute-start.39) | collective-permute-done | bytes 1048608 | tf_op jit(solution)/shard_map/ppermute | solution.py:31
  243.0 3.1 %join_partials.9 = (bf16[6,16,2048]{2,1,0:T(8,128)(2,1)S(1)}, bf16[6,16,2048]{2,1,0:T(8,128)(2,1)S(1)}, bf16[6,16,2048]{2,1,0:T(8,128)(2,1)S(1)}, bf16[6,16,2048]{2,1,0:T(8,128)(2,1)S(1)}, f32[4,6,16,128]{3,2,1,0:T(8,128)S(1)}) custom-call(s32[5,24]{1,0:T(8,128)S(1)} %stack.72.table_ref, bf16[16,16,2048]{2,1,0:T(8,128)(2,1)S(1)} %bitcast.103, ...), custom_call_target="tpu_custom_call" | custom-call | flops 1 | bytes 1 | tf_op jit(solution)/shard_map/join_partials/pallas_call | solution.py:243
  249.4 7.1 %collective-permute-done.38.refs_3_ = bf16[6,16,2048]{2,1,0:T(8,128)(2,1)} collective-permute-done((bf16[6,16,2048]{2,1,0:T(8,128)(2,1)}, bf16[6,16,2048]{2,1,0:T(8,128)(2,1)}, u32[]{:S(2)}, u32[]{:S(2)}) %collective-permute-start.38) | collective-permute-done | bytes 393248 | tf_op jit(solution)/shard_map/ppermute | solution.py:24
  256.7 3.4 %collective-permute-start.45 = (f32[4,16]{1,0:T(4,128)S(1)}, f32[4,16]{1,0:T(4,128)S(1)}, u32[]{:S(2)}, u32[]{:S(2)}) collective-permute-start(f32[4,16]{1,0:T(4,128)S(1)} %fusion.22), channel_id=1, source_target_pairs={{0,4},{2,6},{4,0},{6,2},{1,5},{3,7},{5,1},{7,3},{8,12},{10,14},{12... | collective-permute-start | bytes 776 | tf_op jit(solution)/shard_map/ppermute | solution.py:31
  263.6 6.8 %collective-permute-done.45 = f32[4,16]{1,0:T(4,128)S(1)} collective-permute-done((f32[4,16]{1,0:T(4,128)S(1)}, f32[4,16]{1,0:T(4,128)S(1)}, u32[]{:S(2)}, u32[]{:S(2)}) %collective-permute-start.45) | collective-permute-done | bytes 288 | tf_op jit(solution)/shard_map/ppermute | solution.py:31
  273.2 3.7 %place_rows.8.refs_4_ = bf16[6,4,16,8192]{3,2,1,0:T(8,128)(2,1)} custom-call(s32[4]{0:T(128)S(1)} %iota_xor_fusion.order_ref, bf16[6,16,2048]{2,1,0:T(8,128)(2,1)S(1)} %get-tuple-element.318.refs_0_, bf16[6,16,2048]{2,1,0:T(8,128)(2,1)S(1)} %collective-permute-done.36.refs_1_, ...), custom_call_target="tpu_custom_call", output_to_operand_aliasing={{}: (5, {})} | custom-call | flops 1 | bytes 1 | tf_op jit(solution)/shard_map/place_rows/pallas_call | solution.py:284
  277.7 9.7 %collective-permute-done.41.refs_2_ = bf16[6,16,2048]{2,1,0:T(8,128)(2,1)S(1)} collective-permute-done((bf16[6,16,2048]{2,1,0:T(8,128)(2,1)}, bf16[6,16,2048]{2,1,0:T(8,128)(2,1)S(1)}, u32[]{:S(2)}, u32[]{:S(2)}) %collective-permute-start.41) | collective-permute-done | bytes 393248 | tf_op jit(solution)/shard_map/ppermute | solution.py:24
  287.3 6.8 %collective-permute-done.42.refs_3_ = bf16[6,16,2048]{2,1,0:T(8,128)(2,1)S(1)} collective-permute-done((bf16[6,16,2048]{2,1,0:T(8,128)(2,1)}, bf16[6,16,2048]{2,1,0:T(8,128)(2,1)S(1)}, u32[]{:S(2)}, u32[]{:S(2)}) %collective-permute-start.42) | collective-permute-done | bytes 393248 | tf_op jit(solution)/shard_map/ppermute | solution.py:24
  (205 shorter events, 84.4 us)
Async XLA Ops:
  0.7 30.6 %collective-permute-start = (bf16[64,8192]{1,0:T(8,128)(2,1)}, bf16[64,8192]{1,0:T(8,128)(2,1)S(1)}, u32[]{:S(2)}, u32[]{:S(2)}) collective-permute-start(bf16[64,8192]{1,0:T(8,128)(2,1)} %bitcast.99), channel_id=1, source_target_pairs={{0,1},{1,0},{2,3},{3,2},{4,5},{5,4},{6,7},{7,6},{8,9},{9,8},{10,11... | collective-permute-start | bytes 3145736 | tf_op jit(solution)/shard_map/ppermute | solution.py:31
  2.3 29.0 %collective-permute-start.1 = (bf16[64,8192]{1,0:T(8,128)(2,1)}, bf16[64,8192]{1,0:T(8,128)(2,1)S(1)}, u32[]{:S(2)}, u32[]{:S(2)}) collective-permute-start(bf16[64,8192]{1,0:T(8,128)(2,1)} %bitcast.100), channel_id=1, source_target_pairs={{0,16},{8,24},{16,0},{24,8},{1,17},{9,25},{17,1},{25,9},{2,18},{10... | collective-permute-start | bytes 3145736 | tf_op jit(solution)/shard_map/ppermute | solution.py:24
  6.8 24.6 %collective-permute-start.3 = (bf16[16,8192]{1,0:T(8,128)(2,1)}, bf16[16,8192]{1,0:T(8,128)(2,1)}, u32[]{:S(2)}, u32[]{:S(2)}) collective-permute-start(bf16[16,8192]{1,0:T(8,128)(2,1)} %get-tuple-element.342), channel_id=1, source_target_pairs={{0,2},{2,0},{4,6},{6,4},{1,3},{3,1},{5,7},{7,5},{8,10},{10,8},{12,... | collective-permute-start | bytes 786440 | tf_op jit(solution)/shard_map/ppermute | solution.py:24
  7.2 24.1 %collective-permute-start.4 = (bf16[16,8192]{1,0:T(8,128)(2,1)}, bf16[16,8192]{1,0:T(8,128)(2,1)}, u32[]{:S(2)}, u32[]{:S(2)}) collective-permute-start(bf16[16,8192]{1,0:T(8,128)(2,1)} %get-tuple-element.341), channel_id=1, source_target_pairs={{0,4},{2,6},{4,0},{6,2},{1,5},{3,7},{5,1},{7,3},{8,12},{10,14},{12... | collective-permute-start | bytes 786440 | tf_op jit(solution)/shard_map/ppermute | solution.py:24
  9.8 23.5 %collective-permute-start.5 = (bf16[16,8192]{1,0:T(8,128)(2,1)}, bf16[16,8192]{1,0:T(8,128)(2,1)}, u32[]{:S(2)}, u32[]{:S(2)}) collective-permute-start(bf16[16,8192]{1,0:T(8,128)(2,1)} %get-tuple-element.340), channel_id=1, source_target_pairs={{0,6},{2,4},{4,2},{6,0},{1,7},{3,5},{5,3},{7,1},{8,14},{10,12},{12... | collective-permute-start | bytes 786440 | tf_op jit(solution)/shard_map/ppermute | solution.py:24
  33.9 32.0 %collective-permute-start.8 = (bf16[32,8192]{1,0:T(8,128)(2,1)S(1)}, bf16[32,8192]{1,0:T(8,128)(2,1)S(1)}, u32[]{:S(2)}, u32[]{:S(2)}) collective-permute-start(bf16[32,8192]{1,0:T(8,128)(2,1)S(1)} %slice.33), channel_id=1, source_target_pairs={{0,1},{1,0},{2,3},{3,2},{4,5},{5,4},{6,7},{7,6},{8,9},{9,8},{10,11... | collective-permute-start | bytes 1572872 | tf_op jit(solution)/shard_map/ppermute | solution.py:31
  34.7 31.2 %collective-permute-start.9 = (bf16[32,8192]{1,0:T(8,128)(2,1)S(1)}, bf16[32,8192]{1,0:T(8,128)(2,1)S(1)}, u32[]{:S(2)}, u32[]{:S(2)}) collective-permute-start(bf16[32,8192]{1,0:T(8,128)(2,1)S(1)} %slice.34), channel_id=1, source_target_pairs={{0,16},{8,24},{16,0},{24,8},{1,17},{9,25},{17,1},{25,9},{2,18},{10... | collective-permute-start | bytes 1572872 | tf_op jit(solution)/shard_map/ppermute | solution.py:24
  68.7 31.1 %collective-permute-start.15 = (bf16[4,16,8192]{2,1,0:T(8,128)(2,1)}, bf16[4,16,8192]{2,1,0:T(8,128)(2,1)}, u32[]{:S(2)}, u32[]{:S(2)}) collective-permute-start(bf16[4,16,8192]{2,1,0:T(8,128)(2,1)} %pad_maximum_fusion.2), channel_id=1, source_target_pairs={{0,16},{8,24},{16,0},{24,8},{1,17},{9,25},{17,1},{25,9},{2,18},{10... | collective-permute-start | bytes 3145736 | tf_op jit(solution)/shard_map/ppermute | solution.py:24
  69.4 27.0 %collective-permute-start.10 = (bf16[2,2,16,2048]{3,2,1,0:T(8,128)(2,1)S(1)}, bf16[2,2,16,2048]{3,2,1,0:T(8,128)(2,1)S(1)}, u32[]{:S(2)}, u32[]{:S(2)}) collective-permute-start(bf16[2,2,16,2048]{3,2,1,0:T(8,128)(2,1)S(1)} %get-tuple-element.338), channel_id=1, source_target_pairs={{0,2},{2,0},{4,6},{6,4},{1,3},{3,1},{5,7},{7,5},{8,10},{10,8},{12,... | collective-permute-start | bytes 786440 | tf_op jit(solution)/shard_map/ppermute | solution.py:24
  69.5 26.9 %collective-permute-start.11 = (bf16[2,2,16,2048]{3,2,1,0:T(8,128)(2,1)S(1)}, bf16[2,2,16,2048]{3,2,1,0:T(8,128)(2,1)S(1)}, u32[]{:S(2)}, u32[]{:S(2)}) collective-permute-start(bf16[2,2,16,2048]{3,2,1,0:T(8,128)(2,1)S(1)} %get-tuple-element.337), channel_id=1, source_target_pairs={{0,4},{2,6},{4,0},{6,2},{1,5},{3,7},{5,1},{7,3},{8,12},{10,14},{12... | collective-permute-start | bytes 786440 | tf_op jit(solution)/shard_map/ppermute | solution.py:24
  72.5 23.9 %collective-permute-start.12 = (bf16[2,2,16,2048]{3,2,1,0:T(8,128)(2,1)S(1)}, bf16[2,2,16,2048]{3,2,1,0:T(8,128)(2,1)S(1)}, u32[]{:S(2)}, u32[]{:S(2)}) collective-permute-start(bf16[2,2,16,2048]{3,2,1,0:T(8,128)(2,1)S(1)} %get-tuple-element.336), channel_id=1, source_target_pairs={{0,6},{2,4},{4,2},{6,0},{1,7},{3,5},{5,3},{7,1},{8,14},{10,12},{12... | collective-permute-start | bytes 786440 | tf_op jit(solution)/shard_map/ppermute | solution.py:24
  110.1 18.2 %collective-permute-start.21 = (bf16[8,16,8192]{2,1,0:T(8,128)(2,1)S(1)}, bf16[8,16,8192]{2,1,0:T(8,128)(2,1)}, u32[]{:S(2)}, u32[]{:S(2)}) collective-permute-start(bf16[8,16,8192]{2,1,0:T(8,128)(2,1)S(1)} %pad_maximum_fusion.resid_ref), channel_id=1, source_target_pairs={{0,8},{8,0},{16,24},{24,16},{1,9},{9,1},{17,25},{25,17},{2,10},{10... | collective-permute-start | bytes 6291464 | tf_op jit(solution)/shard_map/ppermute | solution.py:24
  112.5 14.4 %collective-permute-start.18 = (bf16[2,2,16,2048]{3,2,1,0:T(8,128)(2,1)}, bf16[2,2,16,2048]{3,2,1,0:T(8,128)(2,1)}, u32[]{:S(2)}, u32[]{:S(2)}) collective-permute-start(bf16[2,2,16,2048]{3,2,1,0:T(8,128)(2,1)} %get-tuple-element.213), channel_id=1, source_target_pairs={{0,6},{2,4},{4,2},{6,0},{1,7},{3,5},{5,3},{7,1},{8,14},{10,12},{12... | collective-permute-start | bytes 786440 | tf_op jit(solution)/shard_map/ppermute | solution.py:24
  135.6 28.5 %collective-permute-start.27 = (bf16[8,16,2048]{2,1,0:T(8,128)(2,1)}, bf16[8,16,2048]{2,1,0:T(8,128)(2,1)}, u32[]{:S(2)}, u32[]{:S(2)}) collective-permute-start(bf16[8,16,2048]{2,1,0:T(8,128)(2,1)} %bitcast.49), channel_id=1, source_target_pairs={{0,1},{1,0},{2,3},{3,2},{4,5},{5,4},{6,7},{7,6},{8,9},{9,8},{10,11... | collective-permute-start | bytes 1572872 | tf_op jit(solution)/shard_map/ppermute | solution.py:31
  146.4 14.7 %collective-permute-start.23 = (bf16[6,16,1024]{2,1,0:T(8,128)(2,1)S(1)}, bf16[6,16,1024]{2,1,0:T(8,128)(2,1)S(1)}, u32[]{:S(2)}, u32[]{:S(2)}) collective-permute-start(bf16[6,16,1024]{2,1,0:T(8,128)(2,1)S(1)} %get-tuple-element.246), channel_id=1, source_target_pairs={{0,2},{2,0},{4,6},{6,4},{1,3},{3,1},{5,7},{7,5},{8,10},{10,8},{12,... | collective-permute-start | bytes 589832 | tf_op jit(solution)/shard_map/ppermute | solution.py:24
  148.4 15.8 %collective-permute-start.25 = (bf16[6,16,1024]{2,1,0:T(8,128)(2,1)S(1)}, bf16[6,16,1024]{2,1,0:T(8,128)(2,1)S(1)}, u32[]{:S(2)}, u32[]{:S(2)}) collective-permute-start(bf16[6,16,1024]{2,1,0:T(8,128)(2,1)S(1)} %get-tuple-element.248), channel_id=1, source_target_pairs={{0,6},{2,4},{4,2},{6,0},{1,7},{3,5},{5,3},{7,1},{8,14},{10,12},{12... | collective-permute-start | bytes 589832 | tf_op jit(solution)/shard_map/ppermute | solution.py:24
  164.2 14.1 %collective-permute-start.31 = (bf16[8,16,2048]{2,1,0:T(8,128)(2,1)S(1)}, bf16[8,16,2048]{2,1,0:T(8,128)(2,1)S(1)}, u32[]{:S(2)}, u32[]{:S(2)}) collective-permute-start(bf16[8,16,2048]{2,1,0:T(8,128)(2,1)S(1)} %bitcast.121), channel_id=1, source_target_pairs={{0,1},{1,0},{2,3},{3,2},{4,5},{5,4},{6,7},{7,6},{8,9},{9,8},{10,11... | collective-permute-start | bytes 1572872 | tf_op jit(solution)/shard_map/ppermute | solution.py:31
  165.6 15.9 %collective-permute-start.28 = (bf16[6,16,1024]{2,1,0:T(8,128)(2,1)S(1)}, bf16[6,16,1024]{2,1,0:T(8,128)(2,1)S(1)}, u32[]{:S(2)}, u32[]{:S(2)}) collective-permute-start(bf16[6,16,1024]{2,1,0:T(8,128)(2,1)S(1)} %get-tuple-element.263), channel_id=1, source_target_pairs={{0,2},{2,0},{4,6},{6,4},{1,3},{3,1},{5,7},{7,5},{8,10},{10,8},{12,... | collective-permute-start | bytes 589832 | tf_op jit(solution)/shard_map/ppermute | solution.py:24
  165.6 16.0 %collective-permute-start.29 = (bf16[6,16,1024]{2,1,0:T(8,128)(2,1)S(1)}, bf16[6,16,1024]{2,1,0:T(8,128)(2,1)S(1)}, u32[]{:S(2)}, u32[]{:S(2)}) collective-permute-start(bf16[6,16,1024]{2,1,0:T(8,128)(2,1)S(1)} %get-tuple-element.264), channel_id=1, source_target_pairs={{0,4},{2,6},{4,0},{6,2},{1,5},{3,7},{5,1},{7,3},{8,12},{10,14},{12... | collective-permute-start | bytes 589832 | tf_op jit(solution)/shard_map/ppermute | solution.py:24
  167.6 16.5 %collective-permute-start.30 = (bf16[6,16,1024]{2,1,0:T(8,128)(2,1)S(1)}, bf16[6,16,1024]{2,1,0:T(8,128)(2,1)S(1)}, u32[]{:S(2)}, u32[]{:S(2)}) collective-permute-start(bf16[6,16,1024]{2,1,0:T(8,128)(2,1)S(1)} %get-tuple-element.265), channel_id=1, source_target_pairs={{0,6},{2,4},{4,2},{6,0},{1,7},{3,5},{5,3},{7,1},{8,14},{10,12},{12... | collective-permute-start | bytes 589832 | tf_op jit(solution)/shard_map/ppermute | solution.py:24
  184.1 23.5 %collective-permute-start.35 = (bf16[16,16,2048]{2,1,0:T(8,128)(2,1)S(1)}, bf16[16,16,2048]{2,1,0:T(8,128)(2,1)S(1)}, u32[]{:S(2)}, u32[]{:S(2)}) collective-permute-start(bf16[16,16,2048]{2,1,0:T(8,128)(2,1)S(1)} %bitcast.119), channel_id=1, source_target_pairs={{0,1},{1,0},{2,3},{3,2},{4,5},{5,4},{6,7},{7,6},{8,9},{9,8},{10,11... | collective-permute-start | bytes 3145736 | tf_op jit(solution)/shard_map/ppermute | solution.py:31
  184.8 26.7 %collective-permute-start.32 = (bf16[6,16,2048]{2,1,0:T(8,128)(2,1)S(1)}, bf16[6,16,2048]{2,1,0:T(8,128)(2,1)S(1)}, u32[]{:S(2)}, u32[]{:S(2)}) collective-permute-start(bf16[6,16,2048]{2,1,0:T(8,128)(2,1)S(1)} %get-tuple-element.282), channel_id=1, source_target_pairs={{0,2},{2,0},{4,6},{6,4},{1,3},{3,1},{5,7},{7,5},{8,10},{10,8},{12,... | collective-permute-start | bytes 1179656 | tf_op jit(solution)/shard_map/ppermute | solution.py:24
  184.8 28.3 %collective-permute-start.33 = (bf16[6,16,2048]{2,1,0:T(8,128)(2,1)S(1)}, bf16[6,16,2048]{2,1,0:T(8,128)(2,1)S(1)}, u32[]{:S(2)}, u32[]{:S(2)}) collective-permute-start(bf16[6,16,2048]{2,1,0:T(8,128)(2,1)S(1)} %get-tuple-element.283), channel_id=1, source_target_pairs={{0,4},{2,6},{4,0},{6,2},{1,5},{3,7},{5,1},{7,3},{8,12},{10,14},{12... | collective-permute-start | bytes 1179656 | tf_op jit(solution)/shard_map/ppermute | solution.py:24
  186.7 33.9 %collective-permute-start.34 = (bf16[6,16,2048]{2,1,0:T(8,128)(2,1)S(1)}, bf16[6,16,2048]{2,1,0:T(8,128)(2,1)S(1)}, u32[]{:S(2)}, u32[]{:S(2)}) collective-permute-start(bf16[6,16,2048]{2,1,0:T(8,128)(2,1)S(1)} %get-tuple-element.284), channel_id=1, source_target_pairs={{0,6},{2,4},{4,2},{6,0},{1,7},{3,5},{5,3},{7,1},{8,14},{10,12},{12... | collective-permute-start | bytes 1179656 | tf_op jit(solution)/shard_map/ppermute | solution.py:24
  220.6 22.4 %collective-permute-start.39 = (bf16[16,16,2048]{2,1,0:T(8,128)(2,1)S(1)}, bf16[16,16,2048]{2,1,0:T(8,128)(2,1)S(1)}, u32[]{:S(2)}, u32[]{:S(2)}) collective-permute-start(bf16[16,16,2048]{2,1,0:T(8,128)(2,1)S(1)} %bitcast.120), channel_id=1, source_target_pairs={{0,1},{1,0},{2,3},{3,2},{4,5},{5,4},{6,7},{7,6},{8,9},{9,8},{10,11... | collective-permute-start | bytes 3145736 | tf_op jit(solution)/shard_map/ppermute | solution.py:31
  221.8 26.9 %collective-permute-start.36 = (bf16[6,16,2048]{2,1,0:T(8,128)(2,1)}, bf16[6,16,2048]{2,1,0:T(8,128)(2,1)S(1)}, u32[]{:S(2)}, u32[]{:S(2)}) collective-permute-start(bf16[6,16,2048]{2,1,0:T(8,128)(2,1)} %get-tuple-element.300), channel_id=1, source_target_pairs={{0,2},{2,0},{4,6},{6,4},{1,3},{3,1},{5,7},{7,5},{8,10},{10,8},{12,... | collective-permute-start | bytes 1179656 | tf_op jit(solution)/shard_map/ppermute | solution.py:24
  221.9 27.5 %collective-permute-start.37 = (bf16[6,16,2048]{2,1,0:T(8,128)(2,1)}, bf16[6,16,2048]{2,1,0:T(8,128)(2,1)}, u32[]{:S(2)}, u32[]{:S(2)}) collective-permute-start(bf16[6,16,2048]{2,1,0:T(8,128)(2,1)} %get-tuple-element.301), channel_id=1, source_target_pairs={{0,4},{2,6},{4,0},{6,2},{1,5},{3,7},{5,1},{7,3},{8,12},{10,14},{12... | collective-permute-start | bytes 1179656 | tf_op jit(solution)/shard_map/ppermute | solution.py:24
  223.2 33.4 %collective-permute-start.38 = (bf16[6,16,2048]{2,1,0:T(8,128)(2,1)}, bf16[6,16,2048]{2,1,0:T(8,128)(2,1)}, u32[]{:S(2)}, u32[]{:S(2)}) collective-permute-start(bf16[6,16,2048]{2,1,0:T(8,128)(2,1)} %get-tuple-element.302), channel_id=1, source_target_pairs={{0,6},{2,4},{4,2},{6,0},{1,7},{3,5},{5,3},{7,1},{8,14},{10,12},{12... | collective-permute-start | bytes 1179656 | tf_op jit(solution)/shard_map/ppermute | solution.py:24
  256.6 21.0 %collective-permute-start.40 = (bf16[6,16,2048]{2,1,0:T(8,128)(2,1)}, bf16[6,16,2048]{2,1,0:T(8,128)(2,1)S(1)}, u32[]{:S(2)}, u32[]{:S(2)}) collective-permute-start(bf16[6,16,2048]{2,1,0:T(8,128)(2,1)} %copy-done.21), channel_id=1, source_target_pairs={{0,2},{2,0},{4,6},{6,4},{1,3},{3,1},{5,7},{7,5},{8,10},{10,8},{12,... | collective-permute-start | bytes 1179656 | tf_op jit(solution)/shard_map/ppermute | solution.py:24
  256.7 13.7 %collective-permute-start.45 = (f32[4,16]{1,0:T(4,128)S(1)}, f32[4,16]{1,0:T(4,128)S(1)}, u32[]{:S(2)}, u32[]{:S(2)}) collective-permute-start(f32[4,16]{1,0:T(4,128)S(1)} %fusion.22), channel_id=1, source_target_pairs={{0,4},{2,6},{4,0},{6,2},{1,5},{3,7},{5,1},{7,3},{8,12},{10,14},{12... | collective-permute-start | bytes 776 | tf_op jit(solution)/shard_map/ppermute | solution.py:31
  260.2 27.2 %collective-permute-start.41 = (bf16[6,16,2048]{2,1,0:T(8,128)(2,1)}, bf16[6,16,2048]{2,1,0:T(8,128)(2,1)S(1)}, u32[]{:S(2)}, u32[]{:S(2)}) collective-permute-start(bf16[6,16,2048]{2,1,0:T(8,128)(2,1)} %copy-done.20), channel_id=1, source_target_pairs={{0,4},{2,6},{4,0},{6,2},{1,5},{3,7},{5,1},{7,3},{8,12},{10,14},{12... | collective-permute-start | bytes 1179656 | tf_op jit(solution)/shard_map/ppermute | solution.py:24
  262.5 31.6 %collective-permute-start.42 = (bf16[6,16,2048]{2,1,0:T(8,128)(2,1)}, bf16[6,16,2048]{2,1,0:T(8,128)(2,1)S(1)}, u32[]{:S(2)}, u32[]{:S(2)}) collective-permute-start(bf16[6,16,2048]{2,1,0:T(8,128)(2,1)} %copy-done.19), channel_id=1, source_target_pairs={{0,6},{2,4},{4,2},{6,0},{1,7},{3,5},{5,3},{7,1},{8,14},{10,12},{12... | collective-permute-start | bytes 1179656 | tf_op jit(solution)/shard_map/ppermute | solution.py:24
  (49 other events, 262.7 us)

commit v6 on v5

--- a/solution.py
+++ b/solution.py
@@ -339,26 +339,20 @@
     (kept,) = attend([mine, mine_pair], None, 0)
     near, far_mine, resid, kept = sync((near, far_mine, resid, kept))
 
-    half = local_len // 2
-    far = []
-    for k in range(1, n_tp):
-        parts = [shift(far_mine[:half], "tp", n_tp, k), swap(near[k - 1][half:], "sec", n_sec, 2)]
-        far += parts if half % 16 == 0 else [jnp.concatenate(parts, axis=0)]
+    far = [shift(far_mine, "tp", n_tp, k) for k in range(1, n_tp)]
     near_pair = [swap(v, "sec", n_sec, 1) for v in near]
     far_mine_pair = swap(far_mine, "sec", n_sec, 1)
     resid = jnp.stack(resid)
-    near, near_pair, far_mine, far_mine_pair, kept, resid = sync(
-        (near, near_pair, far_mine, far_mine_pair, kept, resid)
-    )
+    resid_far = swap(resid, "sec", n_sec, 2)
+    near, near_pair, far_mine, far_mine_pair, kept = sync((near, near_pair, far_mine, far_mine_pair, kept))
 
     more = 2 * (seq - local_len)
     near_ctx, kept = attend(near + near_pair + [far_mine, far_mine_pair], kept, more)
-    near_ctx, kept, far = sync((near_ctx, kept, far))
+    near_ctx, kept, far, resid, resid_far = sync((near_ctx, kept, far, resid, resid_far))
 
     near_rows = spread(by_step(near_ctx))
     far_pair = [swap(v, "sec", n_sec, 1) for v in far]
-    far, far_pair, kept, resid = sync((far, far_pair, kept, resid))
-    resid_far = swap(resid, "sec", n_sec, 2)
+    far, far_pair, kept = sync((far, far_pair, kept))
     (far_ctx,) = attend(far + far_pair, kept, more)
     across = lax.dynamic_index_in_dim(far_ctx, my_dp ^ 2, 0, keepdims=False)
     near_rows, far_ctx, across = sync((near_rows, far_ctx, across))

time: 297 us -> 292 us (0.983)
  local copies, waits for them, and re-layouts: 18.2 us -> 12.3 us
  starting transfers between devices: 53.7 us -> 50.1 us
  waiting for transfers between devices: 82.8 us -> 85.9 us
    unnamed x62 -> x50, local copies, waits for them, and re-layouts: 12.9 us -> 7.09 us
    ppermute x33 -> x31, waiting for transfers between devices: 46 us -> 48.5 us  [swap(): return lax.ppermute(value, axis, [(j, j ^ step) for j in range(size)])]
    ppermute x33 -> x31, starting transfers between devices: 35.6 us -> 33.4 us  [swap(): return lax.ppermute(value, axis, [(j, j ^ step) for j in range(size)])]
  transfers between devices with their start and end apart: 50 -> 48, of which waited for: 19 -> 18; matrix products, arithmetic and copies ran while one was open for 4% -> 4% of each run, Pallas kernels for 43% -> 44%
where the time goes in v6:
time: 292 us; the launch traced here: 291 us
  Pallas kernels  134 us (46%)
  waiting for transfers between devices  85.9 us (29%)
  starting transfers between devices  50.1 us (17%)
  local copies, waits for them, and re-layouts  12.3 us (4%)
  other arithmetic  7.42 us (3%)
    pallas_call x3, Pallas kernels, attention(): pl.pallas_call(functools.partial(attention_kernel, n_dp, n_tp, len(pieces...  66.6 us
    ppermute x31, waiting for transfers between devices, swap(): return lax.ppermute(value, axis, [(j, j ^ step) for j in range(size)])  48.5 us
    pallas_call x8, Pallas kernels, out_projection(): pl.pallas_call(out_kernel, out_shape=[jax.ShapeDtypeStruct((mine, cols),...  39.7 us
    ppermute x17, waiting for transfers between devices, shift(): lax.ppermute(value, axis, [(j, (j + step) % size) for j in range(size)])  37.4 us
    ppermute x31, starting transfers between devices, swap(): return lax.ppermute(value, axis, [(j, j ^ step) for j in range(size)])  33.4 us
    ppermute x17, starting transfers between devices, shift(): lax.ppermute(value, axis, [(j, (j + step) % size) for j in range(size)])  16.7 us
    pallas_call x5, Pallas kernels, join(): pl.pallas_call(functools.partial(join_kernel, n_slots, block), out_shape=...  15.5 us
    pallas_call x5, Pallas kernels, place(): pl.pallas_call(functools.partial(place_kernel, count), out_shape=jax.Shap...  12.2 us
  transfers between devices with their start and end apart: 48, of which 18 were waited for; matrix products, arithmetic and copies ran while one was open for 4% of the time, Pallas kernels for 44%

profile of v6, /device:TPU:8, one launch (start us, length us, event | category | flops | bytes accessed | tf_op | source)
XLA Modules:
  0.0 290.8 jit_solution(9799836409976380981)
XLA Ops:
  7.2 2.6 collective-permute-start.4
  12.3 19.2 %project_and_attend.3.refs_10_ = bf16[2,128,1536]{2,1,0:T(8,128)(2,1)S(1)} custom-call(bf16[64,8192]{1,0:T(8,128)(2,1)S(1)} %bitcast.102, bf16[64,8192]{1,0:T(8,128)(2,1)} %collective-permute-done.2.refs_1_, f32[1,8192]{1,0:T(1,128)S(1)} %copy-done.7, f32[128,128]{1,0:T(8,128)S(1)} %copy.49.refs_3_.refs_5_, ...), custom_call_target="tpu_custom_call" | custom-call | flops 1 | bytes 1 | tf_op jit(solution)/shard_map/project_and_attend/pallas_call | solution.py:162
  38.1 27.1 %project_and_attend.4 = (bf16[4,2,2,16,2048]{4,3,2,1,0:T(8,128)(2,1)S(1)}, bf16[2,128,1536]{2,1,0:T(8,128)(2,1)S(1)}) custom-call(bf16[64,8192]{1,0:T(8,128)(2,1)S(1)} %collective-permute-done.refs_0_, bf16[64,8192]{1,0:T(8,128)(2,1)} %collective-permute-done.6.refs_1_, bf16[64,8192]{1,0:T(8,128)(2,1)S(1)} %collective-permute-done.1.refs_2_, ...), custom_call_target="tpu_custom_call" | custom-call | flops 1 | bytes 1 | tf_op jit(solution)/shard_map/project_and_attend/pallas_call | solution.py:162
  65.5 3.0 %collective-permute-start.11 = (bf16[2,2,16,2048]{3,2,1,0:T(8,128)(2,1)S(1)}, bf16[2,2,16,2048]{3,2,1,0:T(8,128)(2,1)S(1)}, u32[]{:S(2)}, u32[]{:S(2)}) collective-permute-start(bf16[2,2,16,2048]{3,2,1,0:T(8,128)(2,1)S(1)} %get-tuple-element.331), channel_id=1, source_target_pairs={{0,4},{2,6},{4,0},{6,2},{1,5},{3,7},{5,1},{7,3},{8,12},{10,14},{12... | collective-permute-start | bytes 786440 | tf_op jit(solution)/shard_map/ppermute | solution.py:24
  70.7 20.3 %project_and_attend.5 = bf16[4,2,2,16,2048]{4,3,2,1,0:T(8,128)(2,1)S(1)} custom-call(bf16[64,8192]{1,0:T(8,128)(2,1)} %collective-permute-done.8.refs_0_, bf16[64,8192]{1,0:T(8,128)(2,1)S(1)} %collective-permute-done.13.refs_1_, f32[1,8192]{1,0:T(1,128)S(1)} %copy-done.8, f32[128,128]{1,0:T(8,128)S(1)} %copy.49.refs_3_.refs_5_, ...), custom_call_target="tpu_custom_call" | custom-call | flops 1 | bytes 1 | tf_op jit(solution)/shard_map/project_and_attend/pallas_call | solution.py:162
  94.7 3.1 %out_projection.8 = (bf16[128,1024]{1,0:T(8,128)(2,1)S(1)}, bf16[128,1024]{1,0:T(8,128)(2,1)S(1)}) custom-call(bf16[256,2048]{1,0:T(8,128)(2,1)S(1)} %bitcast.88, bf16[1,2048,8192]{2,1,0:T(8,128)(2,1)} %wo_ref.15), custom_call_target="tpu_custom_call" | custom-call | flops 1 | bytes 1 | tf_op jit(solution)/shard_map/out_projection/pallas_call | solution.py:192
  98.5 3.3 %out_projection.9 = (bf16[128,1024]{1,0:T(8,128)(2,1)S(1)}, bf16[128,1024]{1,0:T(8,128)(2,1)S(1)}) custom-call(bf16[256,2048]{1,0:T(8,128)(2,1)S(1)} %bitcast.89, bf16[1,2048,8192]{2,1,0:T(8,128)(2,1)} %wo_ref.15), custom_call_target="tpu_custom_call" | custom-call | flops 1 | bytes 1 | tf_op jit(solution)/shard_map/out_projection/pallas_call | solution.py:192
  101.8 2.9 collective-permute-done.14
  111.6 6.3 %out_projection.10 = (bf16[128,2048]{1,0:T(8,128)(2,1)S(1)}, bf16[128,2048]{1,0:T(8,128)(2,1)}) custom-call(bf16[256,2048]{1,0:T(8,128)(2,1)S(1)} %bitcast.90, bf16[1,2048,8192]{2,1,0:T(8,128)(2,1)} %wo_ref.15), custom_call_target="tpu_custom_call" | custom-call | flops 1 | bytes 1 | tf_op jit(solution)/shard_map/out_projection/pallas_call | solution.py:192
  118.7 3.4 %collective-permute-done.16 = bf16[2,2,16,2048]{3,2,1,0:T(8,128)(2,1)} collective-permute-done((bf16[2,2,16,2048]{3,2,1,0:T(8,128)(2,1)}, bf16[2,2,16,2048]{3,2,1,0:T(8,128)(2,1)}, u32[]{:S(2)}, u32[]{:S(2)}) %collective-permute-start.16) | collective-permute-done | bytes 262176 | tf_op jit(solution)/shard_map/ppermute | solution.py:24
  124.7 4.1 %out_projection.11 = (bf16[128,1024]{1,0:T(8,128)(2,1)S(1)}, bf16[128,1024]{1,0:T(8,128)(2,1)}) custom-call(bf16[256,2048]{1,0:T(8,128)(2,1)S(1)} %bitcast.92, bf16[1,2048,8192]{2,1,0:T(8,128)(2,1)} %wo_ref.15), custom_call_target="tpu_custom_call" | custom-call | flops 1 | bytes 1 | tf_op jit(solution)/shard_map/out_projection/pallas_call | solution.py:192
  134.3 3.1 %out_projection.12 = (bf16[128,1024]{1,0:T(8,128)(2,1)S(1)}, bf16[128,1024]{1,0:T(8,128)(2,1)S(1)}) custom-call(bf16[256,2048]{1,0:T(8,128)(2,1)S(1)} %bitcast.93, bf16[1,2048,8192]{2,1,0:T(8,128)(2,1)} %wo_ref.15), custom_call_target="tpu_custom_call" | custom-call | flops 1 | bytes 1 | tf_op jit(solution)/shard_map/out_projection/pallas_call | solution.py:192
  139.1 2.6 join_partials.5
  145.8 5.6 %out_projection.13 = (bf16[128,2048]{1,0:T(8,128)(2,1)S(1)}, bf16[128,2048]{1,0:T(8,128)(2,1)S(1)}) custom-call(bf16[256,2048]{1,0:T(8,128)(2,1)S(1)} %bitcast.94, bf16[1,2048,8192]{2,1,0:T(8,128)(2,1)} %wo_ref.15), custom_call_target="tpu_custom_call" | custom-call | flops 1 | bytes 1 | tf_op jit(solution)/shard_map/out_projection/pallas_call | solution.py:192
  153.9 2.5 join_partials.6
  156.4 3.0 %collective-permute-done.23.refs_3_ = bf16[6,16,1024]{2,1,0:T(8,128)(2,1)S(1)} collective-permute-done((bf16[6,16,1024]{2,1,0:T(8,128)(2,1)S(1)}, bf16[6,16,1024]{2,1,0:T(8,128)(2,1)S(1)}, u32[]{:S(2)}, u32[]{:S(2)}) %collective-permute-start.23) | collective-permute-done | bytes 196640 | tf_op jit(solution)/shard_map/ppermute | solution.py:24
  163.4 7.1 %out_projection.14 = (bf16[256,2048]{1,0:T(8,128)(2,1)S(1)}, bf16[256,2048]{1,0:T(8,128)(2,1)S(1)}) custom-call(bf16[512,2048]{1,0:T(8,128)(2,1)S(1)} %bitcast.96, bf16[1,2048,8192]{2,1,0:T(8,128)(2,1)} %wo_ref.15), custom_call_target="tpu_custom_call" | custom-call | flops 1 | bytes 1 | tf_op jit(solution)/shard_map/out_projection/pallas_call | solution.py:192
  172.6 3.3 %join_partials.7 = (bf16[6,16,2048]{2,1,0:T(8,128)(2,1)S(1)}, bf16[6,16,2048]{2,1,0:T(8,128)(2,1)S(1)}, bf16[6,16,2048]{2,1,0:T(8,128)(2,1)S(1)}, bf16[6,16,2048]{2,1,0:T(8,128)(2,1)S(1)}, f32[4,6,16,128]{3,2,1,0:T(8,128)S(1)}) custom-call(s32[5,24]{1,0:T(8,128)S(1)} %stack.72.table_ref, bf16[8,16,2048]{2,1,0:T(8,128)(2,1)S(1)} %bitcast.111, ...), custom_call_target="tpu_custom_call" | custom-call | flops 1 | bytes 1 | tf_op jit(solution)/shard_map/join_partials/pallas_call | solution.py:243
  175.9 2.6 collective-permute-done.28.refs_3_
  183.5 7.1 %out_projection.15 = (bf16[256,2048]{1,0:T(8,128)(2,1)S(1)}, bf16[256,2048]{1,0:T(8,128)(2,1)S(1)}) custom-call(bf16[512,2048]{1,0:T(8,128)(2,1)S(1)} %bitcast.97, bf16[1,2048,8192]{2,1,0:T(8,128)(2,1)} %wo_ref.15), custom_call_target="tpu_custom_call" | custom-call | flops 1 | bytes 1 | tf_op jit(solution)/shard_map/out_projection/pallas_call | solution.py:192
  192.7 9.3 %collective-permute-done.33 = bf16[16,16,2048]{2,1,0:T(8,128)(2,1)S(1)} collective-permute-done((bf16[16,16,2048]{2,1,0:T(8,128)(2,1)S(1)}, bf16[16,16,2048]{2,1,0:T(8,128)(2,1)S(1)}, u32[]{:S(2)}, u32[]{:S(2)}) %collective-permute-start.33) | collective-permute-done | bytes 1048608 | tf_op jit(solution)/shard_map/ppermute | solution.py:31
  202.0 3.9 %join_partials.8 = (bf16[6,16,2048]{2,1,0:T(8,128)(2,1)S(1)}, bf16[6,16,2048]{2,1,0:T(8,128)(2,1)}, bf16[6,16,2048]{2,1,0:T(8,128)(2,1)}, bf16[6,16,2048]{2,1,0:T(8,128)(2,1)}, f32[4,6,16,128]{3,2,1,0:T(8,128)S(1)}) custom-call(s32[5,24]{1,0:T(8,128)S(1)} %stack.72.table_ref, bf16[16,16,2048]{2,1,0:T(8,128)(2,1)S(1)} %bitcast.105, ...), custom_call_target="tpu_custom_call" | custom-call | flops 1 | bytes 1 | tf_op jit(solution)/shard_map/join_partials/pallas_call | solution.py:243
  205.9 2.5 collective-permute-done.31.refs_2_
  208.4 7.2 %collective-permute-done.32.refs_3_ = bf16[6,16,2048]{2,1,0:T(8,128)(2,1)S(1)} collective-permute-done((bf16[6,16,2048]{2,1,0:T(8,128)(2,1)S(1)}, bf16[6,16,2048]{2,1,0:T(8,128)(2,1)S(1)}, u32[]{:S(2)}, u32[]{:S(2)}) %collective-permute-start.32) | collective-permute-done | bytes 393248 | tf_op jit(solution)/shard_map/ppermute | solution.py:24
  222.0 15.9 %collective-permute-done.37 = bf16[16,16,2048]{2,1,0:T(8,128)(2,1)S(1)} collective-permute-done((bf16[16,16,2048]{2,1,0:T(8,128)(2,1)S(1)}, bf16[16,16,2048]{2,1,0:T(8,128)(2,1)S(1)}, u32[]{:S(2)}, u32[]{:S(2)}) %collective-permute-start.37) | collective-permute-done | bytes 1048608 | tf_op jit(solution)/shard_map/ppermute | solution.py:31
  237.9 3.1 %join_partials.9 = (bf16[6,16,2048]{2,1,0:T(8,128)(2,1)S(1)}, bf16[6,16,2048]{2,1,0:T(8,128)(2,1)S(1)}, bf16[6,16,2048]{2,1,0:T(8,128)(2,1)S(1)}, bf16[6,16,2048]{2,1,0:T(8,128)(2,1)S(1)}, f32[4,6,16,128]{3,2,1,0:T(8,128)S(1)}) custom-call(s32[5,24]{1,0:T(8,128)S(1)} %stack.72.table_ref, bf16[16,16,2048]{2,1,0:T(8,128)(2,1)S(1)} %bitcast.103, ...), custom_call_target="tpu_custom_call" | custom-call | flops 1 | bytes 1 | tf_op jit(solution)/shard_map/join_partials/pallas_call | solution.py:243
  243.9 7.1 %collective-permute-done.36.refs_3_ = bf16[6,16,2048]{2,1,0:T(8,128)(2,1)} collective-permute-done((bf16[6,16,2048]{2,1,0:T(8,128)(2,1)}, bf16[6,16,2048]{2,1,0:T(8,128)(2,1)}, u32[]{:S(2)}, u32[]{:S(2)}) %collective-permute-start.36) | collective-permute-done | bytes 393248 | tf_op jit(solution)/shard_map/ppermute | solution.py:24
  251.2 3.4 %collective-permute-start.43 = (f32[4,16]{1,0:T(4,128)S(1)}, f32[4,16]{1,0:T(4,128)S(1)}, u32[]{:S(2)}, u32[]{:S(2)}) collective-permute-start(f32[4,16]{1,0:T(4,128)S(1)} %fusion.22), channel_id=1, source_target_pairs={{0,4},{2,6},{4,0},{6,2},{1,5},{3,7},{5,1},{7,3},{8,12},{10,14},{12... | collective-permute-start | bytes 776 | tf_op jit(solution)/shard_map/ppermute | solution.py:31
  258.1 6.8 %collective-permute-done.43 = f32[4,16]{1,0:T(4,128)S(1)} collective-permute-done((f32[4,16]{1,0:T(4,128)S(1)}, f32[4,16]{1,0:T(4,128)S(1)}, u32[]{:S(2)}, u32[]{:S(2)}) %collective-permute-start.43) | collective-permute-done | bytes 288 | tf_op jit(solution)/shard_map/ppermute | solution.py:31
  268.1 3.7 %place_rows.8.refs_4_ = bf16[6,4,16,8192]{3,2,1,0:T(8,128)(2,1)} custom-call(s32[4]{0:T(128)S(1)} %iota_xor_fusion.order_ref, bf16[6,16,2048]{2,1,0:T(8,128)(2,1)S(1)} %get-tuple-element.312.refs_0_, bf16[6,16,2048]{2,1,0:T(8,128)(2,1)S(1)} %collective-permute-done.34.refs_1_, ...), custom_call_target="tpu_custom_call", output_to_operand_aliasing={{}: (5, {})} | custom-call | flops 1 | bytes 1 | tf_op jit(solution)/shard_map/place_rows/pallas_call | solution.py:284
  272.6 9.2 %collective-permute-done.39.refs_2_ = bf16[6,16,2048]{2,1,0:T(8,128)(2,1)S(1)} collective-permute-done((bf16[6,16,2048]{2,1,0:T(8,128)(2,1)}, bf16[6,16,2048]{2,1,0:T(8,128)(2,1)S(1)}, u32[]{:S(2)}, u32[]{:S(2)}) %collective-permute-start.39) | collective-permute-done | bytes 393248 | tf_op jit(solution)/shard_map/ppermute | solution.py:24
  281.8 6.8 %collective-permute-done.40.refs_3_ = bf16[6,16,2048]{2,1,0:T(8,128)(2,1)S(1)} collective-permute-done((bf16[6,16,2048]{2,1,0:T(8,128)(2,1)}, bf16[6,16,2048]{2,1,0:T(8,128)(2,1)S(1)}, u32[]{:S(2)}, u32[]{:S(2)}) %collective-permute-start.40) | collective-permute-done | bytes 393248 | tf_op jit(solution)/shard_map/ppermute | solution.py:24
  (187 shorter events, 78.3 us)
Async XLA Ops:
  0.7 30.8 %collective-permute-start = (bf16[64,8192]{1,0:T(8,128)(2,1)}, bf16[64,8192]{1,0:T(8,128)(2,1)S(1)}, u32[]{:S(2)}, u32[]{:S(2)}) collective-permute-start(bf16[64,8192]{1,0:T(8,128)(2,1)} %bitcast.99), channel_id=1, source_target_pairs={{0,1},{1,0},{2,3},{3,2},{4,5},{5,4},{6,7},{7,6},{8,9},{9,8},{10,11... | collective-permute-start | bytes 3145736 | tf_op jit(solution)/shard_map/ppermute | solution.py:31
  2.3 29.3 %collective-permute-start.1 = (bf16[64,8192]{1,0:T(8,128)(2,1)}, bf16[64,8192]{1,0:T(8,128)(2,1)S(1)}, u32[]{:S(2)}, u32[]{:S(2)}) collective-permute-start(bf16[64,8192]{1,0:T(8,128)(2,1)} %bitcast.100), channel_id=1, source_target_pairs={{0,16},{8,24},{16,0},{24,8},{1,17},{9,25},{17,1},{25,9},{2,18},{10... | collective-permute-start | bytes 3145736 | tf_op jit(solution)/shard_map/ppermute | solution.py:24
  6.8 24.8 %collective-permute-start.3 = (bf16[16,8192]{1,0:T(8,128)(2,1)}, bf16[16,8192]{1,0:T(8,128)(2,1)}, u32[]{:S(2)}, u32[]{:S(2)}) collective-permute-start(bf16[16,8192]{1,0:T(8,128)(2,1)} %get-tuple-element.336), channel_id=1, source_target_pairs={{0,2},{2,0},{4,6},{6,4},{1,3},{3,1},{5,7},{7,5},{8,10},{10,8},{12,... | collective-permute-start | bytes 786440 | tf_op jit(solution)/shard_map/ppermute | solution.py:24
  7.2 24.4 %collective-permute-start.4 = (bf16[16,8192]{1,0:T(8,128)(2,1)}, bf16[16,8192]{1,0:T(8,128)(2,1)}, u32[]{:S(2)}, u32[]{:S(2)}) collective-permute-start(bf16[16,8192]{1,0:T(8,128)(2,1)} %get-tuple-element.335), channel_id=1, source_target_pairs={{0,4},{2,6},{4,0},{6,2},{1,5},{3,7},{5,1},{7,3},{8,12},{10,14},{12... | collective-permute-start | bytes 786440 | tf_op jit(solution)/shard_map/ppermute | solution.py:24
  9.8 23.5 %collective-permute-start.5 = (bf16[16,8192]{1,0:T(8,128)(2,1)}, bf16[16,8192]{1,0:T(8,128)(2,1)}, u32[]{:S(2)}, u32[]{:S(2)}) collective-permute-start(bf16[16,8192]{1,0:T(8,128)(2,1)} %get-tuple-element.334), channel_id=1, source_target_pairs={{0,6},{2,4},{4,2},{6,0},{1,7},{3,5},{5,3},{7,1},{8,14},{10,12},{12... | collective-permute-start | bytes 786440 | tf_op jit(solution)/shard_map/ppermute | solution.py:24
  33.3 31.9 %collective-permute-start.8 = (bf16[64,8192]{1,0:T(8,128)(2,1)S(1)}, bf16[64,8192]{1,0:T(8,128)(2,1)}, u32[]{:S(2)}, u32[]{:S(2)}) collective-permute-start(bf16[64,8192]{1,0:T(8,128)(2,1)S(1)} %collective-permute-done.1.refs_2_), channel_id=1, source_target_pairs={{0,1},{1,0},{2,3},{3,2},{4,5},{5,4},{6,7},{7,6},{8,9},{9,8},{10,11... | collective-permute-start | bytes 3145736 | tf_op jit(solution)/shard_map/ppermute | solution.py:31
  36.6 28.6 %collective-permute-start.9 = (bf16[4,16,8192]{2,1,0:T(8,128)(2,1)}, bf16[4,16,8192]{2,1,0:T(8,128)(2,1)}, u32[]{:S(2)}, u32[]{:S(2)}) collective-permute-start(bf16[4,16,8192]{2,1,0:T(8,128)(2,1)} %pad_maximum_fusion.2), channel_id=1, source_target_pairs={{0,16},{8,24},{16,0},{24,8},{1,17},{9,25},{17,1},{25,9},{2,18},{10... | collective-permute-start | bytes 3145736 | tf_op jit(solution)/shard_map/ppermute | solution.py:24
  65.4 25.6 %collective-permute-start.10 = (bf16[2,2,16,2048]{3,2,1,0:T(8,128)(2,1)S(1)}, bf16[2,2,16,2048]{3,2,1,0:T(8,128)(2,1)S(1)}, u32[]{:S(2)}, u32[]{:S(2)}) collective-permute-start(bf16[2,2,16,2048]{3,2,1,0:T(8,128)(2,1)S(1)} %get-tuple-element.332), channel_id=1, source_target_pairs={{0,2},{2,0},{4,6},{6,4},{1,3},{3,1},{5,7},{7,5},{8,10},{10,8},{12,... | collective-permute-start | bytes 786440 | tf_op jit(solution)/shard_map/ppermute | solution.py:24
  65.5 25.5 %collective-permute-start.11 = (bf16[2,2,16,2048]{3,2,1,0:T(8,128)(2,1)S(1)}, bf16[2,2,16,2048]{3,2,1,0:T(8,128)(2,1)S(1)}, u32[]{:S(2)}, u32[]{:S(2)}) collective-permute-start(bf16[2,2,16,2048]{3,2,1,0:T(8,128)(2,1)S(1)} %get-tuple-element.331), channel_id=1, source_target_pairs={{0,4},{2,6},{4,0},{6,2},{1,5},{3,7},{5,1},{7,3},{8,12},{10,14},{12... | collective-permute-start | bytes 786440 | tf_op jit(solution)/shard_map/ppermute | solution.py:24
  68.5 23.7 %collective-permute-start.12 = (bf16[2,2,16,2048]{3,2,1,0:T(8,128)(2,1)S(1)}, bf16[2,2,16,2048]{3,2,1,0:T(8,128)(2,1)S(1)}, u32[]{:S(2)}, u32[]{:S(2)}) collective-permute-start(bf16[2,2,16,2048]{3,2,1,0:T(8,128)(2,1)S(1)} %get-tuple-element.330), channel_id=1, source_target_pairs={{0,6},{2,4},{4,2},{6,0},{1,7},{3,5},{5,3},{7,1},{8,14},{10,12},{12... | collective-permute-start | bytes 786440 | tf_op jit(solution)/shard_map/ppermute | solution.py:24
  105.4 18.2 %collective-permute-start.19 = (bf16[8,16,8192]{2,1,0:T(8,128)(2,1)S(1)}, bf16[8,16,8192]{2,1,0:T(8,128)(2,1)}, u32[]{:S(2)}, u32[]{:S(2)}) collective-permute-start(bf16[8,16,8192]{2,1,0:T(8,128)(2,1)S(1)} %pad_maximum_fusion.resid_ref), channel_id=1, source_target_pairs={{0,8},{8,0},{16,24},{24,16},{1,9},{9,1},{17,25},{25,17},{2,10},{10... | collective-permute-start | bytes 6291464 | tf_op jit(solution)/shard_map/ppermute | solution.py:24
  107.6 14.4 %collective-permute-start.16 = (bf16[2,2,16,2048]{3,2,1,0:T(8,128)(2,1)}, bf16[2,2,16,2048]{3,2,1,0:T(8,128)(2,1)}, u32[]{:S(2)}, u32[]{:S(2)}) collective-permute-start(bf16[2,2,16,2048]{3,2,1,0:T(8,128)(2,1)} %get-tuple-element.207), channel_id=1, source_target_pairs={{0,6},{2,4},{4,2},{6,0},{1,7},{3,5},{5,3},{7,1},{8,14},{10,12},{12... | collective-permute-start | bytes 786440 | tf_op jit(solution)/shard_map/ppermute | solution.py:24
  109.9 13.6 %collective-permute-start.18 = (bf16[8,16,1024]{2,1,0:T(8,128)(2,1)}, bf16[8,16,1024]{2,1,0:T(8,128)(2,1)}, u32[]{:S(2)}, u32[]{:S(2)}) collective-permute-start(bf16[8,16,1024]{2,1,0:T(8,128)(2,1)} %bitcast.122), channel_id=1, source_target_pairs={{0,1},{1,0},{2,3},{3,2},{4,5},{5,4},{6,7},{7,6},{8,9},{9,8},{10,11... | collective-permute-start | bytes 786440 | tf_op jit(solution)/shard_map/ppermute | solution.py:31
  130.0 29.4 %collective-permute-start.25 = (bf16[8,16,2048]{2,1,0:T(8,128)(2,1)}, bf16[8,16,2048]{2,1,0:T(8,128)(2,1)}, u32[]{:S(2)}, u32[]{:S(2)}) collective-permute-start(bf16[8,16,2048]{2,1,0:T(8,128)(2,1)} %bitcast.49), channel_id=1, source_target_pairs={{0,1},{1,0},{2,3},{3,2},{4,5},{5,4},{6,7},{7,6},{8,9},{9,8},{10,11... | collective-permute-start | bytes 1572872 | tf_op jit(solution)/shard_map/ppermute | solution.py:31
  141.7 14.7 %collective-permute-start.21 = (bf16[6,16,1024]{2,1,0:T(8,128)(2,1)S(1)}, bf16[6,16,1024]{2,1,0:T(8,128)(2,1)S(1)}, u32[]{:S(2)}, u32[]{:S(2)}) collective-permute-start(bf16[6,16,1024]{2,1,0:T(8,128)(2,1)S(1)} %get-tuple-element.240), channel_id=1, source_target_pairs={{0,2},{2,0},{4,6},{6,4},{1,3},{3,1},{5,7},{7,5},{8,10},{10,8},{12,... | collective-permute-start | bytes 589832 | tf_op jit(solution)/shard_map/ppermute | solution.py:24
  143.0 13.4 %collective-permute-start.22 = (bf16[6,16,1024]{2,1,0:T(8,128)(2,1)S(1)}, bf16[6,16,1024]{2,1,0:T(8,128)(2,1)S(1)}, u32[]{:S(2)}, u32[]{:S(2)}) collective-permute-start(bf16[6,16,1024]{2,1,0:T(8,128)(2,1)S(1)} %get-tuple-element.241), channel_id=1, source_target_pairs={{0,4},{2,6},{4,0},{6,2},{1,5},{3,7},{5,1},{7,3},{8,12},{10,14},{12... | collective-permute-start | bytes 589832 | tf_op jit(solution)/shard_map/ppermute | solution.py:24
  143.5 15.9 %collective-permute-start.23 = (bf16[6,16,1024]{2,1,0:T(8,128)(2,1)S(1)}, bf16[6,16,1024]{2,1,0:T(8,128)(2,1)S(1)}, u32[]{:S(2)}, u32[]{:S(2)}) collective-permute-start(bf16[6,16,1024]{2,1,0:T(8,128)(2,1)S(1)} %get-tuple-element.242), channel_id=1, source_target_pairs={{0,6},{2,4},{4,2},{6,0},{1,7},{3,5},{5,3},{7,1},{8,14},{10,12},{12... | collective-permute-start | bytes 589832 | tf_op jit(solution)/shard_map/ppermute | solution.py:24
  159.9 15.9 %collective-permute-start.26 = (bf16[6,16,1024]{2,1,0:T(8,128)(2,1)S(1)}, bf16[6,16,1024]{2,1,0:T(8,128)(2,1)S(1)}, u32[]{:S(2)}, u32[]{:S(2)}) collective-permute-start(bf16[6,16,1024]{2,1,0:T(8,128)(2,1)S(1)} %get-tuple-element.257), channel_id=1, source_target_pairs={{0,2},{2,0},{4,6},{6,4},{1,3},{3,1},{5,7},{7,5},{8,10},{10,8},{12,... | collective-permute-start | bytes 589832 | tf_op jit(solution)/shard_map/ppermute | solution.py:24
  159.9 16.0 %collective-permute-start.27 = (bf16[6,16,1024]{2,1,0:T(8,128)(2,1)S(1)}, bf16[6,16,1024]{2,1,0:T(8,128)(2,1)S(1)}, u32[]{:S(2)}, u32[]{:S(2)}) collective-permute-start(bf16[6,16,1024]{2,1,0:T(8,128)(2,1)S(1)} %get-tuple-element.258), channel_id=1, source_target_pairs={{0,4},{2,6},{4,0},{6,2},{1,5},{3,7},{5,1},{7,3},{8,12},{10,14},{12... | collective-permute-start | bytes 589832 | tf_op jit(solution)/shard_map/ppermute | solution.py:24
  162.0 16.5 %collective-permute-start.28 = (bf16[6,16,1024]{2,1,0:T(8,128)(2,1)S(1)}, bf16[6,16,1024]{2,1,0:T(8,128)(2,1)S(1)}, u32[]{:S(2)}, u32[]{:S(2)}) collective-permute-start(bf16[6,16,1024]{2,1,0:T(8,128)(2,1)S(1)} %get-tuple-element.259), channel_id=1, source_target_pairs={{0,6},{2,4},{4,2},{6,0},{1,7},{3,5},{5,3},{7,1},{8,14},{10,12},{12... | collective-permute-start | bytes 589832 | tf_op jit(solution)/shard_map/ppermute | solution.py:24
  178.5 23.5 %collective-permute-start.33 = (bf16[16,16,2048]{2,1,0:T(8,128)(2,1)S(1)}, bf16[16,16,2048]{2,1,0:T(8,128)(2,1)S(1)}, u32[]{:S(2)}, u32[]{:S(2)}) collective-permute-start(bf16[16,16,2048]{2,1,0:T(8,128)(2,1)S(1)} %bitcast.119), channel_id=1, source_target_pairs={{0,1},{1,0},{2,3},{3,2},{4,5},{5,4},{6,7},{7,6},{8,9},{9,8},{10,11... | collective-permute-start | bytes 3145736 | tf_op jit(solution)/shard_map/ppermute | solution.py:31
  180.0 25.9 %collective-permute-start.30 = (bf16[6,16,2048]{2,1,0:T(8,128)(2,1)S(1)}, bf16[6,16,2048]{2,1,0:T(8,128)(2,1)S(1)}, u32[]{:S(2)}, u32[]{:S(2)}) collective-permute-start(bf16[6,16,2048]{2,1,0:T(8,128)(2,1)S(1)} %get-tuple-element.276), channel_id=1, source_target_pairs={{0,2},{2,0},{4,6},{6,4},{1,3},{3,1},{5,7},{7,5},{8,10},{10,8},{12,... | collective-permute-start | bytes 1179656 | tf_op jit(solution)/shard_map/ppermute | solution.py:24
  180.0 28.4 %collective-permute-start.31 = (bf16[6,16,2048]{2,1,0:T(8,128)(2,1)S(1)}, bf16[6,16,2048]{2,1,0:T(8,128)(2,1)S(1)}, u32[]{:S(2)}, u32[]{:S(2)}) collective-permute-start(bf16[6,16,2048]{2,1,0:T(8,128)(2,1)S(1)} %get-tuple-element.277), channel_id=1, source_target_pairs={{0,4},{2,6},{4,0},{6,2},{1,5},{3,7},{5,1},{7,3},{8,12},{10,14},{12... | collective-permute-start | bytes 1179656 | tf_op jit(solution)/shard_map/ppermute | solution.py:24
  182.0 33.7 %collective-permute-start.32 = (bf16[6,16,2048]{2,1,0:T(8,128)(2,1)S(1)}, bf16[6,16,2048]{2,1,0:T(8,128)(2,1)S(1)}, u32[]{:S(2)}, u32[]{:S(2)}) collective-permute-start(bf16[6,16,2048]{2,1,0:T(8,128)(2,1)S(1)} %get-tuple-element.278), channel_id=1, source_target_pairs={{0,6},{2,4},{4,2},{6,0},{1,7},{3,5},{5,3},{7,1},{8,14},{10,12},{12... | collective-permute-start | bytes 1179656 | tf_op jit(solution)/shard_map/ppermute | solution.py:24
  215.7 22.2 %collective-permute-start.37 = (bf16[16,16,2048]{2,1,0:T(8,128)(2,1)S(1)}, bf16[16,16,2048]{2,1,0:T(8,128)(2,1)S(1)}, u32[]{:S(2)}, u32[]{:S(2)}) collective-permute-start(bf16[16,16,2048]{2,1,0:T(8,128)(2,1)S(1)} %bitcast.120), channel_id=1, source_target_pairs={{0,1},{1,0},{2,3},{3,2},{4,5},{5,4},{6,7},{7,6},{8,9},{9,8},{10,11... | collective-permute-start | bytes 3145736 | tf_op jit(solution)/shard_map/ppermute | solution.py:31
  216.2 27.0 %collective-permute-start.34 = (bf16[6,16,2048]{2,1,0:T(8,128)(2,1)}, bf16[6,16,2048]{2,1,0:T(8,128)(2,1)S(1)}, u32[]{:S(2)}, u32[]{:S(2)}) collective-permute-start(bf16[6,16,2048]{2,1,0:T(8,128)(2,1)} %get-tuple-element.294), channel_id=1, source_target_pairs={{0,2},{2,0},{4,6},{6,4},{1,3},{3,1},{5,7},{7,5},{8,10},{10,8},{12,... | collective-permute-start | bytes 1179656 | tf_op jit(solution)/shard_map/ppermute | solution.py:24
  216.3 27.6 %collective-permute-start.35 = (bf16[6,16,2048]{2,1,0:T(8,128)(2,1)}, bf16[6,16,2048]{2,1,0:T(8,128)(2,1)}, u32[]{:S(2)}, u32[]{:S(2)}) collective-permute-start(bf16[6,16,2048]{2,1,0:T(8,128)(2,1)} %get-tuple-element.295), channel_id=1, source_target_pairs={{0,4},{2,6},{4,0},{6,2},{1,5},{3,7},{5,1},{7,3},{8,12},{10,14},{12... | collective-permute-start | bytes 1179656 | tf_op jit(solution)/shard_map/ppermute | solution.py:24
  217.5 33.5 %collective-permute-start.36 = (bf16[6,16,2048]{2,1,0:T(8,128)(2,1)}, bf16[6,16,2048]{2,1,0:T(8,128)(2,1)}, u32[]{:S(2)}, u32[]{:S(2)}) collective-permute-start(bf16[6,16,2048]{2,1,0:T(8,128)(2,1)} %get-tuple-element.296), channel_id=1, source_target_pairs={{0,6},{2,4},{4,2},{6,0},{1,7},{3,5},{5,3},{7,1},{8,14},{10,12},{12... | collective-permute-start | bytes 1179656 | tf_op jit(solution)/shard_map/ppermute | solution.py:24
  251.1 21.4 %collective-permute-start.38 = (bf16[6,16,2048]{2,1,0:T(8,128)(2,1)}, bf16[6,16,2048]{2,1,0:T(8,128)(2,1)S(1)}, u32[]{:S(2)}, u32[]{:S(2)}) collective-permute-start(bf16[6,16,2048]{2,1,0:T(8,128)(2,1)} %copy-done.15), channel_id=1, source_target_pairs={{0,2},{2,0},{4,6},{6,4},{1,3},{3,1},{5,7},{7,5},{8,10},{10,8},{12,... | collective-permute-start | bytes 1179656 | tf_op jit(solution)/shard_map/ppermute | solution.py:24
  251.2 13.7 %collective-permute-start.43 = (f32[4,16]{1,0:T(4,128)S(1)}, f32[4,16]{1,0:T(4,128)S(1)}, u32[]{:S(2)}, u32[]{:S(2)}) collective-permute-start(f32[4,16]{1,0:T(4,128)S(1)} %fusion.22), channel_id=1, source_target_pairs={{0,4},{2,6},{4,0},{6,2},{1,5},{3,7},{5,1},{7,3},{8,12},{10,14},{12... | collective-permute-start | bytes 776 | tf_op jit(solution)/shard_map/ppermute | solution.py:31
  254.7 27.1 %collective-permute-start.39 = (bf16[6,16,2048]{2,1,0:T(8,128)(2,1)}, bf16[6,16,2048]{2,1,0:T(8,128)(2,1)S(1)}, u32[]{:S(2)}, u32[]{:S(2)}) collective-permute-start(bf16[6,16,2048]{2,1,0:T(8,128)(2,1)} %copy-done.14), channel_id=1, source_target_pairs={{0,4},{2,6},{4,0},{6,2},{1,5},{3,7},{5,1},{7,3},{8,12},{10,14},{12... | collective-permute-start | bytes 1179656 | tf_op jit(solution)/shard_map/ppermute | solution.py:24
  257.0 31.6 %collective-permute-start.40 = (bf16[6,16,2048]{2,1,0:T(8,128)(2,1)}, bf16[6,16,2048]{2,1,0:T(8,128)(2,1)S(1)}, u32[]{:S(2)}, u32[]{:S(2)}) collective-permute-start(bf16[6,16,2048]{2,1,0:T(8,128)(2,1)} %copy-done.13), channel_id=1, source_target_pairs={{0,6},{2,4},{4,2},{6,0},{1,7},{3,5},{5,3},{7,1},{8,14},{10,12},{12... | collective-permute-start | bytes 1179656 | tf_op jit(solution)/shard_map/ppermute | solution.py:24
  (41 other events, 247.9 us)
